TPU v7x, 32 devices: a whole 2x2x4 slice. The times are simulated.
32 devices in a mesh: seg: 16 (over z, y, core), item: 2 (over x).
Axes of the slice: x: 2, y: 2, z: 4, core: 2. Of those that a mesh axis runs over, the one named last changes fastest.
Arguments:
- text: bfloat16 [8, 16, 64, 768], P('item', 'seg'), may hold values from -6 to 6
- cotangent: bfloat16 [8, 16, 84, 768], P('item', 'seg'), may hold values from -6 to 6
- unroll: int32 [8], P('item'), may hold values from 1 to 16, as said below
- memory: bfloat16 [10, 768], replicated, may hold values from -6 to 6
- qkv_weight: bfloat16 [768, 2304], P('seg'), may hold values from -0.21875 to 0.21875
- qv_bias: bfloat16 [1536], P('seg'), may hold values from -3 to 3
- out_weight: bfloat16 [768, 768], P('seg'), may hold values from -2 to 2
- out_bias: bfloat16 [768], P('seg'), may hold values from -3 to 3
- norm1_gain: bfloat16 [768], P('seg'), may hold values from 0.099609375 to 1.8984375
- norm1_bias: bfloat16 [768], P('seg'), may hold values from -3 to 3
- up_weight: bfloat16 [768, 3072], P('seg'), may hold values from -0.21875 to 0.21875
- up_bias: bfloat16 [3072], P('seg'), may hold values from -3 to 3
- down_weight: bfloat16 [3072, 768], P('seg'), may hold values from -0.109375 to 0.109375
- down_bias: bfloat16 [768], P('seg'), may hold values from -3 to 3
- norm2_gain: bfloat16 [768], P('seg'), may hold values from 0.099609375 to 1.8984375
- norm2_bias: bfloat16 [768], P('seg'), may hold values from -3 to 3
- deep_qkv_weight: bfloat16 [768, 2304], P('seg'), may hold values from -0.21875 to 0.21875
- deep_qv_bias: bfloat16 [1536], P('seg'), may hold values from -3 to 3
- deep_out_weight: bfloat16 [768, 768], P('seg'), may hold values from -2 to 2
- deep_out_bias: bfloat16 [768], P('seg'), may hold values from -3 to 3
- deep_norm1_gain: bfloat16 [768], P('seg'), may hold values from 0.099609375 to 1.8984375
- deep_norm1_bias: bfloat16 [768], P('seg'), may hold values from -3 to 3
- deep_up_weight: bfloat16 [768, 3072], P('seg'), may hold values from -0.21875 to 0.21875
- deep_up_bias: bfloat16 [3072], P('seg'), may hold values from -3 to 3
- deep_down_weight: bfloat16 [3072, 768], P('seg'), may hold values from -0.109375 to 0.109375
- deep_down_bias: bfloat16 [768], P('seg'), may hold values from -3 to 3
- deep_norm2_gain: bfloat16 [768], P('seg'), may hold values from 0.099609375 to 1.8984375
- deep_norm2_bias: bfloat16 [768], P('seg'), may hold values from -3 to 3
Outputs:
- layer_out: bfloat16 [8, 16, 84, 768], P('item', 'seg')
- text_grad: float32 [8, 16, 64, 768], P('item', 'seg')
- memory_grad: float32 [10, 768], P(None, 'seg')
- qkv_weight_grad: float32 [768, 2304], P('seg')
- qv_bias_grad: float32 [1536], P('seg')
- out_weight_grad: float32 [768, 768], P('seg')
- out_bias_grad: float32 [768], P('seg')
- norm1_gain_grad: float32 [768], P('seg')
- norm1_bias_grad: float32 [768], P('seg')
- up_weight_grad: float32 [768, 3072], P('seg')
- up_bias_grad: float32 [3072], P('seg')
- down_weight_grad: float32 [3072, 768], P('seg')
- down_bias_grad: float32 [768], P('seg')
- norm2_gain_grad: float32 [768], P('seg')
- norm2_bias_grad: float32 [768], P('seg')
- deep_qkv_weight_grad: float32 [768, 2304], P('seg')
- deep_qv_bias_grad: float32 [1536], P('seg')
- deep_out_weight_grad: float32 [768, 768], P('seg')
- deep_out_bias_grad: float32 [768], P('seg')
- deep_norm1_gain_grad: float32 [768], P('seg')
- deep_norm1_bias_grad: float32 [768], P('seg')
- deep_up_weight_grad: float32 [768, 3072], P('seg')
- deep_up_bias_grad: float32 [3072], P('seg')
- deep_down_weight_grad: float32 [3072, 768], P('seg')
- deep_down_bias_grad: float32 [768], P('seg')
- deep_norm2_gain_grad: float32 [768], P('seg')
- deep_norm2_bias_grad: float32 [768], P('seg')
Inputs may be any that keep to these rules, and one draw needn't show every extreme that they name: Among the items of each aligned group of 4 items (one index of item) at least one has unroll 16.
All inputs are finite; a program needn't handle non-finite values.
Results may differ from a plain program's by a relative error of at most 0.029.
Values may be sent and summed in bfloat16 or wider, within the bound.
No kernel may reach another device: no remote copies, remote signals or barrier semaphores. Data moves between devices by JAX's collectives and lax.ppermute only.
A program may use at most 256 MiB of HBM per device.

v0:
```python
import jax
import jax.numpy as jnp
from jax import lax
from jax.sharding import PartitionSpec as P

HEADS = 12
HEAD_DIM = 64


epsilon = 1e-05


def from_behind(value, axis, steps):
    count = lax.axis_size(axis)
    first, last = (max(0, -steps), min(count, count - steps))
    return lax.ppermute(value, axis, [(source, source + steps) for source in range(first, last)])


def norm_rows(total, gain, shift):
    centre = total - jnp.mean(total, -1, keepdims=True)
    spread = jnp.mean(centre * centre, -1, keepdims=True)
    return centre * lax.rsqrt(spread + epsilon) * gain + shift


def gelu_exact(value):
    return jax.nn.gelu(value, approximate=False)


def matmul(left, right):
    return jnp.dot(left, right, preferred_element_type=jnp.float32)


def rows_product(left, right):
    return lax.dot_general(
        left, right, (((0,), (0,)), ((), ())), preferred_element_type=jnp.float32
    )


def cols_product(left, right):
    return lax.dot_general(
        left, right, (((1,), (1,)), ((), ())), preferred_element_type=jnp.float32
    )


def split_heads(block):
    return block.reshape(block.shape[0], HEADS, block.shape[1] // HEADS)


def qkv_parts(qkv_low):
    width = qkv_low.shape[1] // 3
    return (
        split_heads(qkv_low[:, :width]),
        split_heads(qkv_low[:, width : 2 * width]),
        split_heads(qkv_low[:, 2 * width :]),
    )


def scores_of(query, keys):
    return jnp.einsum(
        "qhe,khe->hqk", query, keys, preferred_element_type=jnp.float32
    ) * HEAD_DIM ** (-0.5)


def layer_forward(inputs, weights):
    (
        qkv_weight,
        qv_bias,
        out_weight,
        out_bias,
        norm1_gain,
        norm1_bias,
        up_weight,
        up_bias,
        down_weight,
        down_bias,
        norm2_gain,
        norm2_bias,
    ) = weights
    rows, width = inputs.shape
    inputs_low = inputs.astype(jnp.bfloat16)
    wide_bias = qv_bias.astype(jnp.float32)
    bias_full = jnp.concatenate(
        [wide_bias[:width], jnp.zeros((width,), jnp.float32), wide_bias[width:]]
    )
    qkv_low = (matmul(inputs_low, qkv_weight) + bias_full).astype(jnp.bfloat16)
    query, keys, values = qkv_parts(qkv_low)
    scores = scores_of(query, keys)
    log_total = jax.nn.logsumexp(scores, axis=-1)
    probs_low = jnp.exp(scores - log_total[:, :, None]).astype(jnp.bfloat16)
    context = jnp.einsum("hqk,khe->qhe", probs_low, values, preferred_element_type=jnp.float32)
    context = context.reshape(rows, width).astype(jnp.bfloat16)
    first = inputs + matmul(context, out_weight) + out_bias.astype(jnp.float32)
    hidden = norm_rows(first, norm1_gain.astype(jnp.float32), norm1_bias.astype(jnp.float32))
    upper = matmul(hidden.astype(jnp.bfloat16), up_weight) + up_bias.astype(jnp.float32)
    activated = gelu_exact(upper).astype(jnp.bfloat16)
    second = hidden + matmul(activated, down_weight) + down_bias.astype(jnp.float32)
    result = norm_rows(second, norm2_gain.astype(jnp.float32), norm2_bias.astype(jnp.float32))
    return (result, (inputs_low, qkv_low, log_total, context, first, upper, second))


def layer_backward(grad_out, saved, weights):
    (
        qkv_weight,
        qv_bias,
        out_weight,
        out_bias,
        norm1_gain,
        norm1_bias,
        up_weight,
        up_bias,
        down_weight,
        down_bias,
        norm2_gain,
        norm2_bias,
    ) = weights
    inputs_low, qkv_low, log_total, context, first, upper, second = saved
    rows, width = first.shape
    _, pull_two = jax.vjp(
        norm_rows, second, norm2_gain.astype(jnp.float32), norm2_bias.astype(jnp.float32)
    )
    grad_second, grad_gain_two, grad_shift_two = pull_two(grad_out)
    grad_down = grad_second.astype(jnp.bfloat16)
    _, pull_gelu = jax.vjp(gelu_exact, upper)
    grad_upper = pull_gelu(cols_product(grad_down, down_weight))[0].astype(jnp.bfloat16)
    _, pull_one = jax.vjp(
        norm_rows, first, norm1_gain.astype(jnp.float32), norm1_bias.astype(jnp.float32)
    )
    grad_hidden = grad_second + cols_product(grad_upper, up_weight)
    grad_first, grad_gain_one, grad_shift_one = pull_one(grad_hidden)
    grad_proj = grad_first.astype(jnp.bfloat16)
    grad_context = split_heads(cols_product(grad_proj, out_weight).astype(jnp.bfloat16))
    query, keys, values = qkv_parts(qkv_low)
    probs = jnp.exp(scores_of(query, keys) - log_total[:, :, None])
    grad_values = jnp.einsum(
        "hqk,qhe->khe", probs.astype(jnp.bfloat16), grad_context, preferred_element_type=jnp.float32
    )
    grad_probs = jnp.einsum(
        "qhe,khe->hqk", grad_context, values, preferred_element_type=jnp.float32
    )
    grad_scores = probs * (grad_probs - jnp.sum(probs * grad_probs, -1, keepdims=True))
    grad_scores = grad_scores.astype(jnp.bfloat16)
    scale = HEAD_DIM ** (-0.5)
    grad_query = (
        jnp.einsum("hqk,khe->qhe", grad_scores, keys, preferred_element_type=jnp.float32) * scale
    )
    grad_keys = (
        jnp.einsum("hqk,qhe->khe", grad_scores, query, preferred_element_type=jnp.float32) * scale
    )
    grad_qkv = jnp.concatenate(
        [
            grad_query.reshape(rows, width),
            grad_keys.reshape(rows, width),
            grad_values.reshape(rows, width),
        ],
        axis=1,
    ).astype(jnp.bfloat16)
    grad_inputs = grad_first + cols_product(grad_qkv, qkv_weight)
    column_sums = jnp.sum(grad_qkv.astype(jnp.float32), 0)
    vector_terms = (
        jnp.concatenate([column_sums[:width], column_sums[2 * width :]]),
        jnp.sum(grad_proj.astype(jnp.float32), 0),
        grad_gain_one,
        grad_shift_one,
        jnp.sum(grad_upper.astype(jnp.float32), 0),
        jnp.sum(grad_down.astype(jnp.float32), 0),
        grad_gain_two,
        grad_shift_two,
    )
    return (grad_inputs, (grad_qkv, grad_proj, grad_upper, grad_down), vector_terms)


def flatten(block):
    return block.reshape(block.shape[0] * block.shape[1], block.shape[2])


def empty_store(micro, rows, width, hidden_units):
    return (
        jnp.zeros((micro, rows, width), jnp.bfloat16),
        jnp.zeros((micro, rows, 3 * width), jnp.bfloat16),
        jnp.zeros((micro, HEADS, rows), jnp.float32),
        jnp.zeros((micro, rows, width), jnp.bfloat16),
        jnp.zeros((micro, rows, width), jnp.float32),
        jnp.zeros((micro, rows, hidden_units), jnp.float32),
        jnp.zeros((micro, rows, width), jnp.float32),
    )


def empty_grads(micro, rows, width, hidden_units):
    return (
        jnp.zeros((micro, rows, 3 * width), jnp.bfloat16),
        jnp.zeros((micro, rows, width), jnp.bfloat16),
        jnp.zeros((micro, rows, hidden_units), jnp.bfloat16),
        jnp.zeros((micro, rows, width), jnp.bfloat16),
    )


def empty_vectors(width, hidden_units):
    return (
        jnp.zeros((2 * width,), jnp.float32),
        jnp.zeros((width,), jnp.float32),
        jnp.zeros((width,), jnp.float32),
        jnp.zeros((width,), jnp.float32),
        jnp.zeros((hidden_units,), jnp.float32),
        jnp.zeros((width,), jnp.float32),
        jnp.zeros((width,), jnp.float32),
        jnp.zeros((width,), jnp.float32),
    )


def put_all(held, values, index):
    return tuple(
        (
            lax.dynamic_update_index_in_dim(buffer, value, index, 0)
            for buffer, value in zip(held, values)
        )
    )


def take_all(held, index):
    return tuple((lax.dynamic_index_in_dim(buffer, index, 0, keepdims=False) for buffer in held))


def factors_of(held, grads, weights):
    inputs_all, qkv_all, log_all, context_all, first_all, upper_all, second_all = held
    hidden_low = norm_rows(
        first_all, weights[4].astype(jnp.float32), weights[5].astype(jnp.float32)
    ).astype(jnp.bfloat16)
    activated_all = gelu_exact(upper_all).astype(jnp.bfloat16)
    return (
        (flatten(inputs_all), flatten(grads[0])),
        (flatten(context_all), flatten(grads[1])),
        (flatten(hidden_low), flatten(grads[2])),
        (flatten(activated_all), flatten(grads[3])),
    )


def body(
    text,
    cotangent,
    unroll,
    memory,
    qkv_weight,
    qv_bias,
    out_weight,
    out_bias,
    norm1_gain,
    norm1_bias,
    up_weight,
    up_bias,
    down_weight,
    down_bias,
    norm2_gain,
    norm2_bias,
    deep_qkv_weight,
    deep_qv_bias,
    deep_out_weight,
    deep_out_bias,
    deep_norm1_gain,
    deep_norm1_bias,
    deep_up_weight,
    deep_up_bias,
    deep_down_weight,
    deep_down_bias,
    deep_norm2_gain,
    deep_norm2_bias,
):
    gathered = (
        lax.all_gather(qkv_weight, "seg", axis=0, tiled=True),
        lax.all_gather(qv_bias, "seg", axis=0, tiled=True),
        lax.all_gather(out_weight, "seg", axis=0, tiled=True),
        lax.all_gather(out_bias, "seg", axis=0, tiled=True),
        lax.all_gather(norm1_gain, "seg", axis=0, tiled=True),
        lax.all_gather(norm1_bias, "seg", axis=0, tiled=True),
        lax.all_gather(up_weight, "seg", axis=0, tiled=True),
        lax.all_gather(up_bias, "seg", axis=0, tiled=True),
        lax.all_gather(down_weight, "seg", axis=0, tiled=True),
        lax.all_gather(down_bias, "seg", axis=0, tiled=True),
        lax.all_gather(norm2_gain, "seg", axis=0, tiled=True),
        lax.all_gather(norm2_bias, "seg", axis=0, tiled=True),
        lax.all_gather(deep_qkv_weight, "seg", axis=0, tiled=True),
        lax.all_gather(deep_qv_bias, "seg", axis=0, tiled=True),
        lax.all_gather(deep_out_weight, "seg", axis=0, tiled=True),
        lax.all_gather(deep_out_bias, "seg", axis=0, tiled=True),
        lax.all_gather(deep_norm1_gain, "seg", axis=0, tiled=True),
        lax.all_gather(deep_norm1_bias, "seg", axis=0, tiled=True),
        lax.all_gather(deep_up_weight, "seg", axis=0, tiled=True),
        lax.all_gather(deep_up_bias, "seg", axis=0, tiled=True),
        lax.all_gather(deep_down_weight, "seg", axis=0, tiled=True),
        lax.all_gather(deep_down_bias, "seg", axis=0, tiled=True),
        lax.all_gather(deep_norm2_gain, "seg", axis=0, tiled=True),
        lax.all_gather(deep_norm2_bias, "seg", axis=0, tiled=True),
    )
    weights_one = tuple(gathered[:12])
    weights_two = tuple(gathered[12:])
    micro = text.shape[0]
    text_rows = text.shape[2]
    width = text.shape[3]
    mem_rows = memory.shape[0]
    rows = text_rows + 2 * mem_rows
    hidden_units = weights_one[6].shape[1]
    chain = lax.axis_size("seg")
    place = lax.axis_index("seg")
    steps = chain + micro - 1
    memory_wide = memory.astype(jnp.float32)
    text_all = text[:, 0]
    cotangent_all = cotangent[:, 0]
    slots = jnp.arange(micro, dtype=jnp.int32)

    def lookup(slot):
        index = jnp.clip(slot, 0, micro - 1)
        limit = jnp.sum(jnp.where(slots == index, unroll, 0))
        fresh = jnp.logical_or(place == 0, place == limit)
        active = jnp.logical_and(slot >= 0, slot < micro)
        return (index, fresh, active)

    empty_rows = jnp.zeros((mem_rows, width), jnp.bfloat16)
    store_start = (
        empty_store(micro, rows, width, hidden_units),
        empty_store(micro, rows, width, hidden_units),
        jnp.zeros((micro, rows, width), jnp.bfloat16),
    )

    def forward_step(step, state):
        inbox, buffers = state
        index, fresh, active = lookup(step - place)

        def forward_run(held):
            held_one, held_two, held_out = held
            read = jnp.where(fresh, memory_wide, inbox.astype(jnp.float32))
            segment_text = lax.dynamic_index_in_dim(text_all, index, 0, keepdims=False).astype(
                jnp.float32
            )
            inputs = jnp.concatenate([read, segment_text, memory_wide], axis=0)
            middle, saved_one = layer_forward(inputs, weights_one)
            result, saved_two = layer_forward(middle, weights_two)
            result_low = result.astype(jnp.bfloat16)
            held_one = put_all(held_one, saved_one, index)
            held_two = put_all(held_two, saved_two, index)
            held_out = lax.dynamic_update_index_in_dim(held_out, result_low, index, 0)
            return ((held_one, held_two, held_out), result_low[rows - mem_rows :])

        def forward_skip(held):
            return (held, empty_rows)

        buffers, outgoing = lax.cond(active, forward_run, forward_skip, buffers)
        inbox = from_behind(outgoing, "seg", 1)
        return (inbox, buffers)

    _, store = lax.fori_loop(0, steps, forward_step, (empty_rows, store_start))
    store_one, store_two, result_all = store
    back_start = (
        empty_grads(micro, rows, width, hidden_units),
        empty_grads(micro, rows, width, hidden_units),
        jnp.zeros((micro, text_rows, width), jnp.float32),
        empty_vectors(width, hidden_units),
        empty_vectors(width, hidden_units),
        jnp.zeros((mem_rows, width), jnp.float32),
    )

    def backward_step(step, state):
        inbox, carried = state
        index, fresh, active = lookup(step - (chain - 1 - place))

        def backward_run(held):
            grads_one, grads_two, text_held, vectors_one, vectors_two, memory_held = held
            saved_one = take_all(store_one, index)
            saved_two = take_all(store_two, index)
            grad_out = lax.dynamic_index_in_dim(cotangent_all, index, 0, keepdims=False).astype(
                jnp.float32
            )
            grad_out = jnp.concatenate(
                [
                    grad_out[: rows - mem_rows],
                    grad_out[rows - mem_rows :] + inbox.astype(jnp.float32),
                ],
                axis=0,
            )
            grad_middle, outs_two, terms_two = layer_backward(grad_out, saved_two, weights_two)
            grad_inputs, outs_one, terms_one = layer_backward(grad_middle, saved_one, weights_one)
            grads_one = put_all(grads_one, outs_one, index)
            grads_two = put_all(grads_two, outs_two, index)
            text_held = lax.dynamic_update_index_in_dim(
                text_held, grad_inputs[mem_rows : mem_rows + text_rows], index, 0
            )
            vectors_one = tuple((total + term for total, term in zip(vectors_one, terms_one)))
            vectors_two = tuple((total + term for total, term in zip(vectors_two, terms_two)))
            read_grad = grad_inputs[:mem_rows]
            memory_held = (
                memory_held + grad_inputs[rows - mem_rows :] + jnp.where(fresh, read_grad, 0.0)
            )
            send = jnp.where(fresh, 0.0, read_grad).astype(jnp.bfloat16)
            return ((grads_one, grads_two, text_held, vectors_one, vectors_two, memory_held), send)

        def backward_skip(held):
            return (held, empty_rows)

        carried, outgoing = lax.cond(active, backward_run, backward_skip, carried)
        inbox = from_behind(outgoing, "seg", -1)
        return (inbox, carried)

    _, carried = lax.fori_loop(0, steps, backward_step, (empty_rows, back_start))
    grads_one, grads_two, text_grad, vectors_one, vectors_two, memory_grad = carried
    factors_one = factors_of(store_one, grads_one, weights_one)
    factors_two = factors_of(store_two, grads_two, weights_two)
    fulls_one = [rows_product(left, right) for left, right in factors_one]
    fulls_two = [rows_product(left, right) for left, right in factors_two]
    shares = (
        lax.psum_scatter(
            fulls_one[0].astype(jnp.bfloat16), "seg", scatter_dimension=0, tiled=True
        ).astype(jnp.float32),
        lax.psum_scatter(
            fulls_one[1].astype(jnp.bfloat16), "seg", scatter_dimension=0, tiled=True
        ).astype(jnp.float32),
        lax.psum_scatter(
            fulls_one[2].astype(jnp.bfloat16), "seg", scatter_dimension=0, tiled=True
        ).astype(jnp.float32),
        lax.psum_scatter(
            fulls_one[3].astype(jnp.bfloat16), "seg", scatter_dimension=0, tiled=True
        ).astype(jnp.float32),
        lax.psum_scatter(
            fulls_two[0].astype(jnp.bfloat16), "seg", scatter_dimension=0, tiled=True
        ).astype(jnp.float32),
        lax.psum_scatter(
            fulls_two[1].astype(jnp.bfloat16), "seg", scatter_dimension=0, tiled=True
        ).astype(jnp.float32),
        lax.psum_scatter(
            fulls_two[2].astype(jnp.bfloat16), "seg", scatter_dimension=0, tiled=True
        ).astype(jnp.float32),
        lax.psum_scatter(
            fulls_two[3].astype(jnp.bfloat16), "seg", scatter_dimension=0, tiled=True
        ).astype(jnp.float32),
        lax.psum_scatter(
            vectors_one[0].astype(jnp.bfloat16), "seg", scatter_dimension=0, tiled=True
        ).astype(jnp.float32),
        lax.psum_scatter(
            vectors_one[1].astype(jnp.bfloat16), "seg", scatter_dimension=0, tiled=True
        ).astype(jnp.float32),
        lax.psum_scatter(
            vectors_one[2].astype(jnp.bfloat16), "seg", scatter_dimension=0, tiled=True
        ).astype(jnp.float32),
        lax.psum_scatter(
            vectors_one[3].astype(jnp.bfloat16), "seg", scatter_dimension=0, tiled=True
        ).astype(jnp.float32),
        lax.psum_scatter(
            vectors_one[4].astype(jnp.bfloat16), "seg", scatter_dimension=0, tiled=True
        ).astype(jnp.float32),
        lax.psum_scatter(
            vectors_one[5].astype(jnp.bfloat16), "seg", scatter_dimension=0, tiled=True
        ).astype(jnp.float32),
        lax.psum_scatter(
            vectors_one[6].astype(jnp.bfloat16), "seg", scatter_dimension=0, tiled=True
        ).astype(jnp.float32),
        lax.psum_scatter(
            vectors_one[7].astype(jnp.bfloat16), "seg", scatter_dimension=0, tiled=True
        ).astype(jnp.float32),
        lax.psum_scatter(
            vectors_two[0].astype(jnp.bfloat16), "seg", scatter_dimension=0, tiled=True
        ).astype(jnp.float32),
        lax.psum_scatter(
            vectors_two[1].astype(jnp.bfloat16), "seg", scatter_dimension=0, tiled=True
        ).astype(jnp.float32),
        lax.psum_scatter(
            vectors_two[2].astype(jnp.bfloat16), "seg", scatter_dimension=0, tiled=True
        ).astype(jnp.float32),
        lax.psum_scatter(
            vectors_two[3].astype(jnp.bfloat16), "seg", scatter_dimension=0, tiled=True
        ).astype(jnp.float32),
        lax.psum_scatter(
            vectors_two[4].astype(jnp.bfloat16), "seg", scatter_dimension=0, tiled=True
        ).astype(jnp.float32),
        lax.psum_scatter(
            vectors_two[5].astype(jnp.bfloat16), "seg", scatter_dimension=0, tiled=True
        ).astype(jnp.float32),
        lax.psum_scatter(
            vectors_two[6].astype(jnp.bfloat16), "seg", scatter_dimension=0, tiled=True
        ).astype(jnp.float32),
        lax.psum_scatter(
            vectors_two[7].astype(jnp.bfloat16), "seg", scatter_dimension=0, tiled=True
        ).astype(jnp.float32),
        lax.psum_scatter(
            memory_grad.astype(jnp.bfloat16), "seg", scatter_dimension=1, tiled=True
        ).astype(jnp.float32),
    )
    totals = (
        lax.psum(shares[0].astype(jnp.bfloat16), "item").astype(jnp.float32),
        lax.psum(shares[1].astype(jnp.bfloat16), "item").astype(jnp.float32),
        lax.psum(shares[2].astype(jnp.bfloat16), "item").astype(jnp.float32),
        lax.psum(shares[3].astype(jnp.bfloat16), "item").astype(jnp.float32),
        lax.psum(shares[4].astype(jnp.bfloat16), "item").astype(jnp.float32),
        lax.psum(shares[5].astype(jnp.bfloat16), "item").astype(jnp.float32),
        lax.psum(shares[6].astype(jnp.bfloat16), "item").astype(jnp.float32),
        lax.psum(shares[7].astype(jnp.bfloat16), "item").astype(jnp.float32),
        lax.psum(shares[8].astype(jnp.bfloat16), "item").astype(jnp.float32),
        lax.psum(shares[9].astype(jnp.bfloat16), "item").astype(jnp.float32),
        lax.psum(shares[10].astype(jnp.bfloat16), "item").astype(jnp.float32),
        lax.psum(shares[11].astype(jnp.bfloat16), "item").astype(jnp.float32),
        lax.psum(shares[12].astype(jnp.bfloat16), "item").astype(jnp.float32),
        lax.psum(shares[13].astype(jnp.bfloat16), "item").astype(jnp.float32),
        lax.psum(shares[14].astype(jnp.bfloat16), "item").astype(jnp.float32),
        lax.psum(shares[15].astype(jnp.bfloat16), "item").astype(jnp.float32),
        lax.psum(shares[16].astype(jnp.bfloat16), "item").astype(jnp.float32),
        lax.psum(shares[17].astype(jnp.bfloat16), "item").astype(jnp.float32),
        lax.psum(shares[18].astype(jnp.bfloat16), "item").astype(jnp.float32),
        lax.psum(shares[19].astype(jnp.bfloat16), "item").astype(jnp.float32),
        lax.psum(shares[20].astype(jnp.bfloat16), "item").astype(jnp.float32),
        lax.psum(shares[21].astype(jnp.bfloat16), "item").astype(jnp.float32),
        lax.psum(shares[22].astype(jnp.bfloat16), "item").astype(jnp.float32),
        lax.psum(shares[23].astype(jnp.bfloat16), "item").astype(jnp.float32),
        lax.psum(shares[24].astype(jnp.bfloat16), "item").astype(jnp.float32),
    )
    return (
        result_all[:, None],
        text_grad[:, None],
        totals[24],
        totals[0],
        totals[8],
        totals[1],
        totals[9],
        totals[10],
        totals[11],
        totals[2],
        totals[12],
        totals[3],
        totals[13],
        totals[14],
        totals[15],
        totals[4],
        totals[16],
        totals[5],
        totals[17],
        totals[18],
        totals[19],
        totals[6],
        totals[20],
        totals[7],
        totals[21],
        totals[22],
        totals[23],
    )


def solution(mesh):
    placed = (
        P("item", "seg", None, None),
        P("item", "seg", None, None),
        P("item"),
        P(),
        P("seg", None),
        P("seg"),
        P("seg", None),
        P("seg"),
        P("seg"),
        P("seg"),
        P("seg", None),
        P("seg"),
        P("seg", None),
        P("seg"),
        P("seg"),
        P("seg"),
        P("seg", None),
        P("seg"),
        P("seg", None),
        P("seg"),
        P("seg"),
        P("seg"),
        P("seg", None),
        P("seg"),
        P("seg", None),
        P("seg"),
        P("seg"),
        P("seg"),
    )
    return jax.shard_map(
        body,
        mesh=mesh,
        in_specs=placed,
        out_specs=(
            P("item", "seg", None, None),
            P("item", "seg", None, None),
            P(None, "seg"),
            P("seg", None),
            P("seg"),
            P("seg", None),
            P("seg"),
            P("seg"),
            P("seg"),
            P("seg", None),
            P("seg"),
            P("seg", None),
            P("seg"),
            P("seg"),
            P("seg"),
            P("seg", None),
            P("seg"),
            P("seg", None),
            P("seg"),
            P("seg"),
            P("seg"),
            P("seg", None),
            P("seg"),
            P("seg", None),
            P("seg"),
            P("seg"),
            P("seg"),
        ),
        check_vma=False,
    )
```

profile of v0, /device:TPU:0, one launch (start us, length us, event | category | flops | bytes accessed | tf_op | source)
XLA Modules:
  0.0 4591.3 jit_solution(10154371050326582238)
XLA Ops:
  423.8 1107.2 %while.112 = (s32[]{:T(128)}, bf16[10,768]{1,0:T(8,128)(2,1)}, bf16[4,84,768]{2,1,0:T(8,128)(2,1)}, bf16[4,84,2304]{2,1,0:T(8,128)(2,1)}, f32[4,12,84]{2,1,0:T(8...) while((s32[]{:T(128)}, bf16[10,768]{1,0:T(8,128)(2,1)}, ...), condition=%wide.region_16.17_spmd.clone, body=%wide.region_0.16_spmd.clone.sunk | while | flops 2462462976 | bytes 69839656 | solution.py:349
  424.7 84.4 %conditional.6 = (bf16[4,84,768]{2,1,0:T(8,128)(2,1)}, bf16[4,84,2304]{2,1,0:T(8,128)(2,1)}, f32[4,12,84]{2,1,0:T(8,128)}, bf16[4,84,768]{1,2,0:T(8,128)(2,1)}, ...) conditional(s32[]{:T(128)} %convert_element_type.705, ...), branch_computations={%region_1.1_spmd, %region_2.15_spmd} | conditional | flops 2462462976 | bytes 69777216 | solution.py:345
  512.0 84.4 %conditional.6 = (bf16[4,84,768]{2,1,0:T(8,128)(2,1)}, bf16[4,84,2304]{2,1,0:T(8,128)(2,1)}, f32[4,12,84]{2,1,0:T(8,128)}, bf16[4,84,768]{1,2,0:T(8,128)(2,1)}, ...) conditional(s32[]{:T(128)} %convert_element_type.705, ...), branch_computations={%region_1.1_spmd, %region_2.15_spmd} | conditional | flops 2462462976 | bytes 69777216 | solution.py:345
  600.3 84.4 %conditional.6 = (bf16[4,84,768]{2,1,0:T(8,128)(2,1)}, bf16[4,84,2304]{2,1,0:T(8,128)(2,1)}, f32[4,12,84]{2,1,0:T(8,128)}, bf16[4,84,768]{1,2,0:T(8,128)(2,1)}, ...) conditional(s32[]{:T(128)} %convert_element_type.705, ...), branch_computations={%region_1.1_spmd, %region_2.15_spmd} | conditional | flops 2462462976 | bytes 69777216 | solution.py:345
  688.7 84.3 %conditional.6 = (bf16[4,84,768]{2,1,0:T(8,128)(2,1)}, bf16[4,84,2304]{2,1,0:T(8,128)(2,1)}, f32[4,12,84]{2,1,0:T(8,128)}, bf16[4,84,768]{1,2,0:T(8,128)(2,1)}, ...) conditional(s32[]{:T(128)} %convert_element_type.705, ...), branch_computations={%region_1.1_spmd, %region_2.15_spmd} | conditional | flops 2462462976 | bytes 69777216 | solution.py:345
  779.2 88.6 %collective-permute-start = (bf16[10,768]{1,0:T(8,128)(2,1)}, bf16[10,768]{1,0:T(8,128)(2,1)}, u32[]{:S(2)}, u32[]{:S(2)}) collective-permute-start(bf16[10,768]{1,0:T(8,128)(2,1)} %get-tuple-element.4409), channel_id=1, source_target_pairs={{0,2},{2,4},{4,6},{6,8},{8,10},{10,12},{12,14},{14,16},{16,18},{18... | collective-permute-start | bytes 46088 | tf_op jit(solution)/shard_map/while/body/eval_jaxpr/ppermute | solution.py:16
  876.2 88.6 %collective-permute-start = (bf16[10,768]{1,0:T(8,128)(2,1)}, bf16[10,768]{1,0:T(8,128)(2,1)}, u32[]{:S(2)}, u32[]{:S(2)}) collective-permute-start(bf16[10,768]{1,0:T(8,128)(2,1)} %get-tuple-element.4409), channel_id=1, source_target_pairs={{0,2},{2,4},{4,6},{6,8},{8,10},{10,12},{12,14},{14,16},{16,18},{18... | collective-permute-start | bytes 46088 | tf_op jit(solution)/shard_map/while/body/eval_jaxpr/ppermute | solution.py:16
  973.0 84.2 %collective-permute-start = (bf16[10,768]{1,0:T(8,128)(2,1)}, bf16[10,768]{1,0:T(8,128)(2,1)}, u32[]{:S(2)}, u32[]{:S(2)}) collective-permute-start(bf16[10,768]{1,0:T(8,128)(2,1)} %get-tuple-element.4409), channel_id=1, source_target_pairs={{0,2},{2,4},{4,6},{6,8},{8,10},{10,12},{12,14},{14,16},{16,18},{18... | collective-permute-start | bytes 46088 | tf_op jit(solution)/shard_map/while/body/eval_jaxpr/ppermute | solution.py:16
  1065.9 89.5 %collective-permute-start = (bf16[10,768]{1,0:T(8,128)(2,1)}, bf16[10,768]{1,0:T(8,128)(2,1)}, u32[]{:S(2)}, u32[]{:S(2)}) collective-permute-start(bf16[10,768]{1,0:T(8,128)(2,1)} %get-tuple-element.4409), channel_id=1, source_target_pairs={{0,2},{2,4},{4,6},{6,8},{8,10},{10,12},{12,14},{14,16},{16,18},{18... | collective-permute-start | bytes 46088 | tf_op jit(solution)/shard_map/while/body/eval_jaxpr/ppermute | solution.py:16
  1164.5 83.3 %collective-permute-start = (bf16[10,768]{1,0:T(8,128)(2,1)}, bf16[10,768]{1,0:T(8,128)(2,1)}, u32[]{:S(2)}, u32[]{:S(2)}) collective-permute-start(bf16[10,768]{1,0:T(8,128)(2,1)} %get-tuple-element.4409), channel_id=1, source_target_pairs={{0,2},{2,4},{4,6},{6,8},{8,10},{10,12},{12,14},{14,16},{16,18},{18... | collective-permute-start | bytes 46088 | tf_op jit(solution)/shard_map/while/body/eval_jaxpr/ppermute | solution.py:16
  1257.0 85.3 %collective-permute-start = (bf16[10,768]{1,0:T(8,128)(2,1)}, bf16[10,768]{1,0:T(8,128)(2,1)}, u32[]{:S(2)}, u32[]{:S(2)}) collective-permute-start(bf16[10,768]{1,0:T(8,128)(2,1)} %get-tuple-element.4409), channel_id=1, source_target_pairs={{0,2},{2,4},{4,6},{6,8},{8,10},{10,12},{12,14},{14,16},{16,18},{18... | collective-permute-start | bytes 46088 | tf_op jit(solution)/shard_map/while/body/eval_jaxpr/ppermute | solution.py:16
  1351.4 83.3 %collective-permute-start = (bf16[10,768]{1,0:T(8,128)(2,1)}, bf16[10,768]{1,0:T(8,128)(2,1)}, u32[]{:S(2)}, u32[]{:S(2)}) collective-permute-start(bf16[10,768]{1,0:T(8,128)(2,1)} %get-tuple-element.4409), channel_id=1, source_target_pairs={{0,2},{2,4},{4,6},{6,8},{8,10},{10,12},{12,14},{14,16},{16,18},{18... | collective-permute-start | bytes 46088 | tf_op jit(solution)/shard_map/while/body/eval_jaxpr/ppermute | solution.py:16
  1443.8 86.6 %collective-permute-start = (bf16[10,768]{1,0:T(8,128)(2,1)}, bf16[10,768]{1,0:T(8,128)(2,1)}, u32[]{:S(2)}, u32[]{:S(2)}) collective-permute-start(bf16[10,768]{1,0:T(8,128)(2,1)} %get-tuple-element.4409), channel_id=1, source_target_pairs={{0,2},{2,4},{4,6},{6,8},{8,10},{10,12},{12,14},{14,16},{16,18},{18... | collective-permute-start | bytes 46088 | tf_op jit(solution)/shard_map/while/body/eval_jaxpr/ppermute | solution.py:16
  1560.7 2324.6 %while.113 = (s32[]{:T(128)}, bf16[10,768]{1,0:T(8,128)(2,1)}, bf16[4,84,2304]{1,2,0:T(8,128)(2,1)}, bf16[4,84,768]{2,1,0:T(8,128)(2,1)}, bf16[4,84,3072]{2,1,0:...) while((s32[]{:T(128)}, bf16[10,768]{1,0:T(8,128)(2,1)}, ...), condition=%wide.region_56.57_spmd.clone, body=%wide.region_17.56_spmd.clone.sunk | while | flops 2541629952 | bytes 156375648 | solution.py:401
  1582.1 83.2 %collective-permute-done.1 = bf16[10,768]{1,0:T(8,128)(2,1)} collective-permute-done((bf16[10,768]{1,0:T(8,128)(2,1)}, bf16[10,768]{1,0:T(8,128)(2,1)}, u32[]{:S(2)}, u32[]{:S(2)}) %collective-permute-start.1) | collective-permute-done | bytes 15392 | tf_op jit(solution)/shard_map/while/body/eval_jaxpr/ppermute | solution.py:16
  1675.0 85.2 %collective-permute-done.1 = bf16[10,768]{1,0:T(8,128)(2,1)} collective-permute-done((bf16[10,768]{1,0:T(8,128)(2,1)}, bf16[10,768]{1,0:T(8,128)(2,1)}, u32[]{:S(2)}, u32[]{:S(2)}) %collective-permute-start.1) | collective-permute-done | bytes 15392 | tf_op jit(solution)/shard_map/while/body/eval_jaxpr/ppermute | solution.py:16
  1863.1 86.4 %collective-permute-done.1 = bf16[10,768]{1,0:T(8,128)(2,1)} collective-permute-done((bf16[10,768]{1,0:T(8,128)(2,1)}, bf16[10,768]{1,0:T(8,128)(2,1)}, u32[]{:S(2)}, u32[]{:S(2)}) %collective-permute-start.1) | collective-permute-done | bytes 15392 | tf_op jit(solution)/shard_map/while/body/eval_jaxpr/ppermute | solution.py:16
  2052.4 85.1 %collective-permute-done.1 = bf16[10,768]{1,0:T(8,128)(2,1)} collective-permute-done((bf16[10,768]{1,0:T(8,128)(2,1)}, bf16[10,768]{1,0:T(8,128)(2,1)}, u32[]{:S(2)}, u32[]{:S(2)}) %collective-permute-start.1) | collective-permute-done | bytes 15392 | tf_op jit(solution)/shard_map/while/body/eval_jaxpr/ppermute | solution.py:16
  2147.3 83.1 %collective-permute-done.1 = bf16[10,768]{1,0:T(8,128)(2,1)} collective-permute-done((bf16[10,768]{1,0:T(8,128)(2,1)}, bf16[10,768]{1,0:T(8,128)(2,1)}, u32[]{:S(2)}, u32[]{:S(2)}) %collective-permute-start.1) | collective-permute-done | bytes 15392 | tf_op jit(solution)/shard_map/while/body/eval_jaxpr/ppermute | solution.py:16
  2232.8 1283.3 %collective-permute-done.1 = bf16[10,768]{1,0:T(8,128)(2,1)} collective-permute-done((bf16[10,768]{1,0:T(8,128)(2,1)}, bf16[10,768]{1,0:T(8,128)(2,1)}, u32[]{:S(2)}, u32[]{:S(2)}) %collective-permute-start.1) | collective-permute-done | bytes 15392 | tf_op jit(solution)/shard_map/while/body/eval_jaxpr/ppermute | solution.py:16
  3516.6 86.1 %conditional.7 = (bf16[4,84,2304]{1,2,0:T(8,128)(2,1)}, bf16[4,84,768]{2,1,0:T(8,128)(2,1)}, bf16[4,84,3072]{2,1,0:T(8,128)(2,1)}, bf16[4,84,768]{2,1,0:T(8,128)...) conditional(s32[]{:T(128)} %convert_element_type.706, ...), branch_computations={%region_18.18_spmd, %region_19.55_spmd} | conditional | flops 2541629952 | bytes 156312960 | solution.py:397
  3609.5 86.1 %conditional.7 = (bf16[4,84,2304]{1,2,0:T(8,128)(2,1)}, bf16[4,84,768]{2,1,0:T(8,128)(2,1)}, bf16[4,84,3072]{2,1,0:T(8,128)(2,1)}, bf16[4,84,768]{2,1,0:T(8,128)...) conditional(s32[]{:T(128)} %convert_element_type.706, ...), branch_computations={%region_18.18_spmd, %region_19.55_spmd} | conditional | flops 2541629952 | bytes 156312960 | solution.py:397
  3702.4 86.0 %conditional.7 = (bf16[4,84,2304]{1,2,0:T(8,128)(2,1)}, bf16[4,84,768]{2,1,0:T(8,128)(2,1)}, bf16[4,84,3072]{2,1,0:T(8,128)(2,1)}, bf16[4,84,768]{2,1,0:T(8,128)...) conditional(s32[]{:T(128)} %convert_element_type.706, ...), branch_computations={%region_18.18_spmd, %region_19.55_spmd} | conditional | flops 2541629952 | bytes 156312960 | solution.py:397
  3795.4 86.1 %conditional.7 = (bf16[4,84,2304]{1,2,0:T(8,128)(2,1)}, bf16[4,84,768]{2,1,0:T(8,128)(2,1)}, bf16[4,84,3072]{2,1,0:T(8,128)(2,1)}, bf16[4,84,768]{2,1,0:T(8,128)...) conditional(s32[]{:T(128)} %convert_element_type.706, ...), branch_computations={%region_18.18_spmd, %region_19.55_spmd} | conditional | flops 2541629952 | bytes 156312960 | solution.py:397
  (2042 shorter events, 2172.6 us)
Async XLA Ops:
  8.7 131.1 %all-gather.9.cloned.1.call-start = ((), (), s32[]{:S(2)}) async-start(), calls=%async_computation.9 | async-start | bytes 3760128 | tf_op jit(solution)/shard_map/all_gather | solution.py:268
  9.5 178.7 %all-gather.17.cloned.1.call-start = ((), (), s32[]{:S(2)}) async-start(), calls=%async_computation.13 | async-start | bytes 3760128 | tf_op jit(solution)/shard_map/all_gather | solution.py:280
  10.0 232.7 %all-gather.13.cloned.1.call-start = ((), (), s32[]{:S(2)}) async-start(), calls=%async_computation.11 | async-start | bytes 5013504 | tf_op jit(solution)/shard_map/all_gather | solution.py:274
  10.8 286.0 %all-gather.15.cloned.1.call-start = ((), (), s32[]{:S(2)}) async-start(), calls=%async_computation.12 | async-start | bytes 5013504 | tf_op jit(solution)/shard_map/all_gather | solution.py:276
  11.4 339.7 %all-gather.21.cloned.1.call-start = ((), (), s32[]{:S(2)}) async-start(), calls=%async_computation.15 | async-start | bytes 5013504 | tf_op jit(solution)/shard_map/all_gather | solution.py:286
  12.1 393.2 %all-gather.23.cloned.1.call-start = ((), (), s32[]{:S(2)}) async-start(), calls=%async_computation.16 | async-start | bytes 5013504 | tf_op jit(solution)/shard_map/all_gather | solution.py:288
  12.9 3939.9 %reduce-scatter.14.cloned.1.call-start = ((), (), s32[]{:S(2)}) async-start(), calls=%async_computation.18 | async-start | bytes 1253376 | tf_op jit(solution)/shard_map/reduce_scatter | solution.py:411
  779.2 89.2 %collective-permute-start = (bf16[10,768]{1,0:T(8,128)(2,1)}, bf16[10,768]{1,0:T(8,128)(2,1)}, u32[]{:S(2)}, u32[]{:S(2)}) collective-permute-start(bf16[10,768]{1,0:T(8,128)(2,1)} %get-tuple-element.4409), channel_id=1, source_target_pairs={{0,2},{2,4},{4,6},{6,8},{8,10},{10,12},{12,14},{14,16},{16,18},{18... | collective-permute-start | bytes 46088 | tf_op jit(solution)/shard_map/while/body/eval_jaxpr/ppermute | solution.py:16
  876.2 89.1 %collective-permute-start = (bf16[10,768]{1,0:T(8,128)(2,1)}, bf16[10,768]{1,0:T(8,128)(2,1)}, u32[]{:S(2)}, u32[]{:S(2)}) collective-permute-start(bf16[10,768]{1,0:T(8,128)(2,1)} %get-tuple-element.4409), channel_id=1, source_target_pairs={{0,2},{2,4},{4,6},{6,8},{8,10},{10,12},{12,14},{14,16},{16,18},{18... | collective-permute-start | bytes 46088 | tf_op jit(solution)/shard_map/while/body/eval_jaxpr/ppermute | solution.py:16
  1065.9 90.0 %collective-permute-start = (bf16[10,768]{1,0:T(8,128)(2,1)}, bf16[10,768]{1,0:T(8,128)(2,1)}, u32[]{:S(2)}, u32[]{:S(2)}) collective-permute-start(bf16[10,768]{1,0:T(8,128)(2,1)} %get-tuple-element.4409), channel_id=1, source_target_pairs={{0,2},{2,4},{4,6},{6,8},{8,10},{10,12},{12,14},{14,16},{16,18},{18... | collective-permute-start | bytes 46088 | tf_op jit(solution)/shard_map/while/body/eval_jaxpr/ppermute | solution.py:16
  1443.8 87.2 %collective-permute-start = (bf16[10,768]{1,0:T(8,128)(2,1)}, bf16[10,768]{1,0:T(8,128)(2,1)}, u32[]{:S(2)}, u32[]{:S(2)}) collective-permute-start(bf16[10,768]{1,0:T(8,128)(2,1)} %get-tuple-element.4409), channel_id=1, source_target_pairs={{0,2},{2,4},{4,6},{6,8},{8,10},{10,12},{12,14},{14,16},{16,18},{18... | collective-permute-start | bytes 46088 | tf_op jit(solution)/shard_map/while/body/eval_jaxpr/ppermute | solution.py:16
  1673.7 86.5 %collective-permute-start.1 = (bf16[10,768]{1,0:T(8,128)(2,1)}, bf16[10,768]{1,0:T(8,128)(2,1)}, u32[]{:S(2)}, u32[]{:S(2)}) collective-permute-start(bf16[10,768]{1,0:T(8,128)(2,1)} %get-tuple-element.4480), channel_id=1, source_target_pairs={{2,0},{4,2},{6,4},{8,6},{10,8},{12,10},{14,12},{16,14},{18,16},{20... | collective-permute-start | bytes 46088 | tf_op jit(solution)/shard_map/while/body/eval_jaxpr/ppermute | solution.py:16
  1861.8 87.7 %collective-permute-start.1 = (bf16[10,768]{1,0:T(8,128)(2,1)}, bf16[10,768]{1,0:T(8,128)(2,1)}, u32[]{:S(2)}, u32[]{:S(2)}) collective-permute-start(bf16[10,768]{1,0:T(8,128)(2,1)} %get-tuple-element.4480), channel_id=1, source_target_pairs={{2,0},{4,2},{6,4},{8,6},{10,8},{12,10},{14,12},{16,14},{18,16},{20... | collective-permute-start | bytes 46088 | tf_op jit(solution)/shard_map/while/body/eval_jaxpr/ppermute | solution.py:16
  2051.1 86.4 %collective-permute-start.1 = (bf16[10,768]{1,0:T(8,128)(2,1)}, bf16[10,768]{1,0:T(8,128)(2,1)}, u32[]{:S(2)}, u32[]{:S(2)}) collective-permute-start(bf16[10,768]{1,0:T(8,128)(2,1)} %get-tuple-element.4480), channel_id=1, source_target_pairs={{2,0},{4,2},{6,4},{8,6},{10,8},{12,10},{14,12},{16,14},{18,16},{20... | collective-permute-start | bytes 46088 | tf_op jit(solution)/shard_map/while/body/eval_jaxpr/ppermute | solution.py:16
  2231.5 1284.6 %collective-permute-start.1 = (bf16[10,768]{1,0:T(8,128)(2,1)}, bf16[10,768]{1,0:T(8,128)(2,1)}, u32[]{:S(2)}, u32[]{:S(2)}) collective-permute-start(bf16[10,768]{1,0:T(8,128)(2,1)} %get-tuple-element.4480), channel_id=1, source_target_pairs={{2,0},{4,2},{6,4},{8,6},{10,8},{12,10},{14,12},{16,14},{18,16},{20... | collective-permute-start | bytes 46088 | tf_op jit(solution)/shard_map/while/body/eval_jaxpr/ppermute | solution.py:16
  3888.5 116.0 %reduce-scatter.22.cloned.1.call-start = ((), (), s32[]{:S(2)}) async-start(), calls=%async_computation.22 | async-start | bytes 1253376 | tf_op jit(solution)/shard_map/reduce_scatter | solution.py:423
  3891.5 183.9 %reduce-scatter.12.cloned.1.call-start = ((), (), s32[]{:S(2)}) async-start(), calls=%async_computation.17 | async-start | bytes 3760128 | tf_op jit(solution)/shard_map/reduce_scatter | solution.py:408
  3898.2 247.9 %reduce-scatter.20.cloned.1.call-start = ((), (), s32[]{:S(2)}) async-start(), calls=%async_computation.21 | async-start | bytes 3760128 | tf_op jit(solution)/shard_map/reduce_scatter | solution.py:420
  3904.8 319.5 %reduce-scatter.16.cloned.1.call-start = ((), (), s32[]{:S(2)}) async-start(), calls=%async_computation.19 | async-start | bytes 5013504 | tf_op jit(solution)/shard_map/reduce_scatter | solution.py:414
  3912.3 390.8 %reduce-scatter.18.cloned.1.call-start = ((), (), s32[]{:S(2)}) async-start(), calls=%async_computation.20 | async-start | bytes 5013504 | tf_op jit(solution)/shard_map/reduce_scatter | solution.py:417
  3927.9 453.5 %reduce-scatter.24.cloned.1.call-start = ((), (), s32[]{:S(2)}) async-start(), calls=%async_computation.23 | async-start | bytes 5013504 | tf_op jit(solution)/shard_map/reduce_scatter | solution.py:426
  3935.4 524.9 %reduce-scatter.26.cloned.1.call-start = ((), (), s32[]{:S(2)}) async-start(), calls=%async_computation.24 | async-start | bytes 5013504 | tf_op jit(solution)/shard_map/reduce_scatter | solution.py:429
  3951.0 582.8 %reduce-scatter.28.cloned.1.call-start = ((), (), s32[]{:S(2)}) async-start(), calls=%async_computation.25 | async-start | bytes 208896
  3952.7 623.3 %all-reduce.38.cloned.1.call-start = ((), (), s32[]{:S(2)}) async-start(), calls=%async_computation.26 | async-start | bytes 3538944 | tf_op jit(solution)/shard_map/psum | solution.py:485
  (532 other events, 3790.4 us)
Sparse Core Ops, SparseCore 0:
  10.4 41.2 all-gather.10
  53.9 37.2 all-gather.18
  93.5 46.2 all-gather.8
  141.9 46.1 all-gather.16
  190.3 52.3 all-gather.12
  244.8 51.9 all-gather.14
  299.1 51.9 all-gather.20
  353.4 51.9 all-gather.22
  3888.6 55.2 reduce-scatter.13
  3947.4 56.9 reduce-scatter.21
  4008.3 67.0 reduce-scatter.11
  4079.1 66.8 reduce-scatter.19
  4149.9 74.3 reduce-scatter.15
  4228.5 74.5 reduce-scatter.17
  4306.8 74.5 reduce-scatter.23
  4385.7 74.5 reduce-scatter.25
  4464.2 52.7 reduce-scatter.27
  4519.5 56.3 all-reduce.37
where the time goes:
time: 4610 us; the launch traced here: 4590 us
  waiting for transfers between devices  2790 us (61%)
  starting transfers between devices  765 us (17%)
  other arithmetic  343 us (7%)
  matrix products  290 us (6%)
  local copies, waits for them, and re-layouts  228 us (5%)
  blocking collectives  131 us (3%)
    ppermute x38, waiting for transfers between devices, from_behind(): lax.ppermute(value, axis, [(source, source + steps) for source in range(f...  1940 us
    ppermute x38, starting transfers between devices, from_behind(): lax.ppermute(value, axis, [(source, source + steps) for source in range(f...  764 us
    unnamed x2, blocking collectives  122 us
    dot_general x32, matrix products, matmul(): return jnp.dot(left, right, preferred_element_type=jnp.float32)  114 us
    dot_general x32, matrix products, cols_product(): lax.dot_general(left, right, (((1,), (1,)), ((), ())), preferred_element_...  95.7 us
  transfers between devices with their start and end apart: 56, of which 53 were waited for; matrix products, arithmetic and copies ran while one was open for 2% of the time, Pallas kernels for 0%

commit v1 on v0

v1 whole, which is shorter than its diff:
```python
import jax
import jax.numpy as jnp
from jax import lax
from jax.experimental import pallas as pl
from jax.experimental.pallas import tpu as pltpu
from jax.sharding import PartitionSpec as P

HEAD_DIM = 64
EPSILON = 1e-05
F32 = jnp.float32
LOW = jnp.bfloat16
NN = (((1,), (0,)), ((), ()))
NT = (((1,), (1,)), ((), ()))
TN = (((0,), (0,)), ((), ()))

PAD = 16
BLOCKS = 12
B_QUERY, B_VALUE, B_OUT, GAIN1, SHIFT1, B_UP, B_DOWN, GAIN2, SHIFT2 = 0, 1, 2, 3, 4, 5, 9, 10, 11


def dot(left, right, dims=NN):
    return lax.dot_general(left, right, dims, preferred_element_type=F32)


def norm_rows(total, gain, shift):
    centre = total - jnp.mean(total, -1, keepdims=True)
    scale = lax.rsqrt(jnp.mean(centre * centre, -1, keepdims=True) + EPSILON)
    unit = centre * scale
    return unit, scale, unit * gain + shift


def norm_back(grad, unit, scale, gain):
    t = grad * gain
    return scale * (
        t - jnp.mean(t, -1, keepdims=True) - unit * jnp.mean(t * unit, -1, keepdims=True)
    )


def gelu_and_slope(upper):
    density = jnp.exp(upper * upper * -0.5) * 0.3989422804014327
    below = 0.5 * (1.0 + lax.erf(upper * 0.7071067811865476))
    return upper * below, below + upper * density


def fold(block):
    rows, width = block.shape
    return jnp.sum(block.reshape(rows // 8, 8, width), 0)


def two_heads(block, first):
    zero = jnp.zeros_like(block)
    return jnp.concatenate([jnp.where(first, block, zero), jnp.where(first, zero, block)], 0)


def load_weights(gathered, held, width, sem):
    shards = gathered.shape[0]
    part = width // shards

    def copies(shard):
        out = []
        for layer in range(2):
            src, dst = layer * BLOCKS * part, layer * BLOCKS * width
            for block in range(8):
                out.append((src + block * part, dst + block * width + shard * part, part))
            out.append((src + 8 * part, dst + 8 * width + shard * 4 * part, 4 * part))
        return [
            pltpu.make_async_copy(
                gathered.at[shard, pl.ds(a, n)], held.at[pl.ds(pl.multiple_of(b, 16), n)], sem
            )
            for a, b, n in out
        ]

    def start(shard, none):
        for copy in copies(shard):
            copy.start()
        return none

    def wait(shard, none):
        for copy in copies(shard):
            copy.wait()
        return none

    lax.fori_loop(0, shards, start, 0)
    lax.fori_loop(0, shards, wait, 0)


def forward_kernel(
    fresh_ref, text_ref, memory_ref, vector_ref, gathered_ref,
    low_ref, qkv_ref, probs_ref, context_ref, unit1_ref, hidden_ref, active_ref, slope_ref,
    unit2_ref, scale_ref, out_ref,
    held, carry, state, sem,
):
    step = pl.program_id(0)
    rows, width = state.shape
    texts = rows - 2 * PAD
    mem = 10

    @pl.when(step == 0)
    def _():
        load_weights(gathered_ref, held, width, sem)
        carry[...] = jnp.zeros_like(carry)

    column = lax.broadcasted_iota(jnp.int32, (2 * rows, rows), 1)
    unused = jnp.logical_or(
        column >= texts + PAD + mem,
        jnp.logical_and(column >= texts + mem, column < texts + PAD),
    )
    mask = jnp.where(unused, -1e30, 0.0).astype(F32)
    first_head = lax.broadcasted_iota(jnp.int32, (rows, 2 * HEAD_DIM), 1) < HEAD_DIM

    memory = memory_ref[...]
    state[:texts] = text_ref[0].astype(F32)
    state[texts : texts + PAD] = jnp.where(fresh_ref[step] > 0, memory, carry[...]).astype(F32)
    state[texts + PAD :] = memory.astype(F32)

    def layer(index, none):
        def weight(block):
            return held[pl.ds(pl.multiple_of((index * BLOCKS + block) * width, width), width), :]

        def vector(row):
            return vector_ref[index, row : row + 1, :]

        x = state[...]
        low = x.astype(LOW)
        low_ref[0, index] = low
        query = (dot(low, weight(0)) + vector(B_QUERY)).astype(LOW)
        keys = dot(low, weight(1)).astype(LOW)
        values = (dot(low, weight(2)) + vector(B_VALUE)).astype(LOW)
        qkv_ref[0, index, :, :width] = query
        qkv_ref[0, index, :, width : 2 * width] = keys
        qkv_ref[0, index, :, 2 * width :] = values
        for pair in range(width // (2 * HEAD_DIM)):
            cols = slice(2 * HEAD_DIM * pair, 2 * HEAD_DIM * (pair + 1))
            scores = dot(two_heads(query[:, cols], first_head), keys[:, cols], NT)
            scores = scores * HEAD_DIM ** (-0.5) + mask
            weights = jnp.exp(scores - jnp.max(scores, -1, keepdims=True))
            probs = (weights / jnp.sum(weights, -1, keepdims=True)).astype(LOW)
            probs_ref[0, index, pair] = probs
            both = dot(probs, values[:, cols])
            context_ref[0, index, :, cols] = jnp.where(
                first_head, both[:rows], both[rows:]
            ).astype(LOW)
        first = x + dot(context_ref[0, index], weight(3)) + vector(B_OUT)
        unit, scale, hidden = norm_rows(first, vector(GAIN1), vector(SHIFT1))
        unit1_ref[0, index] = unit.astype(LOW)
        scale_ref[0, index, 0] = jnp.broadcast_to(scale, (rows, 128))
        hidden_low = hidden.astype(LOW)
        hidden_ref[0, index] = hidden_low
        second = hidden + vector(B_DOWN)
        for block in range(4):
            cols = slice(block * width, (block + 1) * width)
            upper = dot(hidden_low, weight(4 + block)) + vector(B_UP + block)
            active, slope = gelu_and_slope(upper)
            active = active.astype(LOW)
            active_ref[0, index, :, cols] = active
            slope_ref[0, index, :, cols] = slope.astype(LOW)
            second = second + dot(active, weight(8 + block))
        unit, scale, final = norm_rows(second, vector(GAIN2), vector(SHIFT2))
        unit2_ref[0, index] = unit.astype(LOW)
        scale_ref[0, index, 1] = jnp.broadcast_to(scale, (rows, 128))
        state[...] = final
        return none

    lax.fori_loop(0, 2, layer, 0)
    final = state[...].astype(LOW)
    out_ref[0] = final
    carry[...] = final[texts + PAD :]


def backward_kernel(
    fresh_ref, cotangent_ref, vector_ref, qkv_ref, probs_ref, unit1_ref, slope_ref, unit2_ref,
    scale_ref, gathered_ref,
    grad_qkv_ref, grad_proj_ref, grad_upper_ref, grad_down_ref, text_ref, narrow_ref, wide_ref,
    memory_ref,
    held, carry, state, sem,
):
    turn = pl.program_id(0)
    step = pl.num_programs(0) - 1 - turn
    rows, width = state.shape
    texts = rows - 2 * PAD

    @pl.when(turn == 0)
    def _():
        load_weights(gathered_ref, held, width, sem)
        carry[...] = jnp.zeros_like(carry)
        narrow_ref[...] = jnp.zeros_like(narrow_ref)
        wide_ref[...] = jnp.zeros_like(wide_ref)
        memory_ref[...] = jnp.zeros_like(memory_ref)

    first_head = lax.broadcasted_iota(jnp.int32, (rows, 2 * HEAD_DIM), 1) < HEAD_DIM
    state[: texts + PAD] = cotangent_ref[0, : texts + PAD].astype(F32)
    state[texts + PAD :] = cotangent_ref[0, texts + PAD :].astype(F32) + carry[...].astype(F32)

    def layer(turned, none):
        index = 1 - turned

        def weight(block):
            return held[pl.ds(pl.multiple_of((index * BLOCKS + block) * width, width), width), :]

        def vector(row):
            return vector_ref[index, row : row + 1, :]

        grad = state[...]
        unit = unit2_ref[0, index].astype(F32)
        narrow_ref[index, 0] += fold(grad * unit)
        narrow_ref[index, 1] += fold(grad)
        grad_second = norm_back(grad, unit, scale_ref[0, index, 1, :, 0:1], vector(GAIN2))
        narrow_ref[index, 2] += fold(grad_second)
        grad_down = grad_second.astype(LOW)
        grad_hidden = grad_second
        for block in range(4):
            cols = slice(block * width, (block + 1) * width)
            grad_upper = dot(grad_down, weight(8 + block), NT) * slope_ref[0, index, :, cols].astype(F32)
            wide_ref[index, block] += fold(grad_upper)
            grad_upper = grad_upper.astype(LOW)
            grad_upper_ref[0, index, :, cols] = grad_upper
            grad_hidden = grad_hidden + dot(grad_upper, weight(4 + block), NT)
        grad_down_ref[0, index] = grad_down
        unit = unit1_ref[0, index].astype(F32)
        narrow_ref[index, 3] += fold(grad_hidden * unit)
        narrow_ref[index, 4] += fold(grad_hidden)
        grad_first = norm_back(grad_hidden, unit, scale_ref[0, index, 0, :, 0:1], vector(GAIN1))
        narrow_ref[index, 5] += fold(grad_first)
        grad_proj = grad_first.astype(LOW)
        grad_proj_ref[0, index] = grad_proj
        grad_context = dot(grad_proj, weight(3), NT).astype(LOW)
        for pair in range(width // (2 * HEAD_DIM)):
            cols = slice(2 * HEAD_DIM * pair, 2 * HEAD_DIM * (pair + 1))
            in_keys = slice(width + cols.start, width + cols.stop)
            in_values = slice(2 * width + cols.start, 2 * width + cols.stop)
            query = two_heads(qkv_ref[0, index, :, cols], first_head)
            keys = qkv_ref[0, index, :, in_keys]
            values = qkv_ref[0, index, :, in_values]
            context = two_heads(grad_context[:, cols], first_head)
            probs_low = probs_ref[0, index, pair]
            probs = probs_low.astype(F32)
            term = dot(context, values, NT) * probs
            grad_scores = term - probs * jnp.sum(term, -1, keepdims=True)
            grad_scores = (grad_scores * HEAD_DIM ** (-0.5)).astype(LOW)
            both = dot(grad_scores, keys)
            grad_query = jnp.where(first_head, both[:rows], both[rows:])
            grad_keys = dot(grad_scores, query, TN)
            grad_values = dot(probs_low, context, TN)
            narrow_ref[index, 6, :, cols] += fold(grad_query)
            narrow_ref[index, 7, :, cols] += fold(grad_values)
            grad_qkv_ref[0, index, :, cols] = grad_query.astype(LOW)
            grad_qkv_ref[0, index, :, in_keys] = grad_keys.astype(LOW)
            grad_qkv_ref[0, index, :, in_values] = grad_values.astype(LOW)
        grad_inputs = grad_first
        for block in range(3):
            cols = slice(block * width, (block + 1) * width)
            grad_inputs = grad_inputs + dot(grad_qkv_ref[0, index, :, cols], weight(block), NT)
        state[...] = grad_inputs
        return none

    lax.fori_loop(0, 2, layer, 0)
    text_ref[0] = state[:texts].astype(LOW)
    read = state[texts : texts + PAD]
    fresh = fresh_ref[step] > 0
    memory_ref[...] += state[texts + PAD :] + jnp.where(fresh, read, 0.0)
    carry[...] = jnp.where(fresh, 0.0, read).astype(LOW)


SMEM = pl.BlockSpec(memory_space=pltpu.SMEM)
VMEM = pl.BlockSpec(memory_space=pltpu.VMEM)
ANY = pl.BlockSpec(memory_space=pl.ANY)


def scratch(rows, width):
    return [
        pltpu.VMEM((2 * BLOCKS * width, width), LOW),
        pltpu.VMEM((PAD, width), LOW),
        pltpu.VMEM((rows, width), F32),
        pltpu.SemaphoreType.DMA,
    ]


def cost(rows, width, segments):
    return pl.CostEstimate(
        flops=2 * rows * 2 * BLOCKS * width * width * segments,
        bytes_accessed=2 * 2 * BLOCKS * width * width,
        transcendentals=0,
    )


def forward_chain(fresh, text, memory, vectors, gathered):
    segments, texts, width = text.shape
    rows = texts + 2 * PAD
    pairs = width // (2 * HEAD_DIM)

    def block(shape):
        return pl.BlockSpec((1,) + shape, lambda s: (s,) + (0,) * len(shape))

    outs = [
        ((2, rows, width), LOW),
        ((2, rows, 3 * width), LOW),
        ((2, pairs, 2 * rows, rows), LOW),
        ((2, rows, width), LOW),
        ((2, rows, width), LOW),
        ((2, rows, width), LOW),
        ((2, rows, 4 * width), LOW),
        ((2, rows, 4 * width), LOW),
        ((2, rows, width), LOW),
        ((2, 2, rows, 128), F32),
        ((rows, width), LOW),
    ]
    return pl.pallas_call(
        forward_kernel,
        grid=(segments,),
        in_specs=[SMEM, block((texts, width)), VMEM, VMEM, ANY],
        out_specs=[block(shape) for shape, _ in outs],
        out_shape=[jax.ShapeDtypeStruct((segments,) + shape, kind) for shape, kind in outs],
        scratch_shapes=scratch(rows, width),
        compiler_params=pltpu.CompilerParams(vmem_limit_bytes=62 << 20),
        cost_estimate=cost(rows, width, segments),
        name="forward_chain",
    )(fresh, text, memory, vectors, gathered)


def backward_chain(fresh, cotangent, vectors, qkv, probs, unit1, slope, unit2, scale, gathered):
    segments, rows, width = cotangent.shape
    texts = rows - 2 * PAD
    pairs = width // (2 * HEAD_DIM)

    def block(shape):
        return pl.BlockSpec((1,) + shape, lambda t: (segments - 1 - t,) + (0,) * len(shape))

    outs = [
        ((2, rows, 3 * width), LOW),
        ((2, rows, width), LOW),
        ((2, rows, 4 * width), LOW),
        ((2, rows, width), LOW),
        ((texts, width), LOW),
    ]
    return pl.pallas_call(
        backward_kernel,
        grid=(segments,),
        in_specs=[
            SMEM,
            block((rows, width)),
            VMEM,
            block((2, rows, 3 * width)),
            block((2, pairs, 2 * rows, rows)),
            block((2, rows, width)),
            block((2, rows, 4 * width)),
            block((2, rows, width)),
            block((2, 2, rows, 128)),
            ANY,
        ],
        out_specs=[block(shape) for shape, _ in outs] + [VMEM, VMEM, VMEM],
        out_shape=[jax.ShapeDtypeStruct((segments,) + shape, kind) for shape, kind in outs]
        + [
            jax.ShapeDtypeStruct((2, 8, 8, width), F32),
            jax.ShapeDtypeStruct((2, 4, 8, width), F32),
            jax.ShapeDtypeStruct((PAD, width), F32),
        ],
        scratch_shapes=scratch(rows, width),
        input_output_aliases={3: 0, 5: 1, 6: 2, 7: 3},
        compiler_params=pltpu.CompilerParams(vmem_limit_bytes=62 << 20),
        cost_estimate=cost(rows, width, segments),
        name="backward_chain",
    )(fresh, cotangent, vectors, qkv, probs, unit1, slope, unit2, scale, gathered)


def split_columns(shard, width):
    rows, columns = shard.shape
    return [shard[:, i : i + width] for i in range(0, columns, width)]


def body(text, cotangent, unroll, memory, *weights):
    micro, _, texts, width = text.shape
    mem = memory.shape[0]
    chain = lax.axis_size("seg")
    place = lax.axis_index("seg")
    stride = 2 if 2 * micro <= chain else 1
    start = (chain - stride * micro) // 2
    homes = [start + stride * i for i in range(micro)]
    layers = (weights[:12], weights[12:])

    vectors = jnp.concatenate([v for w in layers for v in w if v.ndim == 1])
    vectors = lax.all_gather(vectors, "seg").astype(F32)
    shards = []
    for w in layers:
        for matrix in (w[0], w[2], w[6], w[8]):
            shards += split_columns(matrix, width)
    gathered = lax.all_gather(jnp.concatenate(shards), "seg")
    part = width // chain
    if part % 16:
        together = 16 // (part & -part) if part & -part < 16 else 1
        gathered = regroup(gathered, together, part)
    rows_of = []
    at = 0
    for w in layers:
        for v in w:
            if v.ndim == 1:
                rows_of.append(vectors[:, at : at + v.shape[0]].reshape(-1, width))
                at += v.shape[0]
    half = len(rows_of) // 2
    table = jnp.stack([jnp.concatenate(rows_of[:half]), jnp.concatenate(rows_of[half:])])
    table = jnp.pad(table, ((0, 0), (0, 16 - table.shape[1]), (0, 0)))

    def to_home(blocks):
        empty = jnp.zeros(blocks.shape[1:], blocks.dtype)
        lanes = [blocks[homes.index(d)] if d in homes else empty for d in range(chain)]
        return lax.all_to_all(jnp.stack(lanes), "seg", 0, 0, tiled=True)

    def from_home(blocks):
        back = lax.all_to_all(blocks, "seg", 0, 0, tiled=True)
        return jnp.stack([back[d] for d in homes])

    def order(block):
        zero = jnp.zeros((block.shape[0], PAD - mem, width), block.dtype)
        return jnp.concatenate(
            [block[:, mem : mem + texts], block[:, :mem], zero, block[:, mem + texts :], zero], 1
        )

    def disorder(block):
        return jnp.concatenate(
            [
                block[:, texts : texts + mem],
                block[:, :texts],
                block[:, texts + PAD : texts + PAD + mem],
            ],
            1,
        )

    limit = unroll[jnp.clip((place - start) // stride, 0, micro - 1)]
    segments = jnp.arange(chain, dtype=jnp.int32)
    fresh = jnp.logical_or(segments == 0, segments == limit).astype(jnp.int32)
    memory_rows = jnp.pad(memory, ((0, PAD - mem), (0, 0)))

    (low, qkv, probs, context, unit1, hidden, active, slope, unit2, scale, out) = forward_chain(
        fresh, to_home(text[:, 0]), memory_rows, table, gathered
    )
    layer_out = from_home(disorder(out))
    (grad_qkv, grad_proj, grad_upper, grad_down, text_grad, narrow, wide, memory_grad) = (
        backward_chain(
            fresh, to_home(order(cotangent[:, 0])), table, qkv, probs, unit1, slope, unit2, scale,
            gathered,
        )
    )
    text_grad = from_home(text_grad).astype(F32)

    def flat(block, layer):
        return block[:, layer].reshape(-1, block.shape[-1])

    pieces = []
    for layer in range(2):
        for left, right in (
            (low, grad_qkv),
            (context, grad_proj),
            (hidden, grad_upper),
            (active, grad_down),
        ):
            full = dot(flat(left, layer), flat(right, layer), TN).astype(LOW)
            full = full.reshape(chain, full.shape[0] // chain, full.shape[1])
            for i in range(0, full.shape[2], width):
                pieces.append(full[:, :, i : i + width])
    matrices = lax.psum_scatter(
        jnp.concatenate(pieces, 1), "seg", scatter_dimension=0, tiled=True
    )[0]
    narrow = jnp.sum(narrow, 2)
    wide = jnp.sum(wide, 2)
    pieces = [memory_grad[:mem].reshape(mem, chain, part).swapaxes(0, 1).reshape(chain, -1)]
    for layer in range(2):
        gain2, shift2, down, gain1, shift1, out_bias, query, value = (
            narrow[layer, i] for i in range(8)
        )
        for v in (
            jnp.concatenate([query, value]), out_bias, gain1, shift1, wide[layer].reshape(-1), down,
            gain2, shift2,
        ):
            pieces.append(v.reshape(chain, -1))
    vectors = lax.psum_scatter(
        jnp.concatenate(pieces, 1).astype(LOW), "seg", scatter_dimension=0, tiled=True
    )[0]
    matrices, vectors = lax.psum((matrices, vectors), "item")
    matrices, vectors = matrices.astype(F32), vectors.astype(F32)

    results = []
    row, at = 0, mem * part
    for layer in range(2):
        shapes = [w.shape for w in layers[layer]]
        for shape in shapes:
            if len(shape) == 1:
                results.append(vectors[at : at + shape[0]])
                at += shape[0]
            else:
                blocks = []
                for _ in range(shape[1] // width):
                    blocks.append(matrices[row : row + shape[0]])
                    row += shape[0]
                results.append(jnp.concatenate(blocks, 1))
    return (
        layer_out[:, None],
        text_grad[:, None],
        vectors[: mem * part].reshape(mem, part),
        *results,
    )


def regroup(gathered, together, part):
    shards, total, width = gathered.shape
    blocks = gathered.reshape(shards // together, together, total // part, part, width)
    pieces = []
    for layer in range(2):
        base = layer * BLOCKS
        for block in range(8):
            pieces.append(blocks[:, :, base + block])
        pieces.append(blocks[:, :, base + 8 : base + 12])
    return jnp.concatenate(
        [p.reshape(shards // together, -1, width) for p in pieces], 1
    )


def solution(mesh):
    seg = (P("seg", None), P("seg"), P("seg", None)) + (P("seg"),) * 3
    seg = seg + (P("seg", None), P("seg"), P("seg", None)) + (P("seg"),) * 3
    rows = P("item", "seg", None, None)
    return jax.shard_map(
        body,
        mesh=mesh,
        in_specs=(rows, rows, P("item"), P()) + seg + seg,
        out_specs=(rows, rows, P(None, "seg")) + seg + seg,
        check_vma=False,
    )
```

time: 4610 us -> 1130 us (0.25)
  waiting for transfers between devices: 2790 us -> 417 us
  starting transfers between devices: 765 us -> 37.3 us
  Pallas kernels: 0 us -> 379 us
  other arithmetic: 343 us -> 7.38 us
  matrix products: 290 us -> 65.2 us
  local copies, waits for them, and re-layouts: 228 us -> 69.9 us
    ppermute x38 -> x0, waiting for transfers between devices: 1940 us -> none  [from_behind(): lax.ppermute(value, axis, [(source, source + steps) for source in range(f...]
    ppermute x38 -> x0, starting transfers between devices: 764 us -> none  [from_behind(): lax.ppermute(value, axis, [(source, source + steps) for source in range(f...]
    pallas_call x0 -> x2, Pallas kernels: none -> 379 us  [the longest x1 233 us: backward_chain(): pl.pallas_call(backward_kernel, grid=(segments,), in_specs=[SMEM, block((...]
    reduce_scatter x8 -> x1, waiting for transfers between devices: 508 us -> 271 us  [body(): lax.psum_scatter(jnp.concatenate(pieces, 1), 'seg', scatter_dimension=0,...]
    dot_general x128 -> x8, matrix products: 290 us -> 65.2 us  [dot(): return lax.dot_general(left, right, dims, preferred_element_type=F32)]
    all_gather x8 -> x1, waiting for transfers between devices: 320 us -> 119 us  [body(): gathered = lax.all_gather(jnp.concatenate(shards), 'seg')]
    convert_element_type x139 -> x2, other arithmetic: 111 us -> 2.11 us  [the longest x1 1.16 us: body(): fresh = jnp.logical_or(segments == 0, segments == limit).astype(jnp.int32)]
    reduce_sum x140 -> x2, other arithmetic: 100 us -> 0.17 us  [the longest x1 0.11 us: body(): narrow = jnp.sum(narrow, 2)]
  transfers between devices with their start and end apart: 56 -> 7, of which waited for: 53 -> 3; matrix products, arithmetic and copies ran while one was open for 2% -> 3% of each run, Pallas kernels for 0% -> 13%
where the time goes in v1:
time: 1130 us; the launch traced here: 1120 us
  waiting for transfers between devices  417 us (37%)
  Pallas kernels  379 us (34%)
  blocking collectives  132 us (12%)
  local copies, waits for them, and re-layouts  69.9 us (6%)
  matrix products  65.2 us (6%)
  starting transfers between devices  37.3 us (3%)
  between operations  15 us (1%)
    reduce_scatter x1, waiting for transfers between devices, body(): lax.psum_scatter(jnp.concatenate(pieces, 1), 'seg', scatter_dimension=0,...  271 us
    pallas_call x1, Pallas kernels, backward_chain(): pl.pallas_call(backward_kernel, grid=(segments,), in_specs=[SMEM, block((...  233 us
    pallas_call x1, Pallas kernels, forward_chain(): pl.pallas_call(forward_kernel, grid=(segments,), in_specs=[SMEM, block((t...  146 us
    all_gather x1, waiting for transfers between devices, body(): gathered = lax.all_gather(jnp.concatenate(shards), 'seg')  119 us
    all_gather x1, blocking collectives, body(): vectors = lax.all_gather(vectors, 'seg').astype(F32)  67.4 us
    dot_general x8, matrix products, dot(): return lax.dot_general(left, right, dims, preferred_element_type=F32)  65.2 us
    unnamed x1, blocking collectives  59.7 us
    unnamed x135, local copies, waits for them, and re-layouts  49.2 us
  transfers between devices with their start and end apart: 7, of which 3 were waited for; matrix products, arithmetic and copies ran while one was open for 3% of the time, Pallas kernels for 13%

profile of v1, /device:TPU:0, one launch (start us, length us, event | category | flops | bytes accessed | tf_op | source)
XLA Modules:
  0.0 1123.0 jit_solution(12642616713515463715)
XLA Ops:
  27.4 7.5 all-to-all-start
  35.2 67.4 %all-gather.2 = bf16[16,1,1152]{2,1,0:T(2,128)(2,1)S(1)} all-gather(bf16[1,1,1152]{2,1,0:T(2,128)(2,1)S(1)} %reshape.309), channel_id=2, replica_groups=mesh['seg'=16,'item'=2] {'seg'}, dimensions={0}, use_global_device_ids=true | all-gather | bytes 39168 | tf_op jit(solution)/shard_map/all_gather | solution.py:381
  111.2 4.6 all-to-all-start.2
  120.2 119.5 %all-gather.5.cloned.1.call-done = bf16[18432,768]{1,0:T(8,128)(2,1)} async-done(((bf16[1152,768]{1,0:T(8,128)(2,1)}), bf16[18432,768]{1,0:T(8,128)(2,1)}) %all-gather.5.cloned.1.call-update) | async-done | bytes 28311568 | tf_op jit(solution)/shard_map/all_gather | solution.py:386
  239.7 145.7 %forward_chain.1 = (bf16[16,2,96,768]{3,2,1,0:T(8,128)(2,1)}, bf16[16,2,96,2304]{3,2,1,0:T(8,128)(2,1)}, bf16[16,2,6,192,96]{4,3,2,1,0:T(8,128)(2,1)}, bf16[16,2...) custom-call(s32[16]{0:T(128)} %or_convert_fusion.fresh_ref, ...), custom_call_target="tpu_custom_call" | custom-call | flops 43486543872 | bytes 28311552 | tf_op jit(solution)/shard_map/forward_chain/pallas_call | solution.py:307
  385.4 233.2 %backward_chain.1 = (bf16[16,2,96,2304]{3,2,1,0:T(8,128)(2,1)}, bf16[16,2,96,768]{3,2,1,0:T(8,128)(2,1)}, bf16[16,2,96,3072]{3,2,1,0:T(8,128)(2,1)}, bf16[16,2,9...) custom-call(s32[16]{0:T(128)} %or_convert_fusion.fresh_ref, ...), custom_call_target="tpu_custom_call", output_to_operand_aliasing={{0}: (3, {}), {1}: (5, {}), {2}: (6, {}), {3}: (7, {})} | custom-call | flops 43486543872 | bytes 28311552 | tf_op jit(solution)/shard_map/backward_chain/pallas_call | solution.py:335
  618.7 9.5 bitcast_convert_fusion.5
  628.2 9.3 bitcast_convert_fusion.4
  637.6 2.1 bitcast_convert_fusion.7
  639.7 2.1 bitcast_convert_fusion.6
  641.8 10.4 bitcast_convert_fusion.3
  652.2 10.4 bitcast_convert_fusion.1
  662.6 10.3 bitcast_convert_fusion.2
  672.9 11.2 %bitcast_convert_fusion = bf16[3072,768]{1,0:T(8,128)(2,1)S(1)} fusion(bf16[16,2,96,3072]{3,2,1,0:T(8,128)(2,1)} %get-tuple-element.63, bf16[16,2,96,768]{3,2,1,0:T(8,128)(2,1)} %get-tuple-element.64), kind=kOutput, calls=%fused_computation | convolution fusion | flops 7250116608 | bytes 16515072 | tf_op jit(solution)/shard_map/dot_general | solution.py:22
  693.3 2.6 constant_dynamic-update-slice_fusion.32
  705.1 2.6 constant_dynamic-update-slice_fusion.30
  707.7 15.5 %all-to-all-start.3 = ((bf16[16,64,768]{2,1,0:T(8,128)(2,1)}), bf16[16,64,768]{2,1,0:T(8,128)(2,1)S(1)}, u32[]{:S(2)}, u32[]{:S(2)}) async-start(bf16[16,64,768]{2,1,0:T(8,128)(2,1)} %get-tuple-element.53), calls=%async_computation.3 | async-start | bytes 3145728 | tf_op jit(solution)/shard_map/all_to_all | solution.py:408
  726.4 2.3 pad_maximum_fusion
  728.7 26.5 %all-to-all-done.3 = bf16[16,64,768]{2,1,0:T(8,128)(2,1)S(1)} async-done(((bf16[16,64,768]{2,1,0:T(8,128)(2,1)}), bf16[16,64,768]{2,1,0:T(8,128)(2,1)S(1)}, u32[]{:S(2)}, u32[]{:S(2)}) %all-to-all-start.3) | async-done | bytes 1572896 | tf_op jit(solution)/shard_map/all_to_all | solution.py:408
  756.4 9.1 all-to-all-start.1
  767.3 271.3 %reduce-scatter.2.cloned.1.call-done = bf16[1,1152,768]{2,1,0:T(8,128)(2,1)} async-done(((bf16[16,1152,768]{2,1,0:T(8,128)(2,1)}), bf16[1,1152,768]{2,1,0:T(8,128)(2,1)}) %reduce-scatter.2.cloned.1.call-update) | async-done | bytes 1769488 | tf_op jit(solution)/shard_map/reduce_scatter | solution.py:459
  1039.8 59.7 %all-reduce.2 = bf16[16,1632]{1,0:T(8,128)(2,1)S(1)} all-reduce(bf16[16,1632]{1,0:T(8,128)(2,1)S(1)} %concatenate.74), channel_id=4, replica_groups=mesh['seg'=16,'item'=2] {'seg'}, use_global_device_ids=true, to_apply=%region_2.3.clone | all-reduce | flops 26112 | bytes 104448
  1100.1 4.9 psum.14
  1110.7 2.3 fusion.63
  (224 shorter events, 68.2 us)
Async XLA Ops:
  7.2 232.5 %all-gather.5.cloned.1.call-start = ((), (), s32[]{:S(2)}) async-start(), calls=%async_computation.7 | async-start | bytes 30081024 | tf_op jit(solution)/shard_map/all_gather | solution.py:386
  21.3 13.7 %copy-start.14 = (bf16[48]{0:T(256)(128)(2,1)S(1)}, bf16[48]{0:T(256)(128)(2,1)}, u32[]{:S(2)}) copy-start(bf16[48]{0:T(256)(128)(2,1)} %param.36) | copy-start | bytes 292
  21.3 13.7 %copy-start.15 = (bf16[48]{0:T(256)(128)(2,1)S(1)}, bf16[48]{0:T(256)(128)(2,1)}, u32[]{:S(2)}) copy-start(bf16[48]{0:T(256)(128)(2,1)} %param.37) | copy-start | bytes 292
  21.3 13.7 %copy-start.16 = (bf16[192]{0:T(256)(128)(2,1)S(1)}, bf16[192]{0:T(256)(128)(2,1)}, u32[]{:S(2)}) copy-start(bf16[192]{0:T(256)(128)(2,1)} %param.39) | copy-start | bytes 1156
  21.3 13.7 %copy-start.17 = (bf16[48]{0:T(256)(128)(2,1)S(1)}, bf16[48]{0:T(256)(128)(2,1)}, u32[]{:S(2)}) copy-start(bf16[48]{0:T(256)(128)(2,1)} %param.41) | copy-start | bytes 292
  21.3 13.7 %copy-start.18 = (bf16[48]{0:T(256)(128)(2,1)S(1)}, bf16[48]{0:T(256)(128)(2,1)}, u32[]{:S(2)}) copy-start(bf16[48]{0:T(256)(128)(2,1)} %param.42) | copy-start | bytes 292
  21.3 13.7 %copy-start.19 = (bf16[48]{0:T(256)(128)(2,1)S(1)}, bf16[48]{0:T(256)(128)(2,1)}, u32[]{:S(2)}) copy-start(bf16[48]{0:T(256)(128)(2,1)} %param.43) | copy-start | bytes 292
  21.3 13.7 %copy-start.20 = (bf16[96]{0:T(256)(128)(2,1)S(1)}, bf16[96]{0:T(256)(128)(2,1)}, u32[]{:S(2)}) copy-start(bf16[96]{0:T(256)(128)(2,1)} %param.45) | copy-start | bytes 580
  21.3 13.7 %copy-start.21 = (bf16[48]{0:T(256)(128)(2,1)S(1)}, bf16[48]{0:T(256)(128)(2,1)}, u32[]{:S(2)}) copy-start(bf16[48]{0:T(256)(128)(2,1)} %param.47) | copy-start | bytes 292
  24.0 79.1 %copy-start.4 = (bf16[4,1,84,768]{3,0,2,1:T(4,128)(2,1)S(1)}, bf16[4,1,84,768]{3,0,2,1:T(4,128)(2,1)}, u32[]{:S(2)}) copy-start(bf16[4,1,84,768]{3,0,2,1:T(4,128)(2,1)} %param.29) | copy-start | bytes 1548292
  27.4 75.9 %copy-start.10 = (bf16[10,768]{1,0:T(8,128)(2,1)S(1)}, bf16[10,768]{1,0:T(8,128)(2,1)}, u32[]{:S(2)}) copy-start(bf16[10,768]{1,0:T(8,128)(2,1)} %param.31) | copy-start | bytes 46084
  27.4 83.8 %all-to-all-start = ((bf16[16,64,768]{2,1,0:T(8,128)(2,1)}), bf16[16,64,768]{2,1,0:T(8,128)(2,1)S(1)}, u32[]{:S(2)}, u32[]{:S(2)}) async-start(bf16[16,64,768]{2,1,0:T(8,128)(2,1)} %broadcast_dynamic-update-slice_fusion.3), calls=%async_computation | async-start | bytes 3145728 | tf_op jit(solution)/shard_map/all_to_all | solution.py:405
  111.2 274.2 %all-to-all-start.2 = ((bf16[16,96,768]{2,1,0:T(8,128)(2,1)}), bf16[16,96,768]{2,1,0:T(8,128)(2,1)}, u32[]{:S(2)}, u32[]{:S(2)}) async-start(bf16[16,96,768]{2,1,0:T(8,128)(2,1)} %broadcast_dynamic-update-slice_fusion.1), calls=%async_computation.2 | async-start | bytes 4718592 | tf_op jit(solution)/shard_map/all_to_all | solution.py:405
  115.8 922.8 %reduce-scatter.2.cloned.1.call-start = ((), (), s32[]{:S(2)}) async-start(), calls=%async_computation.5 | async-start | bytes 30081024 | tf_op jit(solution)/shard_map/reduce_scatter | solution.py:459
  618.7 18.8 %slice-start = ((s8[4718592]{0:T(1024)(128)(4,1)}), s8[4194304]{0:T(1024)(128)(4,1)S(1)}, s32[]{:S(2)}) async-start(s8[4718592]{0:T(1024)(128)(4,1)} %bitcast.154), calls=%async_computation.8 | async-start | bytes 8388608
  618.7 18.8 %slice-start.2 = ((s8[4718592]{0:T(1024)(128)(4,1)}), s8[4194304]{0:T(1024)(128)(4,1)S(1)}, s32[]{:S(2)}) async-start(s8[4718592]{0:T(1024)(128)(4,1)} %bitcast.156), calls=%async_computation.10 | async-start | bytes 8388608
  641.8 20.8 %slice-start.6 = ((s8[4718592]{0:T(1024)(128)(4,1)}), s8[4194304]{0:T(1024)(128)(4,1)S(1)}, s32[]{:S(2)}) async-start(s8[4718592]{0:T(1024)(128)(4,1)} %bitcast.160), calls=%async_computation.14 | async-start | bytes 8388608
  707.7 47.5 %all-to-all-start.3 = ((bf16[16,64,768]{2,1,0:T(8,128)(2,1)}), bf16[16,64,768]{2,1,0:T(8,128)(2,1)S(1)}, u32[]{:S(2)}, u32[]{:S(2)}) async-start(bf16[16,64,768]{2,1,0:T(8,128)(2,1)} %get-tuple-element.53), calls=%async_computation.3 | async-start | bytes 3145728 | tf_op jit(solution)/shard_map/all_to_all | solution.py:408
  728.7 36.8 %copy-start.29 = (u32[32]{0:T(128)S(1)}, u32[32]{0:T(128)}, u32[]{:S(2)}) copy-start(u32[32]{0:T(128)} %constant.46) | copy-start | bytes 388
  728.7 37.4 %copy-start.11 = (f32[16,768]{1,0:T(8,128)S(1)}, f32[16,768]{1,0:T(8,128)}, u32[]{:S(2)}) copy-start(f32[16,768]{1,0:T(8,128)} %get-tuple-element.54) | copy-start | bytes 147460
  728.7 37.7 %copy-start.6 = (f32[2,8,8,768]{3,2,1,0:T(8,128)S(1)}, f32[2,8,8,768]{3,2,1,0:T(8,128)}, u32[]{:S(2)}) copy-start(f32[2,8,8,768]{3,2,1,0:T(8,128)} %get-tuple-element.55) | copy-start | bytes 1179652
  728.7 38.5 %copy-start.9 = (f32[2,4,8,768]{3,2,1,0:T(8,128)S(1)}, f32[2,4,8,768]{3,2,1,0:T(8,128)}, u32[]{:S(2)}) copy-start(f32[2,4,8,768]{3,2,1,0:T(8,128)} %get-tuple-element.56) | copy-start | bytes 589828
  756.4 353.3 %all-to-all-start.1 = ((bf16[16,84,768]{2,1,0:T(8,128)(2,1)}), bf16[16,84,768]{2,1,0:T(8,128)(2,1)S(1)}, u32[]{:S(2)}, u32[]{:S(2)}) async-start(bf16[16,84,768]{2,1,0:T(8,128)(2,1)} %pad_maximum_fusion), calls=%async_computation.1 | async-start | bytes 4325376 | tf_op jit(solution)/shard_map/all_to_all | solution.py:408
  765.5 345.3 %all-reduce.5.cloned.1.call-start = ((), (), s32[]{:S(2)}) async-start(), calls=%async_computation.6 | async-start | bytes 3538944 | tf_op jit(solution)/shard_map/psum | solution.py:477
  (22 other events, 202.0 us)
Sparse Core Ops, SparseCore 0:
  20.6 219.0 all-gather.4
  707.8 330.7 reduce-scatter.1
  1040.9 54.8 all-reduce.4

commit v2 on v1

v2 whole, which is shorter than its diff:
```python
import jax
import jax.numpy as jnp
from jax import lax
from jax.experimental import pallas as pl
from jax.experimental.pallas import tpu as pltpu
from jax.sharding import PartitionSpec as P

HEAD_DIM = 64
EPSILON = 1e-05
F32 = jnp.float32
LOW = jnp.bfloat16
NN = (((1,), (0,)), ((), ()))
NT = (((1,), (1,)), ((), ()))
TN = (((0,), (0,)), ((), ()))

PAD = 16
BLOCKS = 12
B_QUERY, B_VALUE, B_OUT, GAIN1, SHIFT1, B_UP, B_DOWN, GAIN2, SHIFT2 = 0, 1, 2, 3, 4, 5, 9, 10, 11


def dot(left, right, dims=NN):
    return lax.dot_general(left, right, dims, preferred_element_type=F32)


def norm_rows(total, gain, shift):
    centre = total - jnp.mean(total, -1, keepdims=True)
    scale = lax.rsqrt(jnp.mean(centre * centre, -1, keepdims=True) + EPSILON)
    unit = centre * scale
    return unit, scale, unit * gain + shift


def norm_back(grad, unit, scale, gain):
    t = grad * gain
    return scale * (
        t - jnp.mean(t, -1, keepdims=True) - unit * jnp.mean(t * unit, -1, keepdims=True)
    )


def gelu_and_slope(upper):
    density = jnp.exp(upper * upper * -0.5) * 0.3989422804014327
    below = 0.5 * (1.0 + lax.erf(upper * 0.7071067811865476))
    return upper * below, below + upper * density


def fold(block):
    rows, width = block.shape
    return jnp.sum(block.reshape(rows // 8, 8, width), 0)


def two_heads(block, first):
    zero = jnp.zeros_like(block)
    return jnp.concatenate([jnp.where(first, block, zero), jnp.where(first, zero, block)], 0)


def copy_block(gathered, target, layer, block, part, sem):
    shards = gathered.shape[0]
    base = layer * BLOCKS * part

    def copy(shard, row, to, count):
        pltpu.make_async_copy(
            gathered.at[shard, pl.ds(pl.multiple_of(row, 16), count)],
            target(pl.multiple_of(to, 16), count),
            sem,
        ).start()

    @pl.when(block < 8)
    def _():
        def start(shard, none):
            copy(shard, base + block * part, shard * part, part)
            return none

        lax.fori_loop(0, shards, start, 0)

    @pl.when(block >= 8)
    def _():
        def start(i, none):
            shard = (block - 8) * (shards // 4) + i
            copy(shard, base + 8 * part, i * 4 * part, 4 * part)
            return none

        lax.fori_loop(0, shards // 4, start, 0)


def load_weights(gathered, held, width, sem):
    part = width // gathered.shape[0]

    def start(index, none):
        def target(row, count):
            return held.at[pl.ds(pl.multiple_of(index * width + row, 16), count)]

        copy_block(gathered, target, index // BLOCKS, index % BLOCKS, part, sem)
        return none

    lax.fori_loop(0, 2 * BLOCKS, start, 0)
    pltpu.make_async_copy(held, held, sem).wait()


def load_turned(gathered, held, stage, width, sems):
    part = width // gathered.shape[0]

    def start(index):
        slot = index % 2

        def target(row, count):
            return stage.at[slot, pl.ds(row, count)]

        copy_block(gathered, target, index // BLOCKS, index % BLOCKS, part, sems.at[slot])

    start(0)

    def turn(index, none):
        slot = index % 2

        @pl.when(index + 1 < 2 * BLOCKS)
        def _():
            start(index + 1)

        pltpu.make_async_copy(stage.at[slot], stage.at[slot], sems.at[slot]).wait()
        held[pl.ds(pl.multiple_of(index * width, width), width), :] = stage[slot].T
        return none

    lax.fori_loop(0, 2 * BLOCKS, turn, 0)


def split_refs(refs, sizes):
    parts = []
    for size in sizes:
        parts.append(refs[:size])
        refs = refs[size:]
    return parts


def forward_kernel(*refs):
    (
        (fresh_ref, text_ref, memory_ref, vector_ref, gathered_ref),
        low_ref, qkv_ref, probs_ref, context_ref, unit1_ref, hidden_ref, active_ref, slope_ref,
        unit2_ref,
        (scale_ref, out_ref, held, carry, sem),
    ) = split_refs(refs, [5] + [2] * 9 + [5])
    step = pl.program_id(0)
    texts, width = text_ref.shape[1:]
    rows = texts + 2 * PAD
    mem = 10

    @pl.when(step == 0)
    def _():
        load_weights(gathered_ref, held, width, sem)
        carry[...] = jnp.zeros_like(carry)

    column = lax.broadcasted_iota(jnp.int32, (2 * rows, rows), 1)
    unused = jnp.logical_or(
        column >= texts + PAD + mem,
        jnp.logical_and(column >= texts + mem, column < texts + PAD),
    )
    mask = jnp.where(unused, -1e30, 0.0).astype(F32)
    first_head = lax.broadcasted_iota(jnp.int32, (rows, 2 * HEAD_DIM), 1) < HEAD_DIM

    memory = memory_ref[...]
    read = jnp.where(fresh_ref[step] > 0, memory, carry[...])
    x = jnp.concatenate([text_ref[0], read, memory], 0).astype(F32)
    scales = []
    for index in range(2):

        def weight(block, index=index):
            return held[(index * BLOCKS + block) * width : (index * BLOCKS + block + 1) * width, :]

        def vector(row, index=index):
            return vector_ref[index, row : row + 1, :]

        low = x.astype(LOW)
        low_ref[index][0] = low
        query = (dot(low, weight(0)) + vector(B_QUERY)).astype(LOW)
        keys = dot(low, weight(1)).astype(LOW)
        values = (dot(low, weight(2)) + vector(B_VALUE)).astype(LOW)
        qkv_ref[index][0, :, :width] = query
        qkv_ref[index][0, :, width : 2 * width] = keys
        qkv_ref[index][0, :, 2 * width :] = values
        for pair in range(width // (2 * HEAD_DIM)):
            cols = slice(2 * HEAD_DIM * pair, 2 * HEAD_DIM * (pair + 1))
            scores = dot(two_heads(query[:, cols], first_head), keys[:, cols], NT)
            scores = scores * HEAD_DIM ** (-0.5) + mask
            weights = jnp.exp(scores - jnp.max(scores, -1, keepdims=True))
            probs = (weights / jnp.sum(weights, -1, keepdims=True)).astype(LOW)
            probs_ref[index][0, pair] = probs
            both = dot(probs, values[:, cols])
            context_ref[index][0, :, cols] = jnp.where(
                first_head, both[:rows], both[rows:]
            ).astype(LOW)
        total = x + dot(context_ref[index][0], weight(3)) + vector(B_OUT)
        unit, scale, hidden = norm_rows(total, vector(GAIN1), vector(SHIFT1))
        unit1_ref[index][0] = unit.astype(LOW)
        scales.append(scale)
        hidden_low = hidden.astype(LOW)
        hidden_ref[index][0] = hidden_low
        total = hidden + vector(B_DOWN)
        for block in range(4):
            cols = slice(block * width, (block + 1) * width)
            upper = dot(hidden_low, weight(4 + block)) + vector(B_UP + block)
            active, slope = gelu_and_slope(upper)
            active = active.astype(LOW)
            active_ref[index][0, :, cols] = active
            slope_ref[index][0, :, cols] = slope.astype(LOW)
            total = total + dot(active, weight(8 + block))
        unit, scale, x = norm_rows(total, vector(GAIN2), vector(SHIFT2))
        unit2_ref[index][0] = unit.astype(LOW)
        scales.append(scale)
    lane = lax.broadcasted_iota(jnp.int32, (rows, 128), 1)
    packed = scales[3]
    for i in (2, 1, 0):
        packed = jnp.where(lane < 32 * (i + 1), scales[i], packed)
    scale_ref[0] = packed
    final = x.astype(LOW)
    out_ref[0] = final
    carry[...] = final[texts + PAD :]


def backward_kernel(*refs):
    (
        (fresh_ref, cotangent_ref, vector_ref, scale_ref, gathered_ref),
        qkv_ref, probs_ref, unit1_ref, slope_ref, unit2_ref,
        grad_qkv_ref, grad_proj_ref, grad_upper_ref, grad_down_ref,
        (text_ref, narrow_ref, wide_ref, memory_ref, held, carry, stage, sems),
    ) = split_refs(refs, [5] + [2] * 5 + [2] * 4 + [8])
    turn = pl.program_id(0)
    step = pl.num_programs(0) - 1 - turn
    rows, width = cotangent_ref.shape[1:]
    texts = rows - 2 * PAD

    @pl.when(turn == 0)
    def _():
        load_turned(gathered_ref, held, stage, width, sems)
        carry[...] = jnp.zeros_like(carry)
        narrow_ref[...] = jnp.zeros_like(narrow_ref)
        wide_ref[...] = jnp.zeros_like(wide_ref)
        memory_ref[...] = jnp.zeros_like(memory_ref)

    first_head = lax.broadcasted_iota(jnp.int32, (rows, 2 * HEAD_DIM), 1) < HEAD_DIM
    grad = jnp.concatenate(
        [
            cotangent_ref[0, : texts + PAD].astype(F32),
            cotangent_ref[0, texts + PAD :].astype(F32) + carry[...].astype(F32),
        ],
        0,
    )
    for index in (1, 0):

        def weight(block, index=index):
            return held[(index * BLOCKS + block) * width : (index * BLOCKS + block + 1) * width, :]

        def vector(row, index=index):
            return vector_ref[index, row : row + 1, :]

        def scale(norm, index=index):
            lane = 32 * (2 * index + norm)
            return scale_ref[0, :, lane : lane + 1]

        unit = unit2_ref[index][0].astype(F32)
        narrow_ref[index, 0] += fold(grad * unit)
        narrow_ref[index, 1] += fold(grad)
        grad_second = norm_back(grad, unit, scale(1), vector(GAIN2))
        narrow_ref[index, 2] += fold(grad_second)
        grad_down = grad_second.astype(LOW)
        grad_hidden = grad_second
        for block in range(4):
            cols = slice(block * width, (block + 1) * width)
            grad_upper = dot(grad_down, weight(8 + block)) * slope_ref[index][0, :, cols].astype(F32)
            wide_ref[index, block] += fold(grad_upper)
            grad_upper = grad_upper.astype(LOW)
            grad_upper_ref[index][0, :, cols] = grad_upper
            grad_hidden = grad_hidden + dot(grad_upper, weight(4 + block))
        grad_down_ref[index][0] = grad_down
        unit = unit1_ref[index][0].astype(F32)
        narrow_ref[index, 3] += fold(grad_hidden * unit)
        narrow_ref[index, 4] += fold(grad_hidden)
        grad_first = norm_back(grad_hidden, unit, scale(0), vector(GAIN1))
        narrow_ref[index, 5] += fold(grad_first)
        grad_proj = grad_first.astype(LOW)
        grad_proj_ref[index][0] = grad_proj
        grad_context = dot(grad_proj, weight(3)).astype(LOW)
        for pair in range(width // (2 * HEAD_DIM)):
            cols = slice(2 * HEAD_DIM * pair, 2 * HEAD_DIM * (pair + 1))
            in_keys = slice(width + cols.start, width + cols.stop)
            in_values = slice(2 * width + cols.start, 2 * width + cols.stop)
            query = two_heads(qkv_ref[index][0, :, cols], first_head)
            keys = qkv_ref[index][0, :, in_keys]
            values = qkv_ref[index][0, :, in_values]
            context = two_heads(grad_context[:, cols], first_head)
            probs_low = probs_ref[index][0, pair]
            probs = probs_low.astype(F32)
            term = dot(context, values, NT) * probs
            grad_scores = term - probs * jnp.sum(term, -1, keepdims=True)
            grad_scores = (grad_scores * HEAD_DIM ** (-0.5)).astype(LOW)
            both = dot(grad_scores, keys)
            grad_query = jnp.where(first_head, both[:rows], both[rows:])
            grad_keys = dot(grad_scores, query, TN)
            grad_values = dot(probs_low, context, TN)
            narrow_ref[index, 6, :, cols] += fold(grad_query)
            narrow_ref[index, 7, :, cols] += fold(grad_values)
            grad_qkv_ref[index][0, :, cols] = grad_query.astype(LOW)
            grad_qkv_ref[index][0, :, in_keys] = grad_keys.astype(LOW)
            grad_qkv_ref[index][0, :, in_values] = grad_values.astype(LOW)
        grad = grad_first
        for block in range(3):
            cols = slice(block * width, (block + 1) * width)
            grad = grad + dot(grad_qkv_ref[index][0, :, cols], weight(block))
    text_ref[0] = grad[:texts].astype(LOW)
    read = grad[texts : texts + PAD]
    fresh = fresh_ref[step] > 0
    memory_ref[...] += grad[texts + PAD :] + jnp.where(fresh, read, 0.0)
    carry[...] = jnp.where(fresh, 0.0, read).astype(LOW)


SMEM = pl.BlockSpec(memory_space=pltpu.SMEM)
VMEM = pl.BlockSpec(memory_space=pltpu.VMEM)
ANY = pl.BlockSpec(memory_space=pl.ANY)


def cost(rows, width, segments):
    return pl.CostEstimate(
        flops=2 * rows * 2 * BLOCKS * width * width * segments * 4,
        bytes_accessed=2 * 2 * BLOCKS * width * width,
        transcendentals=0,
    )


def forward_chain(fresh, text, memory, vectors, gathered):
    segments, texts, width = text.shape
    rows = texts + 2 * PAD
    pairs = width // (2 * HEAD_DIM)

    def block(shape):
        return pl.BlockSpec((1,) + shape, lambda s: (s,) + (0,) * len(shape))

    row = (rows, width)
    shapes = [row, (rows, 3 * width), (pairs, 2 * rows, rows), row, row, row]
    shapes += [(rows, 4 * width), (rows, 4 * width), row]
    outs = [(shape, LOW) for shape in shapes for _ in range(2)]
    outs += [((rows, 128), F32), (row, LOW)]
    found = pl.pallas_call(
        forward_kernel,
        grid=(segments,),
        in_specs=[SMEM, block((texts, width)), VMEM, VMEM, ANY],
        out_specs=[block(shape) for shape, _ in outs],
        out_shape=[jax.ShapeDtypeStruct((segments,) + shape, kind) for shape, kind in outs],
        scratch_shapes=[
            pltpu.VMEM((2 * BLOCKS * width, width), LOW),
            pltpu.VMEM((PAD, width), LOW),
            pltpu.SemaphoreType.DMA,
        ],
        compiler_params=pltpu.CompilerParams(vmem_limit_bytes=62 << 20),
        cost_estimate=cost(rows, width, segments),
        name="forward_chain",
    )(fresh, text, memory, vectors, gathered)
    return split_refs(found, [2] * 9 + [1, 1])


def backward_chain(fresh, cotangent, vectors, scale, saved, gathered):
    segments, rows, width = cotangent.shape
    texts = rows - 2 * PAD
    pairs = width // (2 * HEAD_DIM)

    def block(shape):
        return pl.BlockSpec((1,) + shape, lambda t: (segments - 1 - t,) + (0,) * len(shape))

    row, three, four = (rows, width), (rows, 3 * width), (rows, 4 * width)
    outs = [shape for shape in (three, row, four, row) for _ in range(2)] + [(texts, width)]
    ins = [shape for shape in (three, (pairs, 2 * rows, rows), row, four, row) for _ in range(2)]
    found = pl.pallas_call(
        backward_kernel,
        grid=(segments,),
        in_specs=[SMEM, block(row), VMEM, block((rows, 128)), ANY]
        + [block(shape) for shape in ins],
        out_specs=[block(shape) for shape in outs] + [VMEM, VMEM, VMEM],
        out_shape=[jax.ShapeDtypeStruct((segments,) + shape, LOW) for shape in outs]
        + [
            jax.ShapeDtypeStruct((2, 8, 8, width), F32),
            jax.ShapeDtypeStruct((2, 4, 8, width), F32),
            jax.ShapeDtypeStruct((PAD, width), F32),
        ],
        scratch_shapes=[
            pltpu.VMEM((2 * BLOCKS * width, width), LOW),
            pltpu.VMEM((PAD, width), LOW),
            pltpu.VMEM((2, width, width), LOW),
            pltpu.SemaphoreType.DMA((2,)),
        ],
        input_output_aliases={5: 0, 6: 1, 9: 2, 10: 3, 11: 4, 12: 5, 13: 6, 14: 7},
        compiler_params=pltpu.CompilerParams(vmem_limit_bytes=62 << 20),
        cost_estimate=cost(rows, width, segments),
        name="backward_chain",
    )(fresh, cotangent, vectors, scale, gathered, *(a for pair in saved for a in pair))
    return split_refs(found, [2] * 4 + [1] * 4)


def split_columns(shard, width):
    rows, columns = shard.shape
    return [shard[:, i : i + width] for i in range(0, columns, width)]


class Slice:
    def __init__(self, micro):
        self.micro, self.half = micro, micro // 2
        self.bits = self.half.bit_length() - 1
        self.chain, self.items = lax.axis_size("seg"), lax.axis_size("item")
        self.start = (self.chain - 2 * micro) // 2
        self.place, self.item = lax.axis_index("seg"), lax.axis_index("item")
        self.core = self.place % 2
        self.home = jnp.clip((self.place - self.start) // 2, 0, micro - 1)
        self.high, self.low = self.home // self.half, self.home % self.half
        self.at_home = jnp.logical_and(
            self.place >= self.start, self.place < self.start + 2 * micro
        )

    def seat(self, home, core=0):
        return self.start + 2 * home + core

    def far(self, home, core=0):
        return self.seat(home, core) + self.micro * (-1 if home < self.half else 1)

    def send(self, value, pairs):
        flat = [(a * self.items + x, b * self.items + x) for a, b in pairs for x in range(self.items)]
        return lax.ppermute(value, ("seg", "item"), flat)

    def send_across(self, value, bit):
        flat = []
        for i in range(self.micro):
            for c in range(2):
                at = self.seat(i, c) * self.items
                flat += [(at + x, at + (x ^ (1 << bit))) for x in range(self.items)]
        return lax.ppermute(value, ("seg", "item"), flat)

    def between_homes(self, flip):
        return [(self.seat(i, c), self.seat(i ^ flip, c)) for i in range(self.micro) for c in range(2)]

    def in_order(self, mine, got, side, axis):
        return jnp.where(
            side == 0, jnp.stack([mine, got], axis), jnp.stack([got, mine], axis)
        )

    def joined(self, mine, got, side, axis):
        return jnp.where(
            side == 0, jnp.concatenate([mine, got], axis), jnp.concatenate([got, mine], axis)
        )

    def gather(self, value, items=False):
        homes = [(i, c) for i in range(self.micro) for c in range(2)]
        got = self.send(value, [(self.far(i, c), self.seat(i, c)) for i, c in homes])
        whole = self.in_order(value, got, 1 - self.high, 0)
        if items:
            whole = whole.reshape((2,) + (2,) * (1 + self.bits) + value.shape[1:])
        whole = whole.reshape((1,) * (1 + self.bits) + whole.shape)
        for bit in range(self.bits + 1):
            axis = self.bits - bit
            side = (self.home >> bit) % 2
            out = whole
            if items:
                at = 2 + self.bits + axis
                out = lax.dynamic_index_in_dim(whole, 1 - side, at, keepdims=True)
                whole = lax.dynamic_index_in_dim(whole, side, at, keepdims=True)
            whole = self.joined(whole, self.send(out, self.between_homes(1 << bit)), side, axis)
        rest = value.shape[1:] if items else value.shape
        whole = whole.reshape((2, self.half, 2) + rest).swapaxes(1, 2)
        got = self.send(whole, [(self.seat(i, c), self.seat(i, 1 - c)) for i, c in homes])
        return self.in_order(whole, got, self.core, 3).reshape((self.chain,) + rest)

    def spread(self, value, waits):
        rest = value.shape[1:]
        whole = value.reshape((2, 2, self.half, 2) + rest)
        whole = lax.dynamic_index_in_dim(whole, self.core, 3, keepdims=False).swapaxes(1, 2)
        whole = whole.reshape((2,) * (1 + self.bits) + (1,) * (1 + self.bits) + (2,) + rest)
        for bit in reversed(range(self.bits + 1)):
            axis = self.bits - bit
            side = (self.home >> bit) % 2
            wait = waits[min(axis, len(waits) - 1)]
            got = self.send(
                lax.dynamic_index_in_dim(whole, 1 - side + wait, axis, keepdims=True),
                self.between_homes(1 << bit),
            )
            whole = lax.dynamic_index_in_dim(whole, side, axis, keepdims=True)
            wait = waits[min(axis + 1, len(waits) - 1)]
            whole = self.joined(whole, got, side + wait, 1 + self.bits + axis)
        whole = whole.reshape((self.micro, 2) + rest)
        near = lax.dynamic_index_in_dim(whole, 1 - self.high, 1, keepdims=False)
        away = lax.dynamic_index_in_dim(whole, self.high + waits[-1], 1, keepdims=False)
        homes = [(i, c) for i in range(self.micro) for c in range(2)]
        got = self.send(away, [(self.seat(i, c), self.far(i, c)) for i, c in homes])
        return jnp.where(self.at_home, near, got)

    def halvings(self, order):
        stages = []
        for name in order:
            if name == "x":
                stages += [("x", b) for b in range(self.items.bit_length() - 1)]
            elif name == "h":
                stages.append(("h", self.bits))
            else:
                stages += [("l", b) for b in range(self.bits)]
        return stages

    def halve(self, terms, stage, wait):
        name, bit = stage
        side = ((self.item if name == "x" else self.home) >> bit) % 2
        axis = {"x": -1, "h": 0, "l": 1 + self.bits - bit}[name]

        def cut(term, side):
            found = []
            for f in term:
                size = f.shape[axis] // 2
                found.append(lax.dynamic_slice_in_dim(f, side * size, size, axis))
            return found[0] if len(found) == 1 else jnp.concatenate(found, -1)

        out = add([cut(t, 1 - side + wait) for t in terms])
        if name == "x":
            got = self.send_across(out, bit)
        else:
            got = self.send(out, self.between_homes(1 << bit))
        return out, [[cut(t, side)] for t in terms] + [[got]]

    def deliver(self, total):
        near = lax.dynamic_index_in_dim(total, 1 - self.high, 0, keepdims=False)
        away = lax.dynamic_index_in_dim(total, self.high, 0, keepdims=False)

        def of(pair, core):
            return lax.dynamic_index_in_dim(pair, core, 0, keepdims=False)

        homes = [(i, c) for i in range(self.micro) for c in range(2)]
        beside = self.send(
            of(near, 1 - self.core), [(self.seat(i, c), self.seat(i, 1 - c)) for i, c in homes]
        )
        straight = self.send(
            of(away, self.core), [(self.seat(i, c), self.far(i, c)) for i, c in homes]
        )
        crossed = self.send(
            of(away, 1 - self.core), [(self.seat(i, c), self.far(i, 1 - c)) for i, c in homes]
        )
        same = jnp.where(self.at_home, of(near, self.core), straight)
        both = self.in_order(same, beside + crossed, self.core, 0)
        if self.items == 2:
            swapped = lax.ppermute(both, "item", [(0, 1), (1, 0)])
            return [
                jnp.where(self.item == 0, both, swapped),
                jnp.where(self.item == 0, swapped, both),
            ]
        every = lax.all_gather(both, "item")
        width = self.items.bit_length() - 1
        return [every[int(format(x, "0%db" % width)[::-1], 2)] for x in range(self.items)]

    def reduce(self, chunks, text, out):
        kind = (2, 2) + (2,) * self.bits + (2,)
        terms = [[[f.reshape(kind + f.shape[1:]) for f in fulls]] for fulls, _ in chunks]
        stages = [self.halvings(order) for _, order in chunks]
        wait, waits = 0, []
        for turn in range(len(stages[0])):
            outs = []
            for i in range(len(chunks)):
                sent, terms[i] = self.halve(terms[i], stages[i][turn], wait)
                outs.append(sent)
            wait = after(outs[-1])
            waits.append(wait)
        text = self.spread(text, waits).astype(F32)
        out = self.spread(out, [0] + waits[1:])
        rows = min(f.shape[1] for fulls, _ in chunks for f in fulls)
        totals = []
        for t in terms:
            total = add([f[0] for f in t])
            total = total.reshape((2, 2) + total.shape[-2:])
            strips = [total[:, :, i : i + rows] for i in range(0, total.shape[2], rows)]
            totals.append(strips[0] if len(strips) == 1 else jnp.concatenate(strips, -1))
        found = []
        for group in ((0, 1), (2,)):
            sides = self.deliver(jnp.concatenate([totals[i] for i in group], -1))
            at = 0
            for i in group:
                for f in chunks[i][0]:
                    size = f.shape[2] // self.items
                    strips = []
                    for _ in range(f.shape[1] // rows):
                        strips.append(
                            jnp.concatenate([side[..., at : at + size] for side in sides], -1)
                        )
                        at += size
                    found.append(jnp.concatenate(strips, 1).astype(F32))
        return found, text, out


def after(*values):
    zero = jnp.int32(0)
    for v in values:
        one = v[(0,) * v.ndim]
        zero = zero + (one != one).astype(jnp.int32)
    return zero


def add(terms):
    total = terms[0].astype(F32)
    for t in terms[1:]:
        total = total + t.astype(F32)
    return total.astype(LOW)


def body(text, cotangent, unroll, memory, *weights):
    micro, _, texts, width = text.shape
    mem = memory.shape[0]
    chain = lax.axis_size("seg")
    part = width // chain
    layers = (weights[:12], weights[12:])
    net = Slice(micro)

    def order(block):
        zero = jnp.zeros((block.shape[0], PAD - mem, width), block.dtype)
        return jnp.concatenate(
            [block[:, mem : mem + texts], block[:, :mem], zero, block[:, mem + texts :], zero], 1
        )

    def disorder(block):
        return jnp.concatenate(
            [
                block[:, texts : texts + mem],
                block[:, :texts],
                block[:, texts + PAD : texts + PAD + mem],
            ],
            1,
        )

    shards = []
    for w in layers:
        for matrix in (w[0], w[2], w[6], w[8]):
            shards += split_columns(matrix, width)
    gathered = lax.all_gather(jnp.concatenate(shards), "seg")
    if part % 16:
        gathered = regroup(gathered, 16 // (part & -part), part)
    text_home = net.gather(text[:, 0], items=True)
    cotangent_home = order(net.gather(cotangent[:, 0], items=True))
    vectors = jnp.concatenate([v for w in layers for v in w if v.ndim == 1])
    vectors = net.gather(vectors.reshape(-1, 2 * BLOCKS * part // 8)).reshape(chain, -1)
    vectors = vectors.astype(F32)
    rows_of = []
    at = 0
    for w in layers:
        for v in w:
            if v.ndim == 1:
                rows_of.append(vectors[:, at : at + v.shape[0]].reshape(-1, width))
                at += v.shape[0]
    half = len(rows_of) // 2
    table = jnp.stack([jnp.concatenate(rows_of[:half]), jnp.concatenate(rows_of[half:])])
    table = jnp.pad(table, ((0, 0), (0, 16 - table.shape[1]), (0, 0)))

    limit = unroll[net.home]
    segments = jnp.arange(chain, dtype=jnp.int32)
    fresh = jnp.logical_or(segments == 0, segments == limit).astype(jnp.int32)
    memory_rows = jnp.pad(memory, ((0, PAD - mem), (0, 0)))

    (low, qkv, probs, context, unit1, hidden, active, slope, unit2, (scale,), (out,)) = (
        forward_chain(fresh, text_home, memory_rows, table, gathered)
    )
    (grad_qkv, grad_proj, grad_upper, grad_down, (text_grad,), (narrow,), (wide,), (memory_grad,)) = (
        backward_chain(
            fresh, cotangent_home, table, scale,
            (qkv, probs, unit1, slope, unit2), gathered,
        )
    )

    def own_layer(pair):
        mine = jnp.where(net.core == 0, *pair)
        return mine.reshape(-1, mine.shape[-1])

    def product(left, right):
        full = dot(own_layer(left), own_layer(right), TN).astype(LOW)
        return full.reshape(chain, full.shape[0] // chain, full.shape[1])

    def vector_terms():
        sums, wides = jnp.sum(narrow, 2), jnp.sum(wide, 2)
        terms = [memory_grad[:mem].reshape(mem, chain, part).swapaxes(0, 1).reshape(chain, -1)]
        for layer in range(2):
            gain2, shift2, down, gain1, shift1, out_bias, query, value = (
                sums[layer, i] for i in range(8)
            )
            for v in (
                jnp.concatenate([query, value]), out_bias, gain1, shift1, wides[layer].reshape(-1),
                down, gain2, shift2,
            ):
                terms.append(v.reshape(chain, -1))
        terms = jnp.concatenate(terms, 1)
        terms = jnp.where(net.core == 0, terms, 0.0).astype(LOW)
        terms = jnp.pad(terms, ((0, 0), (0, 256 * part - terms.shape[1])))
        return terms.reshape(chain, part, 256)

    (down, up, qkv, proj, terms), text_grad, layer_out = net.reduce(
        [
            ([product(active, grad_down)], "lhx"),
            ([product(hidden, grad_upper)], "hlx"),
            ([product(low, grad_qkv), product(context, grad_proj), vector_terms()], "xlh"),
        ],
        text_grad,
        disorder(out),
    )
    vectors = terms[0].reshape(-1)
    results = []
    at = mem * part
    for layer in range(2):
        left = [qkv[layer], proj[layer], up[layer], down[layer]]
        for w in layers[layer]:
            if w.ndim == 1:
                results.append(vectors[at : at + w.shape[0]])
                at += w.shape[0]
            else:
                results.append(left.pop(0))
    return (
        layer_out[:, None],
        text_grad[:, None],
        vectors[: mem * part].reshape(mem, part),
        *results,
    )


def regroup(gathered, together, part):
    shards, total, width = gathered.shape
    blocks = gathered.reshape(shards // together, together, total // part, part, width)
    pieces = []
    for layer in range(2):
        base = layer * BLOCKS
        for block in range(8):
            pieces.append(blocks[:, :, base + block])
        pieces.append(blocks[:, :, base + 8 : base + 12])
    return jnp.concatenate([p.reshape(shards // together, -1, width) for p in pieces], 1)


def solution(mesh):
    seg = (P("seg", None), P("seg"), P("seg", None)) + (P("seg"),) * 3
    seg = seg + (P("seg", None), P("seg"), P("seg", None)) + (P("seg"),) * 3
    rows = P("item", "seg", None, None)
    return jax.shard_map(
        body,
        mesh=mesh,
        in_specs=(rows, rows, P("item"), P()) + seg + seg,
        out_specs=(rows, rows, P(None, "seg")) + seg + seg,
        check_vma=False,
    )
```

time: 1130 us -> 772 us (0.68)
  waiting for transfers between devices: 417 us -> 232 us
  blocking collectives: 132 us -> 0 us
  Pallas kernels: 379 us -> 317 us
  other arithmetic: 7.38 us -> 49.3 us
  matrix products: 65.2 us -> 32.6 us
  starting transfers between devices: 37.3 us -> 50.9 us
    reduce_scatter x1 -> x0, waiting for transfers between devices: 271 us -> none  [body(): lax.psum_scatter(jnp.concatenate(pieces, 1), 'seg', scatter_dimension=0,...]
    ppermute x0 -> x35, waiting for transfers between devices: none -> 148 us  [the longest x30 133 us: send(): return lax.ppermute(value, ('seg', 'item'), flat)]
    all_gather x1 -> x0, blocking collectives: 67.4 us -> none  [body(): vectors = lax.all_gather(vectors, 'seg').astype(F32)]
    unnamed x1 -> x0, blocking collectives: 59.7 us -> none
    pallas_call x1, Pallas kernels: 233 us -> 178 us  [backward_chain(): pl.pallas_call(backward_kernel, grid=(segments,), in_specs=[SMEM, block(r...]
    ppermute x0 -> x35, starting transfers between devices: none -> 50.9 us  [the longest x30 43.5 us: send(): return lax.ppermute(value, ('seg', 'item'), flat)]
    all_to_all x4 -> x0, starting transfers between devices: 36.7 us -> none  [the longest x2 24.6 us: from_home(): back = lax.all_to_all(blocks, 'seg', 0, 0, tiled=True)]
    all_gather x1, waiting for transfers between devices: 119 us -> 83.4 us  [body(): gathered = lax.all_gather(jnp.concatenate(shards), 'seg')]
  transfers between devices with their start and end apart: 7 -> 36, of which waited for: 3 -> 10; matrix products, arithmetic and copies ran while one was open for 3% -> 15% of each run, Pallas kernels for 13% -> 0%
where the time goes in v2:
time: 772 us; the launch traced here: 765 us
  Pallas kernels  317 us (41%)
  waiting for transfers between devices  232 us (30%)
  local copies, waits for them, and re-layouts  64.1 us (8%)
  starting transfers between devices  50.9 us (7%)
  other arithmetic  49.3 us (6%)
  matrix products  32.6 us (4%)
  between operations  19.2 us (2%)
    pallas_call x1, Pallas kernels, backward_chain(): pl.pallas_call(backward_kernel, grid=(segments,), in_specs=[SMEM, block(r...  178 us
    pallas_call x1, Pallas kernels, forward_chain(): pl.pallas_call(forward_kernel, grid=(segments,), in_specs=[SMEM, block((t...  139 us
    ppermute x30, waiting for transfers between devices, send(): return lax.ppermute(value, ('seg', 'item'), flat)  133 us
    all_gather x1, waiting for transfers between devices, body(): gathered = lax.all_gather(jnp.concatenate(shards), 'seg')  83.4 us
    ppermute x30, starting transfers between devices, send(): return lax.ppermute(value, ('seg', 'item'), flat)  43.5 us
    dot_general x4, matrix products, dot(): return lax.dot_general(left, right, dims, preferred_element_type=F32)  32.6 us
    convert_element_type x7, other arithmetic, add(): return total.astype(LOW)  17.7 us
  transfers between devices with their start and end apart: 36, of which 10 were waited for; matrix products, arithmetic and copies ran while one was open for 15% of the time, Pallas kernels for 0%

profile of v2, /device:TPU:0, one launch (start us, length us, event | category | flops | bytes accessed | tf_op | source)
XLA Modules:
  0.0 765.0 jit_solution(12045504862542379660)
XLA Ops:
  17.2 5.0 collective-permute-start.8
  26.1 15.9 %collective-permute-done.8 = bf16[4,84,768]{2,0,1:T(4,128)(2,1)S(1)} collective-permute-done((bf16[4,84,768]{2,0,1:T(4,128)(2,1)S(1)}, bf16[4,84,768]{2,0,1:T(4,128)(2,1)S(1)}, u32[]{:S(2)}, u32[]{:S(2)}) %collective-permute-start.8) | collective-permute-done | bytes 516128 | tf_op jit(solution)/shard_map/ppermute | solution.py:421
  44.2 13.7 %collective-permute-done = bf16[4,64,768]{2,1,0:T(8,128)(2,1)S(1)} collective-permute-done((bf16[4,64,768]{2,1,0:T(8,128)(2,1)S(1)}, bf16[4,64,768]{2,1,0:T(8,128)(2,1)S(1)}, u32[]{:S(2)}, u32[]{:S(2)}) %collective-permute-start) | collective-permute-done | bytes 393248 | tf_op jit(solution)/shard_map/ppermute | solution.py:421
  75.3 2.7 maximum_select_fusion.1
  80.7 10.3 %concatenate.344.refs_1_ = bf16[16,96,768]{2,1,0:T(8,128)(2,1)} concatenate(bf16[16,64,768]{2,1,0:T(8,128)(2,1)S(1)} %slice.441, bf16[16,10,768]{2,1,0:T(8,128)(2,1)S(1)} %get-tuple-element.114, bf16[16,6,768]{2,1,0:T(8,128)(2,1)S(1)} %broadcast_in_dim.16, bf16[16,10,768]{2,1,0:T(8,128)(2,1)S(1)} %get-tuple-element.113, bf16[16,6,768]{2,1,0:T(8,128)(2,1)S(1)} %broadcast_in_dim.16), dimensions={1} | concatenate | bytes 4718592 | tf_op jit(solution)/shard_map/concatenate | solution.py:610
  91.0 83.4 %all-gather.3.cloned.1.call-done = bf16[18432,768]{1,0:T(8,128)(2,1)} async-done(((bf16[1152,768]{1,0:T(8,128)(2,1)}), bf16[18432,768]{1,0:T(8,128)(2,1)}) %all-gather.3.cloned.1.call-update) | async-done | bytes 28311568 | tf_op jit(solution)/shard_map/all_gather | solution.py:628
  174.5 139.2 %forward_chain.1 = (bf16[16,96,768]{2,1,0:T(8,128)(2,1)}, bf16[16,96,768]{2,1,0:T(8,128)(2,1)}, bf16[16,96,2304]{2,1,0:T(8,128)(2,1)}, bf16[16,96,2304]{2,1,0:T(...) custom-call(s32[16]{0:T(128)} %or_convert_fusion.refs_0_, ...), custom_call_target="tpu_custom_call" | custom-call | flops 173946175488 | bytes 28311552 | tf_op jit(solution)/shard_map/forward_chain/pallas_call | solution.py:339
  313.6 177.9 %backward_chain.1 = (bf16[16,96,2304]{2,1,0:T(8,128)(2,1)}, bf16[16,96,2304]{2,1,0:T(8,128)(2,1)}, bf16[16,96,768]{2,1,0:T(8,128)(2,1)}, bf16[16,96,768]{2,1,0:T...) custom-call(s32[16]{0:T(128)} %or_convert_fusion.refs_0_, ...), custom_call_target="tpu_custom_call", output_to_operand_aliasing={{0}: (5, {}), {1}: (6, {}), {2}: (9, {}), {3}: (10, {}), {4... | custom-call | flops 173946175488 | bytes 28311552 | tf_op jit(solution)/shard_map/backward_chain/pallas_call | solution.py:368
  496.9 10.6 %bitcast_convert_fusion = bf16[768,3072]{1,0:T(8,128)(2,1)S(1)} fusion(bf16[16,96,3072]{2,1,0:T(8,128)(2,1)} %get-tuple-element.89, bf16[16,96,3072]{2,1,0:T(8,128)(2,1)} %get-tuple-element.90, pred[]{:T(512)S(6)} %eq.75, bf16[16,96,768]{2,1,0:T(8,128)(2,1)S(1)} %copy-done.38, bf16[16,96,768]{2,1,0:T(8,128)(2,1)} %get-tuple-element.88), kind=kOutput, calls=%fused_computation | convolution fusion | flops 7256014848 | bytes 28311552 | tf_op jit(solution)/shard_map/dot_general | solution.py:22
  517.6 9.2 %bitcast_convert_fusion.2 = bf16[768,2304]{1,0:T(8,128)(2,1)S(1)} fusion(bf16[16,96,2304]{2,1,0:T(8,128)(2,1)} %get-tuple-element.72, bf16[16,96,2304]{2,1,0:T(8,128)(2,1)} %get-tuple-element.73, pred[]{:T(512)S(6)} %eq.75, bf16[16,96,768]{2,1,0:T(8,128)(2,1)S(1)} %copy-done.36, bf16[16,96,768]{2,1,0:T(8,128)(2,1)S(1)} %copy-done.37), kind=kOutput, calls=%fused_computation.8 | convolution fusion | flops 5442306048 | bytes 22413312 | tf_op jit(solution)/shard_map/dot_general | solution.py:22
  533.2 10.6 %bitcast_convert_fusion.1 = bf16[3072,768]{1,0:T(8,128)(2,1)S(1)} fusion(bf16[16,96,3072]{2,1,0:T(8,128)(2,1)} %get-tuple-element.83, bf16[16,96,3072]{2,1,0:T(8,128)(2,1)} %get-tuple-element.84, pred[]{:T(512)S(6)} %eq.75, bf16[16,96,768]{2,1,0:T(8,128)(2,1)S(1)} %copy-done.39, bf16[16,96,768]{2,1,0:T(8,128)(2,1)S(1)} %copy-done.40), kind=kOutput, calls=%fused_computation.1 | convolution fusion | flops 7256014848 | bytes 28311552 | tf_op jit(solution)/shard_map/dot_general | solution.py:22
  561.7 3.1 add_convert_fusion.1
  566.5 3.0 add_convert_fusion.2
  584.0 3.1 broadcast_select_fusion
  590.1 2.8 add_convert_fusion.6
  594.5 2.9 add_convert_fusion.8
  607.1 3.1 broadcast_select_fusion.1
  621.7 67.9 %collective-permute-done.19 = bf16[4,64,768]{2,1,0:T(8,128)(2,1)S(1)} collective-permute-done((bf16[4,64,768]{2,1,0:T(8,128)(2,1)S(1)}, bf16[4,64,768]{2,1,0:T(8,128)(2,1)S(1)}, u32[]{:S(2)}, u32[]{:S(2)}) %collective-permute-start.19) | collective-permute-done | bytes 393248 | tf_op jit(solution)/shard_map/ppermute | solution.py:421
  691.2 17.2 %collective-permute-done.16 = bf16[4,84,768]{2,0,1:T(4,128)(2,1)S(1)} collective-permute-done((bf16[4,84,768]{2,0,1:T(4,128)(2,1)S(1)}, bf16[4,84,768]{2,0,1:T(4,128)(2,1)S(1)}, u32[]{:S(2)}, u32[]{:S(2)}) %collective-permute-start.16) | collective-permute-done | bytes 516128 | tf_op jit(solution)/shard_map/ppermute | solution.py:421
  709.5 9.7 %collective-permute-done.33 = bf16[48,3072]{1,0:T(8,128)(2,1)S(1)} collective-permute-done((bf16[48,3072]{1,0:T(8,128)(2,1)S(1)}, bf16[48,3072]{1,0:T(8,128)(2,1)S(1)}, u32[]{:S(2)}, u32[]{:S(2)}) %collective-permute-start.33) | collective-permute-done | bytes 294944 | tf_op jit(solution)/shard_map/ppermute | solution.py:421
  724.5 5.5 collective-permute-done.21
  730.1 2.9 collective-permute-done.23
  735.3 8.2 %collective-permute-done.24 = bf16[2,48,1664]{2,1,0:T(8,128)(2,1)S(1)} collective-permute-done((bf16[2,48,1664]{2,1,0:T(8,128)(2,1)S(1)}, bf16[2,48,1664]{2,1,0:T(8,128)(2,1)S(1)}, u32[]{:S(2)}, u32[]{:S(2)}) %collective-permute-start.24) | collective-permute-done | bytes 319520 | tf_op jit(solution)/shard_map/ppermute | solution.py:538
  748.1 7.2 collective-permute-done.34
  (325 shorter events, 130.7 us)
Async XLA Ops:
  7.2 167.2 %all-gather.3.cloned.1.call-start = ((), (), s32[]{:S(2)}) async-start(), calls=%async_computation | async-start | bytes 30081024 | tf_op jit(solution)/shard_map/all_gather | solution.py:628
  17.2 24.9 %collective-permute-start.8 = (bf16[4,84,768]{2,0,1:T(4,128)(2,1)S(1)}, bf16[4,84,768]{2,0,1:T(4,128)(2,1)S(1)}, u32[]{:S(2)}, u32[]{:S(2)}) collective-permute-start(bf16[4,84,768]{2,0,1:T(4,128)(2,1)S(1)} %bitcast.204), channel_id=1, source_target_pairs={{0,8},{1,9},{2,10},{3,11},{4,12},{5,13},{6,14},{7,15},{24,16},{25,... | collective-permute-start | bytes 1548296 | tf_op jit(solution)/shard_map/ppermute | solution.py:421
  22.5 21.0 %collective-permute-start.4 = (bf16[8,144]{1,0:T(8,128)(2,1)S(1)}, bf16[8,144]{1,0:T(8,128)(2,1)S(1)}, u32[]{:S(2)}, u32[]{:S(2)}) collective-permute-start(bf16[8,144]{1,0:T(8,128)(2,1)S(1)} %reshape.873), channel_id=1, source_target_pairs={{0,8},{1,9},{2,10},{3,11},{4,12},{5,13},{6,14},{7,15},{24,16},{25,... | collective-permute-start | bytes 6920 | tf_op jit(solution)/shard_map/ppermute | solution.py:421
  23.8 34.0 %collective-permute-start = (bf16[4,64,768]{2,1,0:T(8,128)(2,1)S(1)}, bf16[4,64,768]{2,1,0:T(8,128)(2,1)S(1)}, u32[]{:S(2)}, u32[]{:S(2)}) collective-permute-start(bf16[4,64,768]{2,1,0:T(8,128)(2,1)S(1)} %bitcast.206), channel_id=1, source_target_pairs={{0,8},{1,9},{2,10},{3,11},{4,12},{5,13},{6,14},{7,15},{24,16},{25,... | collective-permute-start | bytes 1179656 | tf_op jit(solution)/shard_map/ppermute | solution.py:421
  42.8 16.6 %collective-permute-start.9 = (bf16[1,1,2,2,1,84,768]{6,3,5,4,2,1,0:T(2,128)(2,1)S(1)}, bf16[1,1,2,2,1,84,768]{6,3,5,4,2,1,0:T(2,128)(2,1)S(1)}, u32[]{:S(2)}, u32[]{:S(2)}) collective-permute-start(bf16[1,1,2,2,1,84,768]{6,3,5,4,2,1,0:T(2,128)(2,1)S(1)} %copy.144), channel_id=1, source_target_pairs={{8,12},{9,13},{10,14},{11,15},{12,8},{13,9},{14,10},{15,11},{16,20... | collective-permute-start | bytes 1548296 | tf_op jit(solution)/shard_map/ppermute | solution.py:421
  511.0 50.7 %collective-permute-start.28 = (bf16[1,2,2,2,48,3072]{5,4,3,2,1,0:T(8,128)(2,1)}, bf16[1,2,2,2,48,3072]{5,4,3,2,1,0:T(8,128)(2,1)}, u32[]{:S(2)}, u32[]{:S(2)}) collective-permute-start(bf16[1,2,2,2,48,3072]{5,4,3,2,1,0:T(8,128)(2,1)} %constant_dynamic-slice_fusion), channel_id=1, source_target_pairs={{8,16},{9,17},{10,18},{11,19},{12,20},{13,21},{14,22},{15,23},{16,... | collective-permute-start | bytes 7077896 | tf_op jit(solution)/shard_map/ppermute | solution.py:421
  531.0 40.3 %collective-permute-start.12 = (bf16[2,2,2,2,48,1664]{5,4,3,2,1,0:T(8,128)(2,1)}, bf16[2,2,2,2,48,1664]{5,4,3,2,1,0:T(8,128)(2,1)}, u32[]{:S(2)}, u32[]{:S(2)}) collective-permute-start(bf16[2,2,2,2,48,1664]{5,4,3,2,1,0:T(8,128)(2,1)} %pad_maximum_fusion.1), channel_id=1, source_target_pairs={{8,9},{9,8},{10,11},{11,10},{12,13},{13,12},{14,15},{15,14},{16,17... | collective-permute-start | bytes 7667720 | tf_op jit(solution)/shard_map/ppermute | solution.py:429
  546.8 19.7 %collective-permute-start.25 = (bf16[2,2,1,2,192,768]{5,4,3,2,1,0:T(8,128)(2,1)}, bf16[2,2,1,2,192,768]{5,4,3,2,1,0:T(8,128)(2,1)}, u32[]{:S(2)}, u32[]{:S(2)}) collective-permute-start(bf16[2,2,1,2,192,768]{5,4,3,2,1,0:T(8,128)(2,1)} %constant_dynamic-slice_fusion.1), channel_id=1, source_target_pairs={{8,12},{9,13},{10,14},{11,15},{12,8},{13,9},{14,10},{15,11},{16,20... | collective-permute-start | bytes 7077896 | tf_op jit(solution)/shard_map/ppermute | solution.py:421
  555.7 28.3 %collective-permute-start.14 = (bf16[1,2,1,1,2,84,768]{6,4,5,3,2,1,0:T(2,128)(2,1)}, bf16[1,2,1,1,2,84,768]{6,4,5,3,2,1,0:T(2,128)(2,1)}, u32[]{:S(2)}, u32[]{:S(2)}) collective-permute-start(bf16[1,2,1,1,2,84,768]{6,4,5,3,2,1,0:T(2,128)(2,1)} %copy.155), channel_id=1, source_target_pairs={{8,16},{9,17},{10,18},{11,19},{12,20},{13,21},{14,22},{15,23},{16,... | collective-permute-start | bytes 1548296 | tf_op jit(solution)/shard_map/ppermute | solution.py:421
  558.5 21.8 %collective-permute-start.17 = (bf16[1,2,1,1,2,64,768]{6,5,4,1,3,2,0:T(8,128)(2,1)}, bf16[1,2,1,1,2,64,768]{6,5,4,1,3,2,0:T(8,128)(2,1)}, u32[]{:S(2)}, u32[]{:S(2)}) collective-permute-start(bf16[1,2,1,1,2,64,768]{6,5,4,1,3,2,0:T(8,128)(2,1)} %bitcast.173), channel_id=1, source_target_pairs={{8,16},{9,17},{10,18},{11,19},{12,20},{13,21},{14,22},{15,23},{16,... | collective-permute-start | bytes 1179656 | tf_op jit(solution)/shard_map/ppermute | solution.py:421
  564.8 25.4 %collective-permute-start.29 = (bf16[1,2,1,2,48,3072]{5,4,3,2,1,0:T(8,128)(2,1)}, bf16[1,2,1,2,48,3072]{5,4,3,2,1,0:T(8,128)(2,1)}, u32[]{:S(2)}, u32[]{:S(2)}) collective-permute-start(bf16[1,2,1,2,48,3072]{5,4,3,2,1,0:T(8,128)(2,1)} %add_convert_fusion.1), channel_id=1, source_target_pairs={{8,12},{9,13},{10,14},{11,15},{12,8},{13,9},{14,10},{15,11},{16,20... | collective-permute-start | bytes 3538952 | tf_op jit(solution)/shard_map/ppermute | solution.py:421
  569.4 25.0 %collective-permute-start.26 = (bf16[1,2,1,2,192,768]{5,4,3,2,1,0:T(8,128)(2,1)}, bf16[1,2,1,2,192,768]{5,4,3,2,1,0:T(8,128)(2,1)}, u32[]{:S(2)}, u32[]{:S(2)}) collective-permute-start(bf16[1,2,1,2,192,768]{5,4,3,2,1,0:T(8,128)(2,1)} %add_convert_fusion.2), channel_id=1, source_target_pairs={{8,16},{9,17},{10,18},{11,19},{12,20},{13,21},{14,22},{15,23},{16,... | collective-permute-start | bytes 3538952 | tf_op jit(solution)/shard_map/ppermute | solution.py:421
  573.9 24.9 %collective-permute-start.13 = (bf16[2,2,1,2,48,1664]{5,4,3,2,1,0:T(8,128)(2,1)}, bf16[2,2,1,2,48,1664]{5,4,3,2,1,0:T(8,128)(2,1)}, u32[]{:S(2)}, u32[]{:S(2)}) collective-permute-start(bf16[2,2,1,2,48,1664]{5,4,3,2,1,0:T(8,128)(2,1)} %add_convert_fusion), channel_id=1, source_target_pairs={{8,12},{9,13},{10,14},{11,15},{12,8},{13,9},{14,10},{15,11},{16,20... | collective-permute-start | bytes 3833864 | tf_op jit(solution)/shard_map/ppermute | solution.py:421
  582.6 21.9 %collective-permute-start.18 = (bf16[1,1,2,1,2,64,768]{6,5,4,1,3,2,0:T(8,128)(2,1)}, bf16[1,1,2,1,2,64,768]{6,5,4,1,3,2,0:T(8,128)(2,1)}, u32[]{:S(2)}, u32[]{:S(2)}) collective-permute-start(bf16[1,1,2,1,2,64,768]{6,5,4,1,3,2,0:T(8,128)(2,1)} %get-tuple-element.141), channel_id=1, source_target_pairs={{8,12},{9,13},{10,14},{11,15},{12,8},{13,9},{14,10},{15,11},{16,20... | collective-permute-start | bytes 1179656 | tf_op jit(solution)/shard_map/ppermute | solution.py:421
  588.7 18.4 %collective-permute-start.15 = (bf16[1,1,2,1,2,84,768]{6,4,5,3,2,1,0:T(2,128)(2,1)}, bf16[1,1,2,1,2,84,768]{6,4,5,3,2,1,0:T(2,128)(2,1)}, u32[]{:S(2)}, u32[]{:S(2)}) collective-permute-start(bf16[1,1,2,1,2,84,768]{6,4,5,3,2,1,0:T(2,128)(2,1)} %get-tuple-element.137), channel_id=1, source_target_pairs={{8,12},{9,13},{10,14},{11,15},{12,8},{13,9},{14,10},{15,11},{16,20... | collective-permute-start | bytes 1548296 | tf_op jit(solution)/shard_map/ppermute | solution.py:421
  592.9 23.8 %collective-permute-start.30 = (bf16[1,2,1,2,48,1536]{5,4,3,2,1,0:T(8,128)(2,1)}, bf16[1,2,1,2,48,1536]{5,4,3,2,1,0:T(8,128)(2,1)}, u32[]{:S(2)}, u32[]{:S(2)}) collective-permute-start(bf16[1,2,1,2,48,1536]{5,4,3,2,1,0:T(8,128)(2,1)} %add_convert_fusion.6), channel_id=1, source_target_pairs={{8,9},{9,8},{10,11},{11,10},{12,13},{13,12},{14,15},{15,14},{16,17... | collective-permute-start | bytes 1769480 | tf_op jit(solution)/shard_map/ppermute | solution.py:429
  597.3 16.8 %collective-permute-start.27 = (bf16[1,2,1,2,192,384]{5,4,3,2,1,0:T(8,128)(2,1)}, bf16[1,2,1,2,192,384]{5,4,3,2,1,0:T(8,128)(2,1)}, u32[]{:S(2)}, u32[]{:S(2)}) collective-permute-start(bf16[1,2,1,2,192,384]{5,4,3,2,1,0:T(8,128)(2,1)} %add_convert_fusion.8), channel_id=1, source_target_pairs={{8,9},{9,8},{10,11},{11,10},{12,13},{13,12},{14,15},{15,14},{16,17... | collective-permute-start | bytes 1769480 | tf_op jit(solution)/shard_map/ppermute | solution.py:429
  603.0 116.3 %collective-permute-start.20 = (bf16[1,2,1,2,48,1664]{5,4,3,2,1,0:T(8,128)(2,1)}, bf16[1,2,1,2,48,1664]{5,4,3,2,1,0:T(8,128)(2,1)}, u32[]{:S(2)}, u32[]{:S(2)}) collective-permute-start(bf16[1,2,1,2,48,1664]{5,4,3,2,1,0:T(8,128)(2,1)} %copy-done.6), channel_id=1, source_target_pairs={{8,16},{9,17},{10,18},{11,19},{12,20},{13,21},{14,22},{15,23},{16,... | collective-permute-start | bytes 1916936 | tf_op jit(solution)/shard_map/ppermute | solution.py:421
  605.8 83.8 %collective-permute-start.19 = (bf16[4,64,768]{2,1,0:T(8,128)(2,1)S(1)}, bf16[4,64,768]{2,1,0:T(8,128)(2,1)S(1)}, u32[]{:S(2)}, u32[]{:S(2)}) collective-permute-start(bf16[4,64,768]{2,1,0:T(8,128)(2,1)S(1)} %dynamic-slice_bitcast_fusion.1), channel_id=1, source_target_pairs={{8,0},{9,1},{10,2},{11,3},{12,4},{13,5},{14,6},{15,7},{16,24},{17,... | collective-permute-start | bytes 1179656 | tf_op jit(solution)/shard_map/ppermute | solution.py:421
  612.6 95.8 %collective-permute-start.16 = (bf16[4,84,768]{2,0,1:T(4,128)(2,1)S(1)}, bf16[4,84,768]{2,0,1:T(4,128)(2,1)S(1)}, u32[]{:S(2)}, u32[]{:S(2)}) collective-permute-start(bf16[4,84,768]{2,0,1:T(4,128)(2,1)S(1)} %bitcast.203), channel_id=1, source_target_pairs={{8,0},{9,1},{10,2},{11,3},{12,4},{13,5},{14,6},{15,7},{16,24},{17,... | collective-permute-start | bytes 1548296 | tf_op jit(solution)/shard_map/ppermute | solution.py:421
  619.1 103.4 %collective-permute-start.31 = (bf16[48,3072]{1,0:T(8,128)(2,1)S(1)}, bf16[48,3072]{1,0:T(8,128)(2,1)S(1)}, u32[]{:S(2)}, u32[]{:S(2)}) collective-permute-start(bf16[48,3072]{1,0:T(8,128)(2,1)S(1)} %get-tuple-element.123), channel_id=1, source_target_pairs={{8,0},{9,1},{10,2},{11,3},{12,4},{13,5},{14,6},{15,7},{16,24},{17,... | collective-permute-start | bytes 884744 | tf_op jit(solution)/shard_map/ppermute | solution.py:421
  620.4 98.9 %collective-permute-start.33 = (bf16[48,3072]{1,0:T(8,128)(2,1)S(1)}, bf16[48,3072]{1,0:T(8,128)(2,1)S(1)}, u32[]{:S(2)}, u32[]{:S(2)}) collective-permute-start(bf16[48,3072]{1,0:T(8,128)(2,1)S(1)} %get-tuple-element.124), channel_id=1, source_target_pairs={{8,2},{9,3},{10,0},{11,1},{12,6},{13,7},{14,4},{15,5},{16,26},{17,... | collective-permute-start | bytes 884744 | tf_op jit(solution)/shard_map/ppermute | solution.py:421
  689.6 29.7 %collective-permute-start.32 = (bf16[48,3072]{1,0:T(8,128)(2,1)S(1)}, bf16[48,3072]{1,0:T(8,128)(2,1)S(1)}, u32[]{:S(2)}, u32[]{:S(2)}) collective-permute-start(bf16[48,3072]{1,0:T(8,128)(2,1)S(1)} %get-tuple-element.125), channel_id=1, source_target_pairs={{8,10},{9,11},{10,8},{11,9},{12,14},{13,15},{14,12},{15,13},{16,18... | collective-permute-start | bytes 884744 | tf_op jit(solution)/shard_map/ppermute | solution.py:421
  733.7 21.6 %collective-permute-start.34 = (bf16[2,48,3072]{2,1,0:T(8,128)(2,1)S(1)}, bf16[2,48,3072]{2,1,0:T(8,128)(2,1)S(1)}, u32[]{:S(2)}, u32[]{:S(2)}) collective-permute-start(bf16[2,48,3072]{2,1,0:T(8,128)(2,1)S(1)} %maximum_select_fusion.10), channel_id=1, source_target_pairs={{0,1},{1,0},{2,3},{3,2},{4,5},{5,4},{6,7},{7,6},{8,9},{9,8},{10,11... | collective-permute-start | bytes 1769480 | tf_op jit(solution)/shard_map/ppermute | solution.py:538
  (53 other events, 351.0 us)
Sparse Core Ops, SparseCore 0:
  17.3 157.1 all-gather.2

commit v3 on v2

v3 whole, which is shorter than its diff:
```python
import functools

import jax
import jax.numpy as jnp
from jax import lax
from jax.experimental import pallas as pl
from jax.experimental.pallas import tpu as pltpu
from jax.sharding import PartitionSpec as P

HEAD_DIM = 64
EPSILON = 1e-05
F32 = jnp.float32
LOW = jnp.bfloat16
NN = (((1,), (0,)), ((), ()))
NT = (((1,), (1,)), ((), ()))
TN = (((0,), (0,)), ((), ()))

PAD = 16
BLOCKS = 12
B_QUERY, B_VALUE, B_OUT, GAIN1, SHIFT1, B_UP, B_DOWN, GAIN2, SHIFT2 = 0, 1, 2, 3, 4, 5, 9, 10, 11


def dot(left, right, dims=NN):
    return lax.dot_general(left, right, dims, preferred_element_type=F32)


def norm_rows(total, gain, shift):
    centre = total - jnp.mean(total, -1, keepdims=True)
    scale = lax.rsqrt(jnp.mean(centre * centre, -1, keepdims=True) + EPSILON)
    unit = centre * scale
    return unit, scale, unit * gain + shift


def norm_back(grad, unit, scale, gain):
    t = grad * gain
    return scale * (
        t - jnp.mean(t, -1, keepdims=True) - unit * jnp.mean(t * unit, -1, keepdims=True)
    )


def gelu_and_slope(upper):
    density = jnp.exp(upper * upper * -0.5) * 0.3989422804014327
    below = 0.5 * (1.0 + lax.erf(upper * 0.7071067811865476))
    return upper * below, below + upper * density


def fold(block):
    rows, width = block.shape
    return jnp.sum(block.reshape(rows // 8, 8, width), 0)


def two_heads(block, first):
    zero = jnp.zeros_like(block)
    return jnp.concatenate([jnp.where(first, block, zero), jnp.where(first, zero, block)], 0)


def copy_block(gathered, target, layer, block, part, sem):
    shards = gathered.shape[0]
    base = layer * BLOCKS * part

    def copy(shard, row, to, count):
        pltpu.make_async_copy(
            gathered.at[shard, pl.ds(pl.multiple_of(row, 16), count)],
            target(pl.multiple_of(to, 16), count),
            sem,
        ).start()

    @pl.when(block < 8)
    def _():
        def start(shard, none):
            copy(shard, base + block * part, shard * part, part)
            return none

        lax.fori_loop(0, shards, start, 0)

    @pl.when(block >= 8)
    def _():
        def start(i, none):
            shard = (block - 8) * (shards // 4) + i
            copy(shard, base + 8 * part, i * 4 * part, 4 * part)
            return none

        lax.fori_loop(0, shards // 4, start, 0)


def block_of(held, index, width):
    return held.at[pl.ds(pl.multiple_of(index * width, 128), width), :]


def start_weights(gathered, held, width, sems):
    part = width // gathered.shape[0]

    def start(index, none):
        def target(row, count):
            return held.at[pl.ds(pl.multiple_of(index * width + row, 16), count)]

        copy_block(gathered, target, index // BLOCKS, index % BLOCKS, part, sems.at[index])
        return none

    lax.fori_loop(0, 2 * BLOCKS, start, 0)


def start_turned(turned, held, width, sems):
    lanes = width // 128
    per = lanes + lanes // 2
    for index in reversed(range(2 * BLOCKS)):
        for lane in range(lanes):
            block, k = divmod(index * lanes + lane, per)
            for rows, at, part in parts_of(k, width):
                pltpu.make_async_copy(
                    turned.at[block, rows, at : at + 128],
                    held.at[
                        index * width + part.start : index * width + part.stop,
                        128 * lane : 128 * (lane + 1),
                    ],
                    sems.at[index],
                ).start()


def wait_block(held, index, width, sems):
    target = block_of(held, index, width)
    pltpu.make_async_copy(target, target, sems.at[index]).wait()


def split_refs(refs, sizes):
    parts = []
    for size in sizes:
        parts.append(refs[:size])
        refs = refs[size:]
    return parts


def forward_kernel(*refs):
    (
        (fresh_ref, text_ref, memory_ref, vector_ref, gathered_ref),
        low_ref, qkv_ref, probs_ref, context_ref, unit1_ref, hidden_ref, active_ref, slope_ref,
        unit2_ref,
        (scale_ref, out_ref, turned_ref, held, carry, sems),
    ) = split_refs(refs, [5] + [2] * 9 + [6])
    step = pl.program_id(0)
    texts, width = text_ref.shape[1:]
    rows = texts + 2 * PAD
    mem = 10
    first_head = lax.broadcasted_iota(jnp.int32, (rows, 2 * HEAD_DIM), 1) < HEAD_DIM

    def run():
        column = lax.broadcasted_iota(jnp.int32, (2 * rows, rows), 1)
        unused = jnp.logical_or(
            column >= texts + PAD + mem,
            jnp.logical_and(column >= texts + mem, column < texts + PAD),
        )
        mask = jnp.where(unused, -1e30, 0.0).astype(F32)
        memory = memory_ref[...]
        read = jnp.where(fresh_ref[step] > 0, memory, carry[...])
        x = jnp.concatenate([text_ref[0], read, memory], 0).astype(F32)
        scales = []
        for index in range(2):

            def weight(block, index=index):
                at = index * BLOCKS + block
                return held[at * width : (at + 1) * width, :]

            def vector(row, index=index):
                return vector_ref[index, row : row + 1, :]

            low = x.astype(LOW)
            low_ref[index][0] = low
            query = (dot(low, weight(0)) + vector(B_QUERY)).astype(LOW)
            keys = dot(low, weight(1)).astype(LOW)
            values = (dot(low, weight(2)) + vector(B_VALUE)).astype(LOW)
            qkv_ref[index][0, :, :width] = query
            qkv_ref[index][0, :, width : 2 * width] = keys
            qkv_ref[index][0, :, 2 * width :] = values
            query = query * LOW(HEAD_DIM ** (-0.5))
            pairs = range(width // (2 * HEAD_DIM))
            cols = [slice(2 * HEAD_DIM * p, 2 * HEAD_DIM * (p + 1)) for p in pairs]
            scores = [dot(two_heads(query[:, c], first_head), keys[:, c], NT) + mask for c in cols]
            weights = [jnp.exp(e - jnp.max(e, -1, keepdims=True)) for e in scores]
            totals = [jnp.sum(e, -1, keepdims=True) for e in weights]
            both = [dot(weights[p].astype(LOW), values[:, cols[p]]) for p in pairs]
            for p in pairs:
                inverse = 1.0 / totals[p]
                context = both[p] * inverse
                probs_ref[index][0, p] = (weights[p] * inverse).astype(LOW)
                context_ref[index][0, :, cols[p]] = jnp.where(
                    first_head, context[:rows], context[rows:]
                ).astype(LOW)
            total = x + dot(context_ref[index][0], weight(3)) + vector(B_OUT)
            unit, scale, hidden = norm_rows(total, vector(GAIN1), vector(SHIFT1))
            unit1_ref[index][0] = unit.astype(LOW)
            scales.append(scale)
            hidden_low = hidden.astype(LOW)
            hidden_ref[index][0] = hidden_low
            total = hidden + vector(B_DOWN)
            upper = [dot(hidden_low, weight(4 + b)) + vector(B_UP + b) for b in range(4)]
            for block in range(4):
                wide = slice(block * width, (block + 1) * width)
                active, slope = gelu_and_slope(upper[block])
                active = active.astype(LOW)
                active_ref[index][0, :, wide] = active
                slope_ref[index][0, :, wide] = slope.astype(LOW)
                total = total + dot(active, weight(8 + block))
            unit, scale, x = norm_rows(total, vector(GAIN2), vector(SHIFT2))
            unit2_ref[index][0] = unit.astype(LOW)
            scales.append(scale)
        lane = lax.broadcasted_iota(jnp.int32, (rows, 128), 1)
        packed = scales[3]
        for i in (2, 1, 0):
            packed = jnp.where(lane < 32 * (i + 1), scales[i], packed)
        scale_ref[0] = packed
        final = x.astype(LOW)
        out_ref[0] = final
        carry[...] = final[texts + PAD :]

    @pl.when(step == 0)
    def _():
        start_weights(gathered_ref, held, width, sems)
        for block in range(2 * BLOCKS):
            wait_block(held, block, width, sems)
        carry[...] = jnp.zeros_like(carry)

    run()

    steps = turns_of(pl.num_programs(0))
    lanes = width // 128
    per = lanes + lanes // 2

    def turn(k):
        row = pl.multiple_of(((step // steps) * per + k) * 128, 128)
        strip = held[pl.ds(row, 128), :].T
        for rows, at, part in parts_of(k, width):
            turned_ref[0, rows, at : at + 128] = strip[part]

    for k in range(per):
        if steps == 1:
            turn(k)
        else:
            pl.when(step % steps == k % steps)(functools.partial(turn, k))


def parts_of(k, width):
    lanes = width // 128
    if k < lanes:
        return [(slice(0, width), 128 * k, slice(0, width))]
    half, at = width // 2, 256 * (k - lanes)
    return [
        (slice(width, width + half), at + 128 * i, slice(half * i, half * (i + 1))) for i in range(2)
    ]


def turns_of(segments):
    return max(segments // 16, 1)


def backward_kernel(*refs):
    (
        (fresh_ref, cotangent_ref, vector_ref, scale_ref, turned_ref),
        qkv_ref, probs_ref, unit1_ref, slope_ref, unit2_ref,
        grad_qkv_ref, grad_proj_ref, grad_upper_ref, grad_down_ref,
        (text_ref, table_ref, narrow_ref, wide_ref, memory_ref, held, carry, sems),
    ) = split_refs(refs, [5] + [2] * 5 + [2] * 4 + [8])
    turn = pl.program_id(0)
    step = pl.num_programs(0) - 1 - turn
    rows, width = cotangent_ref.shape[1:]
    texts = rows - 2 * PAD
    first_head = lax.broadcasted_iota(jnp.int32, (rows, 2 * HEAD_DIM), 1) < HEAD_DIM

    def run(loading):
        grad = cotangent_ref[0].astype(F32)
        if not loading:
            grad = jnp.concatenate(
                [grad[: texts + PAD], grad[texts + PAD :] + carry[...].astype(F32)], 0
            )
        for index in (1, 0):

            def weight(block, index=index):
                at = index * BLOCKS + block
                if loading:
                    wait_block(held, at, width, sems)
                return held[at * width : (at + 1) * width, :]

            def vector(row, index=index):
                return vector_ref[index, row : row + 1, :]

            def scale(norm, index=index):
                lane = 32 * (2 * index + norm)
                return scale_ref[0, :, lane : lane + 1]

            unit = unit2_ref[index][0].astype(F32)
            narrow_ref[index, 0] += fold(grad * unit)
            narrow_ref[index, 1] += fold(grad)
            grad_second = norm_back(grad, unit, scale(1), vector(GAIN2))
            narrow_ref[index, 2] += fold(grad_second)
            grad_down = grad_second.astype(LOW)
            grad_hidden = grad_second
            ahead = dot(grad_down, weight(11))
            for block in (3, 2, 1, 0):
                wide = slice(block * width, (block + 1) * width)
                grad_upper = ahead * slope_ref[index][0, :, wide].astype(F32)
                if block:
                    ahead = dot(grad_down, weight(7 + block))
                wide_ref[index, block] += fold(grad_upper)
                grad_upper = grad_upper.astype(LOW)
                grad_upper_ref[index][0, :, wide] = grad_upper
                grad_hidden = grad_hidden + dot(grad_upper, weight(4 + block))
            grad_down_ref[index][0] = grad_down
            unit = unit1_ref[index][0].astype(F32)
            narrow_ref[index, 3] += fold(grad_hidden * unit)
            narrow_ref[index, 4] += fold(grad_hidden)
            grad_first = norm_back(grad_hidden, unit, scale(0), vector(GAIN1))
            narrow_ref[index, 5] += fold(grad_first)
            grad_proj = grad_first.astype(LOW)
            grad_proj_ref[index][0] = grad_proj
            grad_context = dot(grad_proj, weight(3)).astype(LOW)
            eighth = LOW(HEAD_DIM ** (-0.5))
            pairs = range(width // (2 * HEAD_DIM))
            cols = [slice(2 * HEAD_DIM * p, 2 * HEAD_DIM * (p + 1)) for p in pairs]
            in_keys = [slice(width + c.start, width + c.stop) for c in cols]
            in_values = [slice(2 * width + c.start, 2 * width + c.stop) for c in cols]
            query = [two_heads(qkv_ref[index][0, :, c] * eighth, first_head) for c in cols]
            context = [two_heads(grad_context[:, c], first_head) for c in cols]
            term = [dot(context[p], qkv_ref[index][0, :, in_values[p]], NT) for p in pairs]
            probs = [probs_ref[index][0, p] for p in pairs]
            term = [term[p] * probs[p].astype(F32) for p in pairs]
            total = [jnp.sum(t, -1, keepdims=True) for t in term]
            grad_scores = [(term[p] - probs[p].astype(F32) * total[p]).astype(LOW) for p in pairs]
            both = [dot(grad_scores[p], qkv_ref[index][0, :, in_keys[p]] * eighth) for p in pairs]
            grad_query = [jnp.where(first_head, b[:rows], b[rows:]) for b in both]
            grad_keys = [dot(grad_scores[p], query[p], TN) for p in pairs]
            grad_values = [dot(probs[p], context[p], TN) for p in pairs]
            for p in pairs:
                narrow_ref[index, 6, :, cols[p]] += fold(grad_query[p])
                narrow_ref[index, 7, :, cols[p]] += fold(grad_values[p])
                grad_qkv_ref[index][0, :, cols[p]] = grad_query[p].astype(LOW)
                grad_qkv_ref[index][0, :, in_keys[p]] = grad_keys[p].astype(LOW)
                grad_qkv_ref[index][0, :, in_values[p]] = grad_values[p].astype(LOW)
            grad = grad_first
            for block in (2, 1, 0):
                cols = slice(block * width, (block + 1) * width)
                grad = grad + dot(grad_qkv_ref[index][0, :, cols], weight(block))
        text_ref[0] = grad[:texts].astype(LOW)
        read = grad[texts : texts + PAD]
        fresh = fresh_ref[step] > 0
        memory_ref[...] += grad[texts + PAD :] + jnp.where(fresh, read, 0.0)
        carry[...] = jnp.where(fresh, 0.0, read).astype(LOW)

    @pl.when(turn == 0)
    def _():
        start_turned(turned_ref, held, width, sems)
        narrow_ref[...] = jnp.zeros_like(narrow_ref)
        wide_ref[...] = jnp.zeros_like(wide_ref)
        memory_ref[...] = jnp.zeros_like(memory_ref)
        run(True)

    @pl.when(turn > 0)
    def _():
        run(False)

    @pl.when(step == 0)
    def _():
        sums = [jnp.sum(narrow_ref[i, j], 0, keepdims=True) for i in range(2) for j in range(8)]
        sums += [jnp.sum(wide_ref[i, j], 0, keepdims=True) for i in range(2) for j in range(4)]
        table_ref[...] = jnp.concatenate(sums + [memory_ref[...]], 0)


SMEM = pl.BlockSpec(memory_space=pltpu.SMEM)
VMEM = pl.BlockSpec(memory_space=pltpu.VMEM)
ANY = pl.BlockSpec(memory_space=pl.ANY)


def cost(rows, width, segments):
    return pl.CostEstimate(
        flops=2 * rows * 2 * BLOCKS * width * width * segments * 4,
        bytes_accessed=2 * 2 * BLOCKS * width * width,
        transcendentals=0,
    )


def forward_chain(fresh, text, memory, vectors, gathered):
    segments, texts, width = text.shape
    rows = texts + 2 * PAD
    pairs = width // (2 * HEAD_DIM)

    def block(shape):
        return pl.BlockSpec((1,) + shape, lambda s: (s,) + (0,) * len(shape))

    row = (rows, width)
    shapes = [row, (rows, 3 * width), (pairs, 2 * rows, rows), row, row, row]
    shapes += [(rows, 4 * width), (rows, 4 * width), row]
    outs = [(shape, LOW) for shape in shapes for _ in range(2)]
    outs += [((rows, 128), F32), (row, LOW)]
    steps = turns_of(segments)
    found = pl.pallas_call(
        forward_kernel,
        grid=(segments,),
        in_specs=[SMEM, block((texts, width)), VMEM, VMEM, ANY],
        out_specs=[block(shape) for shape, _ in outs]
        + [pl.BlockSpec((1,) + gathered.shape[1:], lambda s: (s // steps, 0, 0))],
        out_shape=[jax.ShapeDtypeStruct((segments,) + shape, kind) for shape, kind in outs]
        + [jax.ShapeDtypeStruct(gathered.shape, LOW)],
        input_output_aliases={4: len(outs)} if steps > 1 else {},
        scratch_shapes=[
            pltpu.VMEM((2 * BLOCKS * width, width), LOW),
            pltpu.VMEM((PAD, width), LOW),
            pltpu.SemaphoreType.DMA((2 * BLOCKS,)),
        ],
        compiler_params=pltpu.CompilerParams(vmem_limit_bytes=62 << 20),
        cost_estimate=cost(rows, width, segments),
        name="forward_chain",
    )(fresh, text, memory, vectors, gathered)
    return split_refs(found, [2] * 9 + [1, 1, 1])


def backward_chain(fresh, cotangent, vectors, scale, saved, turned):
    segments, rows, width = cotangent.shape
    texts = rows - 2 * PAD
    pairs = width // (2 * HEAD_DIM)

    def block(shape):
        return pl.BlockSpec((1,) + shape, lambda t: (segments - 1 - t,) + (0,) * len(shape))

    row, three, four = (rows, width), (rows, 3 * width), (rows, 4 * width)
    outs = [shape for shape in (three, row, four, row) for _ in range(2)] + [(texts, width)]
    ins = [shape for shape in (three, (pairs, 2 * rows, rows), row, four, row) for _ in range(2)]
    found = pl.pallas_call(
        backward_kernel,
        grid=(segments,),
        in_specs=[SMEM, block(row), VMEM, block((rows, 128)), ANY]
        + [block(shape) for shape in ins],
        out_specs=[block(shape) for shape in outs] + [VMEM],
        out_shape=[jax.ShapeDtypeStruct((segments,) + shape, LOW) for shape in outs]
        + [jax.ShapeDtypeStruct((24 + PAD, width), F32)],
        scratch_shapes=[
            pltpu.VMEM((2, 8, 8, width), F32),
            pltpu.VMEM((2, 4, 8, width), F32),
            pltpu.VMEM((PAD, width), F32),
            pltpu.VMEM((2 * BLOCKS * width, width), LOW),
            pltpu.VMEM((PAD, width), LOW),
            pltpu.SemaphoreType.DMA((2 * BLOCKS,)),
        ],
        input_output_aliases={5: 0, 6: 1, 9: 2, 10: 3, 11: 4, 12: 5, 13: 6, 14: 7},
        compiler_params=pltpu.CompilerParams(vmem_limit_bytes=62 << 20),
        cost_estimate=cost(rows, width, segments),
        name="backward_chain",
    )(fresh, cotangent, vectors, scale, turned, *(a for pair in saved for a in pair))
    return split_refs(found, [2] * 4 + [1] * 2)


def split_columns(shard, width):
    rows, columns = shard.shape
    return [shard[:, i : i + width] for i in range(0, columns, width)]


class Slice:
    def __init__(self, micro):
        self.micro, self.half = micro, micro // 2
        self.bits = self.half.bit_length() - 1
        self.chain, self.items = lax.axis_size("seg"), lax.axis_size("item")
        self.start = (self.chain - 2 * micro) // 2
        self.place, self.item = lax.axis_index("seg"), lax.axis_index("item")
        self.core = self.place % 2
        self.home = jnp.clip((self.place - self.start) // 2, 0, micro - 1)
        self.high, self.low = self.home // self.half, self.home % self.half
        self.at_home = jnp.logical_and(
            self.place >= self.start, self.place < self.start + 2 * micro
        )

    def seat(self, home, core=0):
        return self.start + 2 * home + core

    def far(self, home, core=0):
        return self.seat(home, core) + self.micro * (-1 if home < self.half else 1)

    def send(self, value, pairs):
        flat = [(a * self.items + x, b * self.items + x) for a, b in pairs for x in range(self.items)]
        return lax.ppermute(value, ("seg", "item"), flat)

    def send_across(self, value, bit):
        flat = []
        for i in range(self.micro):
            for c in range(2):
                at = self.seat(i, c) * self.items
                flat += [(at + x, at + (x ^ (1 << bit))) for x in range(self.items)]
        return lax.ppermute(value, ("seg", "item"), flat)

    def between_homes(self, flip):
        return [(self.seat(i, c), self.seat(i ^ flip, c)) for i in range(self.micro) for c in range(2)]

    def in_order(self, mine, got, side, axis):
        return jnp.where(
            side == 0, jnp.stack([mine, got], axis), jnp.stack([got, mine], axis)
        )

    def joined(self, mine, got, side, axis):
        return jnp.where(
            side == 0, jnp.concatenate([mine, got], axis), jnp.concatenate([got, mine], axis)
        )

    def gather(self, value, items=False):
        homes = [(i, c) for i in range(self.micro) for c in range(2)]
        got = self.send(value, [(self.far(i, c), self.seat(i, c)) for i, c in homes])
        whole = self.in_order(value, got, 1 - self.high, 0)
        if items:
            whole = whole.reshape((2,) + (2,) * (1 + self.bits) + value.shape[1:])
        whole = whole.reshape((1,) * (1 + self.bits) + whole.shape)
        for bit in range(self.bits + 1):
            axis = self.bits - bit
            side = (self.home >> bit) % 2
            out = whole
            if items:
                at = 2 + self.bits + axis
                out = lax.dynamic_index_in_dim(whole, 1 - side, at, keepdims=True)
                whole = lax.dynamic_index_in_dim(whole, side, at, keepdims=True)
            whole = self.joined(whole, self.send(out, self.between_homes(1 << bit)), side, axis)
        rest = value.shape[1:] if items else value.shape
        whole = whole.reshape((2, self.half, 2) + rest).swapaxes(1, 2)
        got = self.send(whole, [(self.seat(i, c), self.seat(i, 1 - c)) for i, c in homes])
        return self.in_order(whole, got, self.core, 3).reshape((self.chain,) + rest)

    def spread(self, values):
        kind = (2, 2, self.half, 2)
        parts = []
        for value in values:
            mine = value.reshape(kind + value.shape[1:])
            mine = lax.dynamic_index_in_dim(mine, self.core, 3, keepdims=False).swapaxes(1, 2)
            parts.append(mine.reshape((2,) * (1 + self.bits) + (2,) + value.shape[1:]))

        def cut(array, side, axis):
            return lax.dynamic_index_in_dim(array, side, axis, keepdims=False)

        wait = yield
        out = jnp.concatenate([cut(p, 1 - self.high + wait, 0) for p in parts], -2)
        got = self.send(out, self.between_homes(self.half))
        wait = yield after(out)
        own = jnp.concatenate([cut(p, self.high, 0) for p in parts], -2)

        def both(k):
            return jnp.stack([cut(p, k, self.bits) for p in (own, got)])

        homes = [(i, c) for i in range(self.micro) for c in range(2)]
        out = both(self.high + wait)
        got_away = self.send(out, [(self.seat(i, c), self.far(i, c)) for i, c in homes])
        wait = yield after(out)
        held = jnp.where(self.at_home, both(1 - self.high), got_away)
        near = (self.place // (2 * self.micro)) * self.half + (self.place // 2) % self.half
        flips = [0, self.half]
        for bit in reversed(range(self.bits)):
            side = (near >> bit) % 2
            out = cut(held, 1 - side + wait, 1)
            pairs = [
                (at(i, c), at(i ^ (1 << bit), c)) for i, c in homes for at in (self.seat, self.far)
            ]
            held = jnp.concatenate([cut(held, side, 1), self.send(out, pairs)])
            flips += [f ^ (1 << bit) for f in flips]
        yield after(out)
        order = jnp.array([flips.index(f) for f in range(self.micro)], jnp.int32)
        held = jnp.stack([cut(held, order[i ^ near], 0) for i in range(self.micro)])
        found, row = [], 0
        for value in values:
            found.append(held[:, row : row + value.shape[1]])
            row += value.shape[1]
        yield found

    def everywhere(self, value, wait):
        value = jnp.where(wait == 0, value, 0.0).astype(LOW)
        for stage in self.halvings("lhx"):
            value = add([value, self.exchange(value, stage)])
        homes = [(i, c) for i in range(self.micro) for c in range(2)]
        got = self.send(value, [(self.seat(i, c), self.far(i, c)) for i, c in homes])
        return jnp.where(self.at_home, value, got)

    def halvings(self, order):
        stages = []
        for name in order:
            if name == "x":
                stages += [("x", b) for b in range(self.items.bit_length() - 1)]
            elif name == "h":
                stages.append(("h", self.bits))
            else:
                stages += [("l", b) for b in range(self.bits)]
        return stages

    def side_of(self, stage):
        name, bit = stage
        return ((self.item if name == "x" else self.home) >> bit) % 2

    def exchange(self, out, stage):
        name, bit = stage
        if name == "x":
            return self.send_across(out, bit)
        return self.send(out, self.between_homes(1 << bit))

    def cut(self, term, stage, side):
        name, bit = stage
        axis = {"x": -1, "h": 0, "l": 1 + self.bits - bit}[name]
        found = []
        for f in term:
            size = f.shape[axis] // 2
            found.append(lax.dynamic_slice_in_dim(f, side * size, size, axis))
        return beside(found)

    def product(self, left, right):
        left, right = (jnp.where(self.core == 0, *pair) for pair in (left, right))
        left, right = (a.reshape(-1, a.shape[-1]) for a in (left, right))
        full = dot(left, right, TN).astype(LOW)
        kind = (2, 2) + (2,) * self.bits + (2,)
        return full.reshape(kind + (full.shape[0] // self.chain, full.shape[1]))

    def deliver(self, total):
        near = lax.dynamic_index_in_dim(total, 1 - self.high, 0, keepdims=False)
        away = lax.dynamic_index_in_dim(total, self.high, 0, keepdims=False)

        def of(pair, core):
            return lax.dynamic_index_in_dim(pair, core, 0, keepdims=False)

        homes = [(i, c) for i in range(self.micro) for c in range(2)]
        level = self.send(
            of(near, 1 - self.core), [(self.seat(i, c), self.seat(i, 1 - c)) for i, c in homes]
        )
        straight = self.send(
            of(away, self.core), [(self.seat(i, c), self.far(i, c)) for i, c in homes]
        )
        crossed = self.send(
            of(away, 1 - self.core), [(self.seat(i, c), self.far(i, 1 - c)) for i, c in homes]
        )
        same = jnp.where(self.at_home, of(near, self.core), straight)
        both = self.in_order(same, level + crossed, self.core, 0)
        if self.items == 2:
            swapped = lax.ppermute(both, "item", [(0, 1), (1, 0)])
            return [
                jnp.where(self.item == 0, both, swapped),
                jnp.where(self.item == 0, swapped, both),
            ]
        every = lax.all_gather(both, "item")
        width = self.items.bit_length() - 1
        return [every[int(format(x, "0%db" % width)[::-1], 2)] for x in range(self.items)]

    def reduce(self, chunks, values):
        stages = [self.halvings(order) for _, order in chunks]
        terms = [[[self.product(*p) for p in products]] for products, _ in chunks]
        wait = 0
        spread = self.spread(values)
        next(spread)
        for turn in range(len(stages[0])):
            outs = []
            for i, stage in enumerate(each[turn] for each in stages):
                side = self.side_of(stage)
                out = add([self.cut(f, stage, 1 - side + wait) for f in terms[i]])
                terms[i] = [[self.cut(f, stage, side)] for f in terms[i]]
                terms[i].append([self.exchange(out, stage)])
                outs.append(out)
            if turn < 3:
                shift = spread.send(wait)
            wait = after(outs[-1])
        wait = wait + shift
        values = spread.send(wait)
        sizes = [
            [(p[0][0].shape[-1] // self.chain, p[1][0].shape[-1]) for p in products]
            for products, _ in chunks
        ]
        rows = min(size[0] for each in sizes for size in each)
        totals = []
        for t in terms:
            total = add([f[0] for f in t])
            total = total.reshape((2, 2) + total.shape[-2:])
            strips = [total[:, :, i : i + rows] for i in range(0, total.shape[2], rows)]
            totals.append(strips[0] if len(strips) == 1 else jnp.concatenate(strips, -1))
        found = []
        for group in (range(len(totals)),):
            sides = self.deliver(jnp.concatenate([totals[i] for i in group], -1))
            at = 0
            for i in group:
                for high, wide in sizes[i]:
                    size = wide // self.items
                    strips = []
                    for _ in range(high // rows):
                        strips.append(
                            jnp.concatenate([side[..., at : at + size] for side in sides], -1)
                        )
                        at += size
                    found.append(jnp.concatenate(strips, 1).astype(F32))
        return found, values, wait


def beside(arrays):
    if len(arrays) == 1:
        return arrays[0]
    return jnp.concatenate(arrays, -1 if arrays[0].shape[-2] == arrays[-1].shape[-2] else -2)


def add(terms):
    total = terms[0].astype(F32)
    for t in terms[1:]:
        total = total + t.astype(F32)
    return total.astype(LOW)


def after(value):
    first, last = value[(0,) * value.ndim], value[(-1,) * value.ndim]
    return (first != first).astype(jnp.int32) + (last != last).astype(jnp.int32)


def body(text, cotangent, unroll, memory, *weights):
    micro, _, texts, width = text.shape
    mem = memory.shape[0]
    chain = lax.axis_size("seg")
    part = width // chain
    layers = (weights[:12], weights[12:])
    net = Slice(micro)

    def order(block):
        zero = jnp.zeros((block.shape[0], PAD - mem, width), block.dtype)
        return jnp.concatenate(
            [block[:, mem : mem + texts], block[:, :mem], zero, block[:, mem + texts :], zero], 1
        )

    def disorder(block):
        return jnp.concatenate(
            [
                block[:, texts : texts + mem],
                block[:, :texts],
                block[:, texts + PAD : texts + PAD + mem],
            ],
            1,
        )

    shards = []
    for w in layers:
        for matrix in (w[0], w[2], w[6], w[8]):
            shards += split_columns(matrix, width)
    gathered = lax.all_gather(jnp.concatenate(shards), "seg")
    if part % 16:
        gathered = regroup(gathered, 16 // (part & -part), part)
    text_home = net.gather(text[:, 0], items=True)
    cotangent_home = order(net.gather(cotangent[:, 0], items=True))
    vectors = jnp.concatenate([v for w in layers for v in w if v.ndim == 1])
    vectors = net.gather(vectors.reshape(-1, 2 * BLOCKS * part // 8)).reshape(chain, -1)
    vectors = vectors.astype(F32)
    rows_of = []
    at = 0
    for w in layers:
        for v in w:
            if v.ndim == 1:
                rows_of.append(vectors[:, at : at + v.shape[0]].reshape(-1, width))
                at += v.shape[0]
    half = len(rows_of) // 2
    table = jnp.stack([jnp.concatenate(rows_of[:half]), jnp.concatenate(rows_of[half:])])
    table = jnp.pad(table, ((0, 0), (0, 16 - table.shape[1]), (0, 0)))

    limit = unroll[net.home]
    segments = jnp.arange(chain, dtype=jnp.int32)
    fresh = jnp.logical_or(segments == 0, segments == limit).astype(jnp.int32)
    memory_rows = jnp.pad(memory, ((0, PAD - mem), (0, 0)))

    (low, qkv, probs, context, unit1, hidden, active, slope, unit2, (scale,), (out,), (turned,)) = (
        forward_chain(fresh, text_home, memory_rows, table, gathered)
    )
    (grad_qkv, grad_proj, grad_upper, grad_down, (text_grad,), (sums,)) = (
        backward_chain(
            fresh, cotangent_home, table, scale,
            (qkv, probs, unit1, slope, unit2), turned,
        )
    )

    (down, proj, up, qkv), (text_grad, layer_out), wait = net.reduce(
        [
            ([(active, grad_down), (context, grad_proj)], "lhx"),
            ([(hidden, grad_upper)], "hxl"),
            ([(low, grad_qkv)], "xlh"),
        ],
        [text_grad, out],
    )
    text_grad, layer_out = text_grad.astype(F32), disorder(layer_out)
    sums = net.everywhere(sums, wait).astype(F32)

    def own(row, rows):
        size = part * rows
        at = net.place * size
        return lax.dynamic_slice(sums, (row + at // width, at % width), (1, size)).reshape(-1)

    results = []
    for layer in range(2):
        base = 8 * layer
        vectors = [(base + 6, 2), (base + 5, 1), (base + 3, 1), (base + 4, 1)]
        vectors += [(16 + 4 * layer, 4), (base + 2, 1), (base, 1), (base + 1, 1)]
        left = [qkv[layer], proj[layer], up[layer], down[layer]]
        for w in layers[layer]:
            results.append(own(*vectors.pop(0)) if w.ndim == 1 else left.pop(0))
    memory_grad = lax.dynamic_slice(sums, (24, net.place * part), (mem, part))
    return (layer_out[:, None], text_grad[:, None], memory_grad, *results)


def regroup(gathered, together, part):
    shards, total, width = gathered.shape
    blocks = gathered.reshape(shards // together, together, total // part, part, width)
    pieces = []
    for layer in range(2):
        base = layer * BLOCKS
        for block in range(8):
            pieces.append(blocks[:, :, base + block])
        pieces.append(blocks[:, :, base + 8 : base + 12])
    return jnp.concatenate([p.reshape(shards // together, -1, width) for p in pieces], 1)


def solution(mesh):
    seg = (P("seg", None), P("seg"), P("seg", None)) + (P("seg"),) * 3
    seg = seg + (P("seg", None), P("seg"), P("seg", None)) + (P("seg"),) * 3
    rows = P("item", "seg", None, None)
    return jax.shard_map(
        body,
        mesh=mesh,
        in_specs=(rows, rows, P("item"), P()) + seg + seg,
        out_specs=(rows, rows, P(None, "seg")) + seg + seg,
        check_vma=False,
    )
```

time: 772 us -> 699 us (0.905)
  Pallas kernels: 317 us -> 255 us
  between operations: 19.2 us -> 34.4 us
  other arithmetic: 49.3 us -> 38.4 us
  starting transfers between devices: 50.9 us -> 40.5 us
    pallas_call x1, Pallas kernels: 178 us -> 124 us  [backward_chain(): pl.pallas_call(backward_kernel, grid=(segments,), in_specs=[SMEM, block(r...]
    ppermute x30 -> x27, starting transfers between devices: 43.5 us -> 34.4 us  [send(): return lax.ppermute(value, ('seg', 'item'), flat)]
    select_n x7 -> x3, other arithmetic: 9.2 us -> 0.26 us  [joined(): jnp.where(side == 0, jnp.concatenate([mine, got], axis), jnp.concatenate(...]
    pallas_call x1, Pallas kernels: 139 us -> 130 us  [forward_chain(): pl.pallas_call(forward_kernel, grid=(segments,), in_specs=[SMEM, block((t...]
    ppermute x30 -> x27, waiting for transfers between devices: 133 us -> 136 us  [send(): return lax.ppermute(value, ('seg', 'item'), flat)]
    convert_element_type x7 -> x9, other arithmetic: 17.7 us -> 14.5 us  [add(): return total.astype(LOW)]
    unnamed x106 -> x124, local copies, waits for them, and re-layouts: 14.7 us -> 17.9 us
  transfers between devices with their start and end apart: 36 -> 33, of which waited for: 10 -> 8; matrix products, arithmetic and copies ran while one was open for 15% -> 15% of each run, Pallas kernels for 0% -> 0%
where the time goes in v3:
time: 699 us; the launch traced here: 692 us
  Pallas kernels  255 us (36%)
  waiting for transfers between devices  233 us (33%)
  local copies, waits for them, and re-layouts  58.2 us (8%)
  starting transfers between devices  40.5 us (6%)
  other arithmetic  38.4 us (5%)
  between operations  34.4 us (5%)
  matrix products  32.7 us (5%)
    ppermute x27, waiting for transfers between devices, send(): return lax.ppermute(value, ('seg', 'item'), flat)  136 us
    pallas_call x1, Pallas kernels, forward_chain(): pl.pallas_call(forward_kernel, grid=(segments,), in_specs=[SMEM, block((t...  130 us
    pallas_call x1, Pallas kernels, backward_chain(): pl.pallas_call(backward_kernel, grid=(segments,), in_specs=[SMEM, block(r...  124 us
    all_gather x1, waiting for transfers between devices, body(): gathered = lax.all_gather(jnp.concatenate(shards), 'seg')  84.7 us
    ppermute x27, starting transfers between devices, send(): return lax.ppermute(value, ('seg', 'item'), flat)  34.4 us
    dot_general x4, matrix products, dot(): return lax.dot_general(left, right, dims, preferred_element_type=F32)  32.7 us
    unnamed x124, local copies, waits for them, and re-layouts  17.9 us
    convert_element_type x9, other arithmetic, add(): return total.astype(LOW)  14.5 us
  transfers between devices with their start and end apart: 33, of which 8 were waited for; matrix products, arithmetic and copies ran while one was open for 15% of the time, Pallas kernels for 0%

profile of v3, /device:TPU:0, one launch (start us, length us, event | category | flops | bytes accessed | tf_op | source)
XLA Modules:
  0.0 692.1 jit_solution(12263287196416445004)
XLA Ops:
  17.2 5.0 collective-permute-start
  26.0 15.9 %collective-permute-done = bf16[4,84,768]{2,0,1:T(4,128)(2,1)S(1)} collective-permute-done((bf16[4,84,768]{2,0,1:T(4,128)(2,1)S(1)}, bf16[4,84,768]{2,0,1:T(4,128)(2,1)S(1)}, u32[]{:S(2)}, u32[]{:S(2)}) %collective-permute-start) | collective-permute-done | bytes 516128 | tf_op jit(solution)/shard_map/ppermute | solution.py:476
  43.5 14.4 %collective-permute-done.4 = bf16[8,144]{1,0:T(8,128)(2,1)S(1)} collective-permute-done((bf16[8,144]{1,0:T(8,128)(2,1)S(1)}, bf16[8,144]{1,0:T(8,128)(2,1)S(1)}, u32[]{:S(2)}, u32[]{:S(2)}) %collective-permute-start.4) | collective-permute-done | bytes 2336 | tf_op jit(solution)/shard_map/ppermute | solution.py:476
  79.4 10.3 %concatenate.248.refs_1_ = bf16[16,96,768]{2,1,0:T(8,128)(2,1)} concatenate(bf16[16,64,768]{2,1,0:T(8,128)(2,1)S(1)} %slice.292, bf16[16,10,768]{2,1,0:T(8,128)(2,1)S(1)} %get-tuple-element.204, bf16[16,6,768]{2,1,0:T(8,128)(2,1)S(1)} %broadcast_in_dim.16, bf16[16,10,768]{2,1,0:T(8,128)(2,1)S(1)} %get-tuple-element.203, bf16[16,6,768]{2,1,0:T(8,128)(2,1)S(1)} %broadcast_in_dim.16), dimensions={1} | concatenate | bytes 4718592 | tf_op jit(solution)/shard_map/concatenate | solution.py:713
  89.8 84.7 %all-gather.3.cloned.1.call-done = bf16[18432,768]{1,0:T(8,128)(2,1)} async-done(((bf16[1152,768]{1,0:T(8,128)(2,1)}), bf16[18432,768]{1,0:T(8,128)(2,1)}) %all-gather.3.cloned.1.call-update) | async-done | bytes 28311568 | tf_op jit(solution)/shard_map/all_gather | solution.py:731
  174.4 130.3 %forward_chain.1 = (bf16[16,96,768]{2,1,0:T(8,128)(2,1)}, bf16[16,96,768]{2,1,0:T(8,128)(2,1)}, bf16[16,96,2304]{2,1,0:T(8,128)(2,1)}, bf16[16,96,2304]{2,1,0:T(...) custom-call(s32[16]{0:T(128)} %or_convert_fusion.refs_0_, ...), custom_call_target="tpu_custom_call" | custom-call | flops 173946175488 | bytes 28311552 | tf_op jit(solution)/shard_map/forward_chain/pallas_call | solution.py:393
  304.7 2.3 dynamic-slice_bitcast_fusion.1
  307.1 124.5 %backward_chain.1 = (bf16[16,96,2304]{2,1,0:T(8,128)(2,1)}, bf16[16,96,2304]{2,1,0:T(8,128)(2,1)}, bf16[16,96,768]{2,1,0:T(8,128)(2,1)}, bf16[16,96,768]{2,1,0:T...) custom-call(s32[16]{0:T(128)} %or_convert_fusion.refs_0_, ...), custom_call_target="tpu_custom_call", output_to_operand_aliasing={{0}: (5, {}), {1}: (6, {}), {2}: (9, {}), {3}: (10, {}), {4... | custom-call | flops 173946175488 | bytes 28311552 | tf_op jit(solution)/shard_map/backward_chain/pallas_call | solution.py:425
  436.4 9.3 %bitcast_convert_fusion.2 = bf16[768,2304]{1,0:T(8,128)(2,1)S(1)} fusion(bf16[16,96,2304]{2,1,0:T(8,128)(2,1)} %get-tuple-element.74, bf16[16,96,2304]{2,1,0:T(8,128)(2,1)} %get-tuple-element.75, pred[]{:T(512)S(6)} %eq.83, bf16[16,96,768]{2,1,0:T(8,128)(2,1)S(1)} %copy-done.44, bf16[16,96,768]{2,1,0:T(8,128)(2,1)} %get-tuple-element.73), kind=kOutput, calls=%fused_computation.8 | convolution fusion | flops 5442306048 | bytes 22413312 | tf_op jit(solution)/shard_map/dot_general | solution.py:24
  450.0 10.4 %bitcast_convert_fusion.1 = bf16[3072,768]{1,0:T(8,128)(2,1)S(1)} fusion(bf16[16,96,3072]{2,1,0:T(8,128)(2,1)S(1)} %bitcast.225, bf16[16,96,3072]{2,1,0:T(8,128)(2,1)} %get-tuple-element.78, pred[]{:T(512)S(6)} %eq.83, bf16[16,96,768]{2,1,0:T(8,128)(2,1)} %get-tuple-element.79, bf16[16,96,768]{2,1,0:T(8,128)(2,1)} %get-tuple-element.80), kind=kOutput, calls=%fused_computation.1 | convolution fusion | flops 7256014848 | bytes 28311552 | tf_op jit(solution)/shard_map/dot_general | solution.py:24
  464.2 2.3 bitcast_convert_fusion.3
  468.3 2.4 collective-permute-start.21
  470.8 10.8 %bitcast_convert_fusion = bf16[768,3072]{1,0:T(8,128)(2,1)S(1)} fusion(bf16[16,96,3072]{2,1,0:T(8,128)(2,1)} %get-tuple-element.87, bf16[16,96,3072]{2,1,0:T(8,128)(2,1)} %get-tuple-element.88, pred[]{:T(512)S(6)} %eq.83, bf16[16,96,768]{2,1,0:T(8,128)(2,1)S(1)} %copy-done.45, bf16[16,96,768]{2,1,0:T(8,128)(2,1)S(1)} %copy-done.46), kind=kOutput, calls=%fused_computation | convolution fusion | flops 7256014848 | bytes 28311552 | tf_op jit(solution)/shard_map/dot_general | solution.py:24
  498.7 3.2 add_convert_fusion
  508.5 28.4 %collective-permute-done.13 = bf16[2,2,160,768]{3,2,0,1:T(8,128)(2,1)} collective-permute-done((bf16[2,2,160,768]{3,2,0,1:T(8,128)(2,1)}, bf16[2,2,160,768]{3,2,0,1:T(8,128)(2,1)}, u32[]{:S(2)}, u32[]{:S(2)}) %collective-permute-start.13) | collective-permute-done | bytes 983072 | tf_op jit(solution)/shard_map/ppermute | solution.py:476
  551.9 3.4 add_convert_fusion.1
  556.9 2.2 fusion.61
  564.7 2.3 add_convert_fusion.4
  573.1 2.4 fusion.38
  575.8 2.1 fusion.42
  583.9 65.1 %collective-permute-done.28 = bf16[48,4608]{1,0:T(8,128)(2,1)S(1)} collective-permute-done((bf16[48,4608]{1,0:T(8,128)(2,1)S(1)}, bf16[48,4608]{1,0:T(8,128)(2,1)S(1)}, u32[]{:S(2)}, u32[]{:S(2)}) %collective-permute-start.28) | collective-permute-done | bytes 442400 | tf_op jit(solution)/shard_map/ppermute | solution.py:476
  649.0 9.5 %collective-permute-done.30 = bf16[48,4608]{1,0:T(8,128)(2,1)S(1)} collective-permute-done((bf16[48,4608]{1,0:T(8,128)(2,1)S(1)}, bf16[48,4608]{1,0:T(8,128)(2,1)S(1)}, u32[]{:S(2)}, u32[]{:S(2)}) %collective-permute-start.30) | collective-permute-done | bytes 442400 | tf_op jit(solution)/shard_map/ppermute | solution.py:476
  663.0 2.9 collective-permute-done.20
  668.5 12.0 %collective-permute-done.31 = bf16[2,48,4608]{2,1,0:T(8,128)(2,1)S(1)} collective-permute-done((bf16[2,48,4608]{2,1,0:T(8,128)(2,1)S(1)}, bf16[2,48,4608]{2,1,0:T(8,128)(2,1)S(1)}, u32[]{:S(2)}, u32[]{:S(2)}) %collective-permute-start.31) | collective-permute-done | bytes 884768 | tf_op jit(solution)/shard_map/ppermute | solution.py:629
  (294 shorter events, 101.4 us)
Async XLA Ops:
  7.2 167.2 %all-gather.3.cloned.1.call-start = ((), (), s32[]{:S(2)}) async-start(), calls=%async_computation | async-start | bytes 30081024 | tf_op jit(solution)/shard_map/all_gather | solution.py:731
  17.2 24.8 %collective-permute-start = (bf16[4,84,768]{2,0,1:T(4,128)(2,1)S(1)}, bf16[4,84,768]{2,0,1:T(4,128)(2,1)S(1)}, u32[]{:S(2)}, u32[]{:S(2)}) collective-permute-start(bf16[4,84,768]{2,0,1:T(4,128)(2,1)S(1)} %bitcast.210), channel_id=1, source_target_pairs={{0,8},{1,9},{2,10},{3,11},{4,12},{5,13},{6,14},{7,15},{24,16},{25,... | collective-permute-start | bytes 1548296 | tf_op jit(solution)/shard_map/ppermute | solution.py:476
  22.2 36.4 %collective-permute-start.8 = (bf16[4,64,768]{2,1,0:T(8,128)(2,1)S(1)}, bf16[4,64,768]{2,1,0:T(8,128)(2,1)S(1)}, u32[]{:S(2)}, u32[]{:S(2)}) collective-permute-start(bf16[4,64,768]{2,1,0:T(8,128)(2,1)S(1)} %bitcast.213), channel_id=1, source_target_pairs={{0,8},{1,9},{2,10},{3,11},{4,12},{5,13},{6,14},{7,15},{24,16},{25,... | collective-permute-start | bytes 1179656 | tf_op jit(solution)/shard_map/ppermute | solution.py:476
  23.8 34.0 %collective-permute-start.4 = (bf16[8,144]{1,0:T(8,128)(2,1)S(1)}, bf16[8,144]{1,0:T(8,128)(2,1)S(1)}, u32[]{:S(2)}, u32[]{:S(2)}) collective-permute-start(bf16[8,144]{1,0:T(8,128)(2,1)S(1)} %reshape.757), channel_id=1, source_target_pairs={{0,8},{1,9},{2,10},{3,11},{4,12},{5,13},{6,14},{7,15},{24,16},{25,... | collective-permute-start | bytes 6920 | tf_op jit(solution)/shard_map/ppermute | solution.py:476
  42.8 17.3 %collective-permute-start.1 = (bf16[1,1,2,2,1,84,768]{6,3,5,4,2,1,0:T(2,128)(2,1)S(1)}, bf16[1,1,2,2,1,84,768]{6,3,5,4,2,1,0:T(2,128)(2,1)S(1)}, u32[]{:S(2)}, u32[]{:S(2)}) collective-permute-start(bf16[1,1,2,2,1,84,768]{6,3,5,4,2,1,0:T(2,128)(2,1)S(1)} %copy.110), channel_id=1, source_target_pairs={{8,12},{9,13},{10,14},{11,15},{12,8},{13,9},{14,10},{15,11},{16,20... | collective-permute-start | bytes 1548296 | tf_op jit(solution)/shard_map/ppermute | solution.py:476
  61.7 7.1 %collective-permute-start.10 = (bf16[1,2,2,1,1,64,768]{6,5,1,2,4,3,0:T(8,128)(2,1)S(1)}, bf16[1,2,2,1,1,64,768]{6,5,1,2,4,3,0:T(8,128)(2,1)S(1)}, u32[]{:S(2)}, u32[]{:S(2)}) collective-permute-start(bf16[1,2,2,1,1,64,768]{6,5,1,2,4,3,0:T(8,128)(2,1)S(1)} %get-tuple-element.250), channel_id=1, source_target_pairs={{8,16},{9,17},{10,18},{11,19},{12,20},{13,21},{14,22},{15,23},{16,... | collective-permute-start | bytes 1179656 | tf_op jit(solution)/shard_map/ppermute | solution.py:476
  67.1 9.6 %collective-permute-start.3 = (bf16[2,2,2,84,768]{4,2,3,1,0:T(2,128)(2,1)}, bf16[2,2,2,84,768]{4,2,3,1,0:T(2,128)(2,1)}, u32[]{:S(2)}, u32[]{:S(2)}) collective-permute-start(bf16[2,2,2,84,768]{4,2,3,1,0:T(2,128)(2,1)} %copy.115), channel_id=1, source_target_pairs={{8,10},{9,11},{10,8},{11,9},{12,14},{13,15},{14,12},{15,13},{16,18... | collective-permute-start | bytes 3096584 | tf_op jit(solution)/shard_map/ppermute | solution.py:476
  434.7 57.6 %collective-permute-start.12 = (bf16[2,2,160,768]{3,2,0,1:T(8,128)(2,1)}, bf16[2,2,160,768]{3,2,0,1:T(8,128)(2,1)}, u32[]{:S(2)}, u32[]{:S(2)}) collective-permute-start(bf16[2,2,160,768]{3,2,0,1:T(8,128)(2,1)} %pad_maximum_fusion.1), channel_id=1, source_target_pairs={{8,16},{9,17},{10,18},{11,19},{12,20},{13,21},{14,22},{15,23},{16,... | collective-permute-start | bytes 2949128 | tf_op jit(solution)/shard_map/ppermute | solution.py:476
  448.1 48.6 %collective-permute-start.14 = (bf16[2,2,2,2,48,1152]{5,4,3,2,1,0:T(8,128)(2,1)}, bf16[2,2,2,2,48,1152]{5,4,3,2,1,0:T(8,128)(2,1)}, u32[]{:S(2)}, u32[]{:S(2)}) collective-permute-start(bf16[2,2,2,2,48,1152]{5,4,3,2,1,0:T(8,128)(2,1)} %constant_dynamic-slice_fusion.6), channel_id=1, source_target_pairs={{8,9},{9,8},{10,11},{11,10},{12,13},{13,12},{14,15},{15,14},{16,17... | collective-permute-start | bytes 5308424 | tf_op jit(solution)/shard_map/ppermute | solution.py:484
  468.3 30.3 %collective-permute-start.21 = (bf16[2,2,1,2,240,768]{5,4,3,2,1,0:T(8,128)(2,1)}, bf16[2,2,1,2,240,768]{5,4,3,2,1,0:T(8,128)(2,1)}, u32[]{:S(2)}, u32[]{:S(2)}) collective-permute-start(bf16[2,2,1,2,240,768]{5,4,3,2,1,0:T(8,128)(2,1)} %pad_maximum_fusion), channel_id=1, source_target_pairs={{8,12},{9,13},{10,14},{11,15},{12,8},{13,9},{14,10},{15,11},{16,20... | collective-permute-start | bytes 8847368 | tf_op jit(solution)/shard_map/ppermute | solution.py:476
  484.4 67.4 %collective-permute-start.24 = (bf16[1,2,2,2,48,3072]{5,4,3,2,1,0:T(8,128)(2,1)}, bf16[1,2,2,2,48,3072]{5,4,3,2,1,0:T(8,128)(2,1)}, u32[]{:S(2)}, u32[]{:S(2)}) collective-permute-start(bf16[1,2,2,2,48,3072]{5,4,3,2,1,0:T(8,128)(2,1)} %constant_dynamic-slice_fusion.1), channel_id=1, source_target_pairs={{8,16},{9,17},{10,18},{11,19},{12,20},{13,21},{14,22},{15,23},{16,... | collective-permute-start | bytes 7077896 | tf_op jit(solution)/shard_map/ppermute | solution.py:476
  495.3 41.6 %collective-permute-start.13 = (bf16[2,2,160,768]{3,2,0,1:T(8,128)(2,1)}, bf16[2,2,160,768]{3,2,0,1:T(8,128)(2,1)}, u32[]{:S(2)}, u32[]{:S(2)}) collective-permute-start(bf16[2,2,160,768]{3,2,0,1:T(8,128)(2,1)} %pad_maximum_fusion.2), channel_id=1, source_target_pairs={{8,0},{9,1},{10,2},{11,3},{12,4},{13,5},{14,6},{15,7},{16,24},{17,... | collective-permute-start | bytes 2949128 | tf_op jit(solution)/shard_map/ppermute | solution.py:476
  501.9 62.8 %collective-permute-start.22 = (bf16[1,2,1,2,240,768]{5,4,3,2,1,0:T(8,128)(2,1)}, bf16[1,2,1,2,240,768]{5,4,3,2,1,0:T(8,128)(2,1)}, u32[]{:S(2)}, u32[]{:S(2)}) collective-permute-start(bf16[1,2,1,2,240,768]{5,4,3,2,1,0:T(8,128)(2,1)} %add_convert_fusion), channel_id=1, source_target_pairs={{8,16},{9,17},{10,18},{11,19},{12,20},{13,21},{14,22},{15,23},{16,... | collective-permute-start | bytes 4423688 | tf_op jit(solution)/shard_map/ppermute | solution.py:476
  506.9 52.3 %collective-permute-start.16 = (bf16[2,2,1,2,48,1152]{5,4,3,2,1,0:T(8,128)(2,1)}, bf16[2,2,1,2,48,1152]{5,4,3,2,1,0:T(8,128)(2,1)}, u32[]{:S(2)}, u32[]{:S(2)}) collective-permute-start(bf16[2,2,1,2,48,1152]{5,4,3,2,1,0:T(8,128)(2,1)} %copy-done.10), channel_id=1, source_target_pairs={{8,12},{9,13},{10,14},{11,15},{12,8},{13,9},{14,10},{15,11},{16,20... | collective-permute-start | bytes 2654216 | tf_op jit(solution)/shard_map/ppermute | solution.py:476
  539.2 17.7 %collective-permute-start.15 = (bf16[2,160,768]{2,1,0:T(8,128)(2,1)S(1)}, bf16[2,160,768]{2,1,0:T(8,128)(2,1)}, u32[]{:S(2)}, u32[]{:S(2)}) collective-permute-start(bf16[2,160,768]{2,1,0:T(8,128)(2,1)S(1)} %get-tuple-element.228), channel_id=1, source_target_pairs={{8,12},{9,13},{0,4},{1,5},{10,14},{11,15},{2,6},{3,7},{12,8},{13,9... | collective-permute-start | bytes 1474568 | tf_op jit(solution)/shard_map/ppermute | solution.py:476
  555.3 14.9 %collective-permute-start.25 = (bf16[1,2,2,2,48,1536]{5,4,3,2,1,0:T(8,128)(2,1)}, bf16[1,2,2,2,48,1536]{5,4,3,2,1,0:T(8,128)(2,1)}, u32[]{:S(2)}, u32[]{:S(2)}) collective-permute-start(bf16[1,2,2,2,48,1536]{5,4,3,2,1,0:T(8,128)(2,1)} %add_convert_fusion.1), channel_id=1, source_target_pairs={{8,9},{9,8},{10,11},{11,10},{12,13},{13,12},{14,15},{15,14},{16,17... | collective-permute-start | bytes 3538952 | tf_op jit(solution)/shard_map/ppermute | solution.py:484
  568.8 9.1 %collective-permute-start.27 = (bf16[1,2,1,2,48,1152]{5,4,3,2,1,0:T(8,128)(2,1)S(1)}, bf16[1,2,1,2,48,1152]{5,4,3,2,1,0:T(8,128)(2,1)S(1)}, u32[]{:S(2)}, u32[]{:S(2)}) collective-permute-start(bf16[1,2,1,2,48,1152]{5,4,3,2,1,0:T(8,128)(2,1)S(1)} %copy-done.14), channel_id=1, source_target_pairs={{8,16},{9,17},{10,18},{11,19},{12,20},{13,21},{14,22},{15,23},{16,... | collective-permute-start | bytes 1327112 | tf_op jit(solution)/shard_map/ppermute | solution.py:476
  569.5 11.6 %collective-permute-start.18 = (bf16[40,768]{1,0:T(8,128)(2,1)S(1)}, bf16[40,768]{1,0:T(8,128)(2,1)S(1)}, u32[]{:S(2)}, u32[]{:S(2)}) collective-permute-start(bf16[40,768]{1,0:T(8,128)(2,1)S(1)} %add_convert_fusion.11), channel_id=1, source_target_pairs={{8,16},{9,17},{10,18},{11,19},{12,20},{13,21},{14,22},{15,23},{16,... | collective-permute-start | bytes 184328 | tf_op jit(solution)/shard_map/ppermute | solution.py:476
  579.7 69.3 %collective-permute-start.28 = (bf16[48,4608]{1,0:T(8,128)(2,1)S(1)}, bf16[48,4608]{1,0:T(8,128)(2,1)S(1)}, u32[]{:S(2)}, u32[]{:S(2)}) collective-permute-start(bf16[48,4608]{1,0:T(8,128)(2,1)S(1)} %get-tuple-element.207), channel_id=1, source_target_pairs={{8,0},{9,1},{10,2},{11,3},{12,4},{13,5},{14,6},{15,7},{16,24},{17,... | collective-permute-start | bytes 1327112 | tf_op jit(solution)/shard_map/ppermute | solution.py:476
  581.2 78.6 %collective-permute-start.19 = (bf16[40,768]{1,0:T(8,128)(2,1)S(1)}, bf16[40,768]{1,0:T(8,128)(2,1)S(1)}, u32[]{:S(2)}, u32[]{:S(2)}) collective-permute-start(bf16[40,768]{1,0:T(8,128)(2,1)S(1)} %add_convert_fusion.10), channel_id=1, source_target_pairs={{8,9},{9,8},{10,11},{11,10},{12,13},{13,12},{14,15},{15,14},{16,17... | collective-permute-start | bytes 184328 | tf_op jit(solution)/shard_map/ppermute | solution.py:484
  581.9 67.1 %collective-permute-start.29 = (bf16[48,4608]{1,0:T(8,128)(2,1)S(1)}, bf16[48,4608]{1,0:T(8,128)(2,1)S(1)}, u32[]{:S(2)}, u32[]{:S(2)}) collective-permute-start(bf16[48,4608]{1,0:T(8,128)(2,1)S(1)} %get-tuple-element.209), channel_id=1, source_target_pairs={{8,10},{9,11},{10,8},{11,9},{12,14},{13,15},{14,12},{15,13},{16,18... | collective-permute-start | bytes 1327112 | tf_op jit(solution)/shard_map/ppermute | solution.py:476
  582.6 76.0 %collective-permute-start.30 = (bf16[48,4608]{1,0:T(8,128)(2,1)S(1)}, bf16[48,4608]{1,0:T(8,128)(2,1)S(1)}, u32[]{:S(2)}, u32[]{:S(2)}) collective-permute-start(bf16[48,4608]{1,0:T(8,128)(2,1)S(1)} %get-tuple-element.208), channel_id=1, source_target_pairs={{8,2},{9,3},{10,0},{11,1},{12,6},{13,7},{14,4},{15,5},{16,26},{17,... | collective-permute-start | bytes 1327112 | tf_op jit(solution)/shard_map/ppermute | solution.py:476
  658.8 21.7 %collective-permute-start.31 = (bf16[2,48,4608]{2,1,0:T(8,128)(2,1)S(1)}, bf16[2,48,4608]{2,1,0:T(8,128)(2,1)S(1)}, u32[]{:S(2)}, u32[]{:S(2)}) collective-permute-start(bf16[2,48,4608]{2,1,0:T(8,128)(2,1)S(1)} %maximum_select_fusion.6), channel_id=1, source_target_pairs={{0,1},{1,0},{2,3},{3,2},{4,5},{5,4},{6,7},{7,6},{8,9},{9,8},{10,11... | collective-permute-start | bytes 2654216 | tf_op jit(solution)/shard_map/ppermute | solution.py:629
  659.8 6.1 collective-permute-start.20
  (60 other events, 370.4 us)
Sparse Core Ops, SparseCore 0:
  17.3 157.1 all-gather.2

commit v4 on v3

--- a/solution.py
+++ b/solution.py
@@ -192,10 +192,13 @@
             hidden_low = hidden.astype(LOW)
             hidden_ref[index][0] = hidden_low
             total = hidden + vector(B_DOWN)
-            upper = [dot(hidden_low, weight(4 + b)) + vector(B_UP + b) for b in range(4)]
+            ahead = dot(hidden_low, weight(4)) + vector(B_UP)
             for block in range(4):
                 wide = slice(block * width, (block + 1) * width)
-                active, slope = gelu_and_slope(upper[block])
+                upper = ahead
+                if block < 3:
+                    ahead = dot(hidden_low, weight(5 + block)) + vector(B_UP + block + 1)
+                active, slope = gelu_and_slope(upper)
                 active = active.astype(LOW)
                 active_ref[index][0, :, wide] = active
                 slope_ref[index][0, :, wide] = slope.astype(LOW)
@@ -321,21 +324,23 @@
             context = [two_heads(grad_context[:, c], first_head) for c in cols]
             term = [dot(context[p], qkv_ref[index][0, :, in_values[p]], NT) for p in pairs]
             probs = [probs_ref[index][0, p] for p in pairs]
+            grad_values = [dot(probs[p], context[p], TN) for p in pairs]
+            for p in pairs:
+                narrow_ref[index, 7, :, cols[p]] += fold(grad_values[p])
+                grad_qkv_ref[index][0, :, in_values[p]] = grad_values[p].astype(LOW)
+            by_values = dot(grad_qkv_ref[index][0, :, 2 * width :], weight(2))
             term = [term[p] * probs[p].astype(F32) for p in pairs]
             total = [jnp.sum(t, -1, keepdims=True) for t in term]
             grad_scores = [(term[p] - probs[p].astype(F32) * total[p]).astype(LOW) for p in pairs]
             both = [dot(grad_scores[p], qkv_ref[index][0, :, in_keys[p]] * eighth) for p in pairs]
             grad_query = [jnp.where(first_head, b[:rows], b[rows:]) for b in both]
             grad_keys = [dot(grad_scores[p], query[p], TN) for p in pairs]
-            grad_values = [dot(probs[p], context[p], TN) for p in pairs]
             for p in pairs:
                 narrow_ref[index, 6, :, cols[p]] += fold(grad_query[p])
-                narrow_ref[index, 7, :, cols[p]] += fold(grad_values[p])
                 grad_qkv_ref[index][0, :, cols[p]] = grad_query[p].astype(LOW)
                 grad_qkv_ref[index][0, :, in_keys[p]] = grad_keys[p].astype(LOW)
-                grad_qkv_ref[index][0, :, in_values[p]] = grad_values[p].astype(LOW)
-            grad = grad_first
-            for block in (2, 1, 0):
+            grad = grad_first + by_values
+            for block in (1, 0):
                 cols = slice(block * width, (block + 1) * width)
                 grad = grad + dot(grad_qkv_ref[index][0, :, cols], weight(block))
         text_ref[0] = grad[:texts].astype(LOW)
@@ -444,6 +449,28 @@
         name="backward_chain",
     )(fresh, cotangent, vectors, scale, turned, *(a for pair in saved for a in pair))
     return split_refs(found, [2] * 4 + [1] * 2)
+
+
+def pack_kernel(*refs):
+    *shards, out_ref = refs
+    width = out_ref.shape[1]
+    row = 0
+    for ref in shards:
+        rows, columns = ref.shape
+        for at in range(0, columns, width):
+            out_ref[row : row + rows] = ref[:, at : at + width]
+            row += rows
+
+
+def pack(matrices, width):
+    rows = sum(m.size for m in matrices) // width
+    return pl.pallas_call(
+        pack_kernel,
+        in_specs=[VMEM] * len(matrices),
+        out_specs=VMEM,
+        out_shape=jax.ShapeDtypeStruct((rows, width), LOW),
+        name="pack",
+    )(*matrices)
 
 
 def split_columns(shard, width):
@@ -724,11 +751,12 @@
             1,
         )
 
-    shards = []
-    for w in layers:
-        for matrix in (w[0], w[2], w[6], w[8]):
-            shards += split_columns(matrix, width)
-    gathered = lax.all_gather(jnp.concatenate(shards), "seg")
+    matrices = [m for w in layers for m in (w[0], w[2], w[6], w[8])]
+    if part % 16:
+        shard = jnp.concatenate([c for m in matrices for c in split_columns(m, width)])
+    else:
+        shard = pack(matrices, width)
+    gathered = lax.all_gather(shard, "seg")
     if part % 16:
         gathered = regroup(gathered, 16 // (part & -part), part)
     text_home = net.gather(text[:, 0], items=True)
@@ -762,11 +790,11 @@
         )
     )
 
-    (down, proj, up, qkv), (text_grad, layer_out), wait = net.reduce(
+    (down, up, qkv, proj), (text_grad, layer_out), wait = net.reduce(
         [
-            ([(active, grad_down), (context, grad_proj)], "lhx"),
+            ([(active, grad_down)], "lhx"),
             ([(hidden, grad_upper)], "hxl"),
-            ([(low, grad_qkv)], "xlh"),
+            ([(low, grad_qkv), (context, grad_proj)], "xlh"),
         ],
         [text_grad, out],
     )

time: 699 us -> 656 us (0.938)
  waiting for transfers between devices: 233 us -> 206 us
  Pallas kernels: 255 us -> 243 us
    ppermute x27, waiting for transfers between devices: 136 us -> 110 us  [send(): return lax.ppermute(value, ('seg', 'item'), flat)]
    pallas_call x1, Pallas kernels: 124 us -> 116 us  [backward_chain(): pl.pallas_call(backward_kernel, grid=(segments,), in_specs=[SMEM, block(r...]
    unnamed x124 -> x94, local copies, waits for them, and re-layouts: 17.9 us -> 15.7 us
  transfers between devices with their start and end apart: 33 -> 33, of which waited for: 8 -> 8; matrix products, arithmetic and copies ran while one was open for 15% -> 16% of each run, Pallas kernels for 0% -> 0%
where the time goes in v4:
time: 656 us; the launch traced here: 650 us
  Pallas kernels  243 us (37%)
  waiting for transfers between devices  206 us (31%)
  local copies, waits for them, and re-layouts  55.1 us (8%)
  starting transfers between devices  40.9 us (6%)
  other arithmetic  38.7 us (6%)
  between operations  33.5 us (5%)
  matrix products  32.7 us (5%)
    pallas_call x1, Pallas kernels, forward_chain(): pl.pallas_call(forward_kernel, grid=(segments,), in_specs=[SMEM, block((t...  124 us
    pallas_call x1, Pallas kernels, backward_chain(): pl.pallas_call(backward_kernel, grid=(segments,), in_specs=[SMEM, block(r...  116 us
    ppermute x27, waiting for transfers between devices, send(): return lax.ppermute(value, ('seg', 'item'), flat)  110 us
    all_gather x1, waiting for transfers between devices, body(): gathered = lax.all_gather(shard, 'seg')  84.2 us
    ppermute x27, starting transfers between devices, send(): return lax.ppermute(value, ('seg', 'item'), flat)  34.7 us
    dot_general x4, matrix products, dot(): return lax.dot_general(left, right, dims, preferred_element_type=F32)  32.7 us
    unnamed x94, local copies, waits for them, and re-layouts  15.7 us
    convert_element_type x9, other arithmetic, add(): return total.astype(LOW)  15.4 us
  transfers between devices with their start and end apart: 33, of which 8 were waited for; matrix products, arithmetic and copies ran while one was open for 16% of the time, Pallas kernels for 0%

profile of v4, /device:TPU:0, one launch (start us, length us, event | category | flops | bytes accessed | tf_op | source)
XLA Modules:
  0.0 649.9 jit_solution(11368764614415450341)
XLA Ops:
  7.3 2.8 pack.1
  11.1 4.9 collective-permute-start
  19.9 16.7 %collective-permute-done = bf16[4,84,768]{2,0,1:T(4,128)(2,1)S(1)} collective-permute-done((bf16[4,84,768]{2,0,1:T(4,128)(2,1)S(1)}, bf16[4,84,768]{2,0,1:T(4,128)(2,1)S(1)}, u32[]{:S(2)}, u32[]{:S(2)}) %collective-permute-start) | collective-permute-done | bytes 516128 | tf_op jit(solution)/shard_map/ppermute | solution.py:503
  38.1 14.4 %collective-permute-done.4 = bf16[8,144]{1,0:T(8,128)(2,1)S(1)} collective-permute-done((bf16[8,144]{1,0:T(8,128)(2,1)S(1)}, bf16[8,144]{1,0:T(8,128)(2,1)S(1)}, u32[]{:S(2)}, u32[]{:S(2)}) %collective-permute-start.4) | collective-permute-done | bytes 2336 | tf_op jit(solution)/shard_map/ppermute | solution.py:503
  73.9 10.3 %concatenate.245.refs_1_ = bf16[16,96,768]{2,1,0:T(8,128)(2,1)} concatenate(bf16[16,64,768]{2,1,0:T(8,128)(2,1)S(1)} %slice.234, bf16[16,10,768]{2,1,0:T(8,128)(2,1)S(1)} %get-tuple-element.202, bf16[16,6,768]{2,1,0:T(8,128)(2,1)S(1)} %broadcast_in_dim.16, bf16[16,10,768]{2,1,0:T(8,128)(2,1)S(1)} %get-tuple-element.201, bf16[16,6,768]{2,1,0:T(8,128)(2,1)S(1)} %broadcast_in_dim.16), dimensions={1} | concatenate | bytes 4718592 | tf_op jit(solution)/shard_map/concatenate | solution.py:740
  84.2 84.2 %all-gather.3.cloned.1.call-done = bf16[18432,768]{1,0:T(8,128)(2,1)} async-done(((bf16[1152,768]{1,0:T(8,128)(2,1)}), bf16[18432,768]{1,0:T(8,128)(2,1)}) %all-gather.3.cloned.1.call-update) | async-done | bytes 28311568 | tf_op jit(solution)/shard_map/all_gather | solution.py:759
  168.4 124.1 %forward_chain.1 = (bf16[16,96,768]{2,1,0:T(8,128)(2,1)}, bf16[16,96,768]{2,1,0:T(8,128)(2,1)}, bf16[16,96,2304]{2,1,0:T(8,128)(2,1)}, bf16[16,96,2304]{2,1,0:T(...) custom-call(s32[16]{0:T(128)} %or_convert_fusion.refs_0_, ...), custom_call_target="tpu_custom_call" | custom-call | flops 173946175488 | bytes 28311552 | tf_op jit(solution)/shard_map/forward_chain/pallas_call | solution.py:398
  292.5 2.3 dynamic-slice_bitcast_fusion.2
  294.8 115.8 %backward_chain.1 = (bf16[16,96,2304]{2,1,0:T(8,128)(2,1)}, bf16[16,96,2304]{2,1,0:T(8,128)(2,1)}, bf16[16,96,768]{2,1,0:T(8,128)(2,1)}, bf16[16,96,768]{2,1,0:T...) custom-call(s32[16]{0:T(128)} %or_convert_fusion.refs_0_, ...), custom_call_target="tpu_custom_call", output_to_operand_aliasing={{0}: (5, {}), {1}: (6, {}), {2}: (9, {}), {3}: (10, {}), {4... | custom-call | flops 173946175488 | bytes 28311552 | tf_op jit(solution)/shard_map/backward_chain/pallas_call | solution.py:430
  414.6 9.3 %bitcast_convert_fusion.2 = bf16[768,2304]{1,0:T(8,128)(2,1)S(1)} fusion(bf16[16,96,2304]{2,1,0:T(8,128)(2,1)} %get-tuple-element.74, bf16[16,96,2304]{2,1,0:T(8,128)(2,1)} %get-tuple-element.75, pred[]{:T(512)S(6)} %eq.83, bf16[16,96,768]{2,1,0:T(8,128)(2,1)S(1)} %copy-done.38, bf16[16,96,768]{2,1,0:T(8,128)(2,1)} %get-tuple-element.73), kind=kOutput, calls=%fused_computation.8 | convolution fusion | flops 5442306048 | bytes 22413312 | tf_op jit(solution)/shard_map/dot_general | solution.py:24
  428.3 2.2 bitcast_convert_fusion.3
  432.4 2.3 collective-permute-start.14
  434.6 10.6 %bitcast_convert_fusion.1 = bf16[3072,768]{1,0:T(8,128)(2,1)S(1)} fusion(bf16[16,96,3072]{2,1,0:T(8,128)(2,1)} %get-tuple-element.81, bf16[16,96,3072]{2,1,0:T(8,128)(2,1)} %get-tuple-element.82, pred[]{:T(512)S(6)} %eq.83, bf16[16,96,768]{2,1,0:T(8,128)(2,1)S(1)} %copy-done.41, bf16[16,96,768]{2,1,0:T(8,128)(2,1)S(1)} %copy-done.42), kind=kOutput, calls=%fused_computation.1 | convolution fusion | flops 7256014848 | bytes 28311552 | tf_op jit(solution)/shard_map/dot_general | solution.py:24
  451.0 10.6 %bitcast_convert_fusion = bf16[768,3072]{1,0:T(8,128)(2,1)S(1)} fusion(bf16[16,96,3072]{2,1,0:T(8,128)(2,1)} %get-tuple-element.87, bf16[16,96,3072]{2,1,0:T(8,128)(2,1)} %get-tuple-element.88, pred[]{:T(512)S(6)} %eq.83, bf16[16,96,768]{2,1,0:T(8,128)(2,1)S(1)} %copy-done.39, bf16[16,96,768]{2,1,0:T(8,128)(2,1)S(1)} %copy-done.40), kind=kOutput, calls=%fused_computation | convolution fusion | flops 7256014848 | bytes 28311552 | tf_op jit(solution)/shard_map/dot_general | solution.py:24
  477.2 2.7 add_convert_fusion.2
  481.7 34.7 %collective-permute-done.13 = bf16[2,2,160,768]{3,2,0,1:T(8,128)(2,1)S(1)} collective-permute-done((bf16[2,2,160,768]{3,2,0,1:T(8,128)(2,1)}, bf16[2,2,160,768]{3,2,0,1:T(8,128)(2,1)S(1)}, u32[]{:S(2)}, u32[]{:S(2)}) %collective-permute-start.13) | collective-permute-done | bytes 983072 | tf_op jit(solution)/shard_map/ppermute | solution.py:503
  522.5 3.0 add_convert_fusion.1
  529.0 3.3 add_convert_fusion
  549.9 2.3 add_convert_fusion.8
  564.6 2.3 fusion.38
  575.2 30.2 %collective-permute-done.28 = bf16[48,4608]{1,0:T(8,128)(2,1)S(1)} collective-permute-done((bf16[48,4608]{1,0:T(8,128)(2,1)S(1)}, bf16[48,4608]{1,0:T(8,128)(2,1)S(1)}, u32[]{:S(2)}, u32[]{:S(2)}) %collective-permute-start.28) | collective-permute-done | bytes 442400 | tf_op jit(solution)/shard_map/ppermute | solution.py:503
  605.5 10.9 %collective-permute-done.30 = bf16[48,4608]{1,0:T(8,128)(2,1)S(1)} collective-permute-done((bf16[48,4608]{1,0:T(8,128)(2,1)S(1)}, bf16[48,4608]{1,0:T(8,128)(2,1)S(1)}, u32[]{:S(2)}, u32[]{:S(2)}) %collective-permute-start.30) | collective-permute-done | bytes 442400 | tf_op jit(solution)/shard_map/ppermute | solution.py:503
  620.7 2.9 collective-permute-done.20
  626.2 12.2 %collective-permute-done.31 = bf16[2,48,4608]{2,1,0:T(8,128)(2,1)S(1)} collective-permute-done((bf16[2,48,4608]{2,1,0:T(8,128)(2,1)S(1)}, bf16[2,48,4608]{2,1,0:T(8,128)(2,1)S(1)}, u32[]{:S(2)}, u32[]{:S(2)}) %collective-permute-start.31) | collective-permute-done | bytes 884768 | tf_op jit(solution)/shard_map/ppermute | solution.py:656
  (262 shorter events, 101.4 us)
Async XLA Ops:
  7.2 161.2 %all-gather.3.cloned.1.call-start = ((), (), s32[]{:S(2)}) async-start(), calls=%async_computation | async-start | bytes 30081024 | tf_op jit(solution)/shard_map/all_gather | solution.py:759
  11.1 25.6 %collective-permute-start = (bf16[4,84,768]{2,0,1:T(4,128)(2,1)S(1)}, bf16[4,84,768]{2,0,1:T(4,128)(2,1)S(1)}, u32[]{:S(2)}, u32[]{:S(2)}) collective-permute-start(bf16[4,84,768]{2,0,1:T(4,128)(2,1)S(1)} %bitcast.223), channel_id=1, source_target_pairs={{0,8},{1,9},{2,10},{3,11},{4,12},{5,13},{6,14},{7,15},{24,16},{25,... | collective-permute-start | bytes 1548296 | tf_op jit(solution)/shard_map/ppermute | solution.py:503
  16.1 37.1 %collective-permute-start.8 = (bf16[4,64,768]{2,1,0:T(8,128)(2,1)S(1)}, bf16[4,64,768]{2,1,0:T(8,128)(2,1)S(1)}, u32[]{:S(2)}, u32[]{:S(2)}) collective-permute-start(bf16[4,64,768]{2,1,0:T(8,128)(2,1)S(1)} %bitcast.226), channel_id=1, source_target_pairs={{0,8},{1,9},{2,10},{3,11},{4,12},{5,13},{6,14},{7,15},{24,16},{25,... | collective-permute-start | bytes 1179656 | tf_op jit(solution)/shard_map/ppermute | solution.py:503
  17.7 34.8 %collective-permute-start.4 = (bf16[8,144]{1,0:T(8,128)(2,1)S(1)}, bf16[8,144]{1,0:T(8,128)(2,1)S(1)}, u32[]{:S(2)}, u32[]{:S(2)}) collective-permute-start(bf16[8,144]{1,0:T(8,128)(2,1)S(1)} %reshape.757), channel_id=1, source_target_pairs={{0,8},{1,9},{2,10},{3,11},{4,12},{5,13},{6,14},{7,15},{24,16},{25,... | collective-permute-start | bytes 6920 | tf_op jit(solution)/shard_map/ppermute | solution.py:503
  37.4 17.4 %collective-permute-start.1 = (bf16[1,1,2,2,1,84,768]{6,3,5,4,2,1,0:T(2,128)(2,1)S(1)}, bf16[1,1,2,2,1,84,768]{6,3,5,4,2,1,0:T(2,128)(2,1)S(1)}, u32[]{:S(2)}, u32[]{:S(2)}) collective-permute-start(bf16[1,1,2,2,1,84,768]{6,3,5,4,2,1,0:T(2,128)(2,1)S(1)} %copy.142), channel_id=1, source_target_pairs={{8,12},{9,13},{10,14},{11,15},{12,8},{13,9},{14,10},{15,11},{16,20... | collective-permute-start | bytes 1548296 | tf_op jit(solution)/shard_map/ppermute | solution.py:503
  56.4 7.0 %collective-permute-start.10 = (bf16[1,2,2,1,1,64,768]{6,5,1,2,4,3,0:T(8,128)(2,1)S(1)}, bf16[1,2,2,1,1,64,768]{6,5,1,2,4,3,0:T(8,128)(2,1)S(1)}, u32[]{:S(2)}, u32[]{:S(2)}) collective-permute-start(bf16[1,2,2,1,1,64,768]{6,5,1,2,4,3,0:T(8,128)(2,1)S(1)} %get-tuple-element.248), channel_id=1, source_target_pairs={{8,16},{9,17},{10,18},{11,19},{12,20},{13,21},{14,22},{15,23},{16,... | collective-permute-start | bytes 1179656 | tf_op jit(solution)/shard_map/ppermute | solution.py:503
  61.8 9.6 %collective-permute-start.3 = (bf16[2,2,2,84,768]{4,2,3,1,0:T(2,128)(2,1)}, bf16[2,2,2,84,768]{4,2,3,1,0:T(2,128)(2,1)}, u32[]{:S(2)}, u32[]{:S(2)}) collective-permute-start(bf16[2,2,2,84,768]{4,2,3,1,0:T(2,128)(2,1)} %copy.147), channel_id=1, source_target_pairs={{8,10},{9,11},{10,8},{11,9},{12,14},{13,15},{14,12},{15,13},{16,18... | collective-permute-start | bytes 3096584 | tf_op jit(solution)/shard_map/ppermute | solution.py:503
  413.0 59.8 %collective-permute-start.12 = (bf16[2,2,160,768]{3,2,0,1:T(8,128)(2,1)}, bf16[2,2,160,768]{3,2,0,1:T(8,128)(2,1)}, u32[]{:S(2)}, u32[]{:S(2)}) collective-permute-start(bf16[2,2,160,768]{3,2,0,1:T(8,128)(2,1)} %pad_maximum_fusion.1), channel_id=1, source_target_pairs={{8,16},{9,17},{10,18},{11,19},{12,20},{13,21},{14,22},{15,23},{16,... | collective-permute-start | bytes 2949128 | tf_op jit(solution)/shard_map/ppermute | solution.py:503
  432.4 44.9 %collective-permute-start.14 = (bf16[2,2,2,2,48,1536]{5,4,3,2,1,0:T(8,128)(2,1)}, bf16[2,2,2,2,48,1536]{5,4,3,2,1,0:T(8,128)(2,1)}, u32[]{:S(2)}, u32[]{:S(2)}) collective-permute-start(bf16[2,2,2,2,48,1536]{5,4,3,2,1,0:T(8,128)(2,1)} %pad_maximum_fusion), channel_id=1, source_target_pairs={{8,9},{9,8},{10,11},{11,10},{12,13},{13,12},{14,15},{15,14},{16,17... | collective-permute-start | bytes 7077896 | tf_op jit(solution)/shard_map/ppermute | solution.py:511
  448.8 73.7 %collective-permute-start.21 = (bf16[2,2,1,2,192,768]{5,4,3,1,2,0:T(8,128)(2,1)}, bf16[2,2,1,2,192,768]{5,4,3,1,2,0:T(8,128)(2,1)}, u32[]{:S(2)}, u32[]{:S(2)}) collective-permute-start(bf16[2,2,1,2,192,768]{5,4,3,1,2,0:T(8,128)(2,1)} %dynamic-slice_bitcast_fusion), channel_id=1, source_target_pairs={{8,12},{9,13},{10,14},{11,15},{12,8},{13,9},{14,10},{15,11},{16,20... | collective-permute-start | bytes 7077896 | tf_op jit(solution)/shard_map/ppermute | solution.py:503
  465.4 63.6 %collective-permute-start.24 = (bf16[1,2,2,2,48,3072]{5,4,3,1,2,0:T(8,128)(2,1)}, bf16[1,2,2,2,48,3072]{5,4,3,1,2,0:T(8,128)(2,1)}, u32[]{:S(2)}, u32[]{:S(2)}) collective-permute-start(bf16[1,2,2,2,48,3072]{5,4,3,1,2,0:T(8,128)(2,1)} %copy.169), channel_id=1, source_target_pairs={{8,16},{9,17},{10,18},{11,19},{12,20},{13,21},{14,22},{15,23},{16,... | collective-permute-start | bytes 7077896 | tf_op jit(solution)/shard_map/ppermute | solution.py:503
  475.8 40.5 %collective-permute-start.13 = (bf16[2,2,160,768]{3,2,0,1:T(8,128)(2,1)}, bf16[2,2,160,768]{3,2,0,1:T(8,128)(2,1)S(1)}, u32[]{:S(2)}, u32[]{:S(2)}) collective-permute-start(bf16[2,2,160,768]{3,2,0,1:T(8,128)(2,1)} %pad_maximum_fusion.2), channel_id=1, source_target_pairs={{8,0},{9,1},{10,2},{11,3},{12,4},{13,5},{14,6},{15,7},{16,24},{17,... | collective-permute-start | bytes 2949128 | tf_op jit(solution)/shard_map/ppermute | solution.py:503
  480.0 69.9 %collective-permute-start.16 = (bf16[2,2,1,2,48,1536]{5,4,3,2,1,0:T(8,128)(2,1)}, bf16[2,2,1,2,48,1536]{5,4,3,2,1,0:T(8,128)(2,1)}, u32[]{:S(2)}, u32[]{:S(2)}) collective-permute-start(bf16[2,2,1,2,48,1536]{5,4,3,2,1,0:T(8,128)(2,1)} %add_convert_fusion.2), channel_id=1, source_target_pairs={{8,12},{9,13},{10,14},{11,15},{12,8},{13,9},{14,10},{15,11},{16,20... | collective-permute-start | bytes 3538952 | tf_op jit(solution)/shard_map/ppermute | solution.py:503
  525.5 32.2 %collective-permute-start.22 = (bf16[1,2,1,2,192,768]{5,4,3,1,2,0:T(8,128)(2,1)}, bf16[1,2,1,2,192,768]{5,4,3,1,2,0:T(8,128)(2,1)}, u32[]{:S(2)}, u32[]{:S(2)}) collective-permute-start(bf16[1,2,1,2,192,768]{5,4,3,1,2,0:T(8,128)(2,1)} %add_convert_fusion.1), channel_id=1, source_target_pairs={{8,16},{9,17},{10,18},{11,19},{12,20},{13,21},{14,22},{15,23},{16,... | collective-permute-start | bytes 3538952 | tf_op jit(solution)/shard_map/ppermute | solution.py:503
  528.1 18.3 %collective-permute-start.15 = (bf16[2,160,768]{2,1,0:T(8,128)(2,1)}, bf16[2,160,768]{2,1,0:T(8,128)(2,1)S(1)}, u32[]{:S(2)}, u32[]{:S(2)}) collective-permute-start(bf16[2,160,768]{2,1,0:T(8,128)(2,1)} %get-tuple-element.228), channel_id=1, source_target_pairs={{8,12},{9,13},{0,4},{1,5},{10,14},{11,15},{2,6},{3,7},{12,8},{13,9... | collective-permute-start | bytes 1474568 | tf_op jit(solution)/shard_map/ppermute | solution.py:503
  532.3 28.9 %collective-permute-start.25 = (bf16[1,2,2,2,48,1536]{5,4,3,1,2,0:T(8,128)(2,1)}, bf16[1,2,2,2,48,1536]{5,4,3,1,2,0:T(8,128)(2,1)}, u32[]{:S(2)}, u32[]{:S(2)}) collective-permute-start(bf16[1,2,2,2,48,1536]{5,4,3,1,2,0:T(8,128)(2,1)} %add_convert_fusion), channel_id=1, source_target_pairs={{8,9},{9,8},{10,11},{11,10},{12,13},{13,12},{14,15},{15,14},{16,17... | collective-permute-start | bytes 3538952 | tf_op jit(solution)/shard_map/ppermute | solution.py:511
  552.1 17.1 %collective-permute-start.27 = (bf16[1,2,1,2,48,1536]{5,4,3,2,1,0:T(8,128)(2,1)}, bf16[1,2,1,2,48,1536]{5,4,3,2,1,0:T(8,128)(2,1)}, u32[]{:S(2)}, u32[]{:S(2)}) collective-permute-start(bf16[1,2,1,2,48,1536]{5,4,3,2,1,0:T(8,128)(2,1)} %add_convert_fusion.8), channel_id=1, source_target_pairs={{8,16},{9,17},{10,18},{11,19},{12,20},{13,21},{14,22},{15,23},{16,... | collective-permute-start | bytes 1769480 | tf_op jit(solution)/shard_map/ppermute | solution.py:503
  563.9 8.6 %collective-permute-start.18 = (bf16[40,768]{1,0:T(8,128)(2,1)S(1)}, bf16[40,768]{1,0:T(8,128)(2,1)S(1)}, u32[]{:S(2)}, u32[]{:S(2)}) collective-permute-start(bf16[40,768]{1,0:T(8,128)(2,1)S(1)} %add_convert_fusion.11), channel_id=1, source_target_pairs={{8,16},{9,17},{10,18},{11,19},{12,20},{13,21},{14,22},{15,23},{16,... | collective-permute-start | bytes 184328 | tf_op jit(solution)/shard_map/ppermute | solution.py:503
  571.1 34.4 %collective-permute-start.28 = (bf16[48,4608]{1,0:T(8,128)(2,1)S(1)}, bf16[48,4608]{1,0:T(8,128)(2,1)S(1)}, u32[]{:S(2)}, u32[]{:S(2)}) collective-permute-start(bf16[48,4608]{1,0:T(8,128)(2,1)S(1)} %get-tuple-element.205), channel_id=1, source_target_pairs={{8,0},{9,1},{10,2},{11,3},{12,4},{13,5},{14,6},{15,7},{16,24},{17,... | collective-permute-start | bytes 1327112 | tf_op jit(solution)/shard_map/ppermute | solution.py:503
  572.6 44.9 %collective-permute-start.19 = (bf16[40,768]{1,0:T(8,128)(2,1)S(1)}, bf16[40,768]{1,0:T(8,128)(2,1)S(1)}, u32[]{:S(2)}, u32[]{:S(2)}) collective-permute-start(bf16[40,768]{1,0:T(8,128)(2,1)S(1)} %add_convert_fusion.10), channel_id=1, source_target_pairs={{8,9},{9,8},{10,11},{11,10},{12,13},{13,12},{14,15},{15,14},{16,17... | collective-permute-start | bytes 184328 | tf_op jit(solution)/shard_map/ppermute | solution.py:511
  573.2 32.3 %collective-permute-start.29 = (bf16[48,4608]{1,0:T(8,128)(2,1)S(1)}, bf16[48,4608]{1,0:T(8,128)(2,1)S(1)}, u32[]{:S(2)}, u32[]{:S(2)}) collective-permute-start(bf16[48,4608]{1,0:T(8,128)(2,1)S(1)} %get-tuple-element.207), channel_id=1, source_target_pairs={{8,10},{9,11},{10,8},{11,9},{12,14},{13,15},{14,12},{15,13},{16,18... | collective-permute-start | bytes 1327112 | tf_op jit(solution)/shard_map/ppermute | solution.py:503
  573.9 42.5 %collective-permute-start.30 = (bf16[48,4608]{1,0:T(8,128)(2,1)S(1)}, bf16[48,4608]{1,0:T(8,128)(2,1)S(1)}, u32[]{:S(2)}, u32[]{:S(2)}) collective-permute-start(bf16[48,4608]{1,0:T(8,128)(2,1)S(1)} %get-tuple-element.206), channel_id=1, source_target_pairs={{8,2},{9,3},{10,0},{11,1},{12,6},{13,7},{14,4},{15,5},{16,26},{17,... | collective-permute-start | bytes 1327112 | tf_op jit(solution)/shard_map/ppermute | solution.py:503
  616.6 21.7 %collective-permute-start.31 = (bf16[2,48,4608]{2,1,0:T(8,128)(2,1)S(1)}, bf16[2,48,4608]{2,1,0:T(8,128)(2,1)S(1)}, u32[]{:S(2)}, u32[]{:S(2)}) collective-permute-start(bf16[2,48,4608]{2,1,0:T(8,128)(2,1)S(1)} %maximum_select_fusion.6), channel_id=1, source_target_pairs={{0,1},{1,0},{2,3},{3,2},{4,5},{5,4},{6,7},{7,6},{8,9},{9,8},{10,11... | collective-permute-start | bytes 2654216 | tf_op jit(solution)/shard_map/ppermute | solution.py:656
  617.5 6.1 collective-permute-start.20
  (52 other events, 328.2 us)
Sparse Core Ops, SparseCore 0:
  10.4 157.9 all-gather.2

commit v5 on v4

--- a/solution.py
+++ b/solution.py
@@ -185,7 +185,11 @@
                 context_ref[index][0, :, cols[p]] = jnp.where(
                     first_head, context[:rows], context[rows:]
                 ).astype(LOW)
-            total = x + dot(context_ref[index][0], weight(3)) + vector(B_OUT)
+            total = x + vector(B_OUT)
+            for part in range(0, width, 256):
+                total = total + dot(
+                    context_ref[index][0, :, part : part + 256], weight(3)[part : part + 256]
+                )
             unit, scale, hidden = norm_rows(total, vector(GAIN1), vector(SHIFT1))
             unit1_ref[index][0] = unit.astype(LOW)
             scales.append(scale)
@@ -672,7 +676,7 @@
             outs = []
             for i, stage in enumerate(each[turn] for each in stages):
                 side = self.side_of(stage)
-                out = add([self.cut(f, stage, 1 - side + wait) for f in terms[i]])
+                out = add([self.cut(f, stage, 1 - side) for f in terms[i]])
                 terms[i] = [[self.cut(f, stage, side)] for f in terms[i]]
                 terms[i].append([self.exchange(out, stage)])
                 outs.append(out)
@@ -760,7 +764,13 @@
     if part % 16:
         gathered = regroup(gathered, 16 // (part & -part), part)
     text_home = net.gather(text[:, 0], items=True)
-    cotangent_home = order(net.gather(cotangent[:, 0], items=True))
+    if chain > 16:
+        cotangent_home = order(net.gather(cotangent[:, 0], items=True))
+    else:
+        later = jnp.where(after(gathered) == 0, order(cotangent[:, 0]), 0)
+        cotangent_home = lax.dynamic_index_in_dim(
+            lax.all_gather(later, "seg"), net.home, 1, keepdims=False
+        )
     vectors = jnp.concatenate([v for w in layers for v in w if v.ndim == 1])
     vectors = net.gather(vectors.reshape(-1, 2 * BLOCKS * part // 8)).reshape(chain, -1)
     vectors = vectors.astype(F32)

time: 656 us -> 659 us (level)
  waiting for transfers between devices: 206 us -> 223 us
  local copies, waits for them, and re-layouts: 55.1 us -> 43.9 us
    all_gather x1, waiting for transfers between devices: 84.2 us -> 122 us  [body(): gathered = lax.all_gather(shard, 'seg')]
    ppermute x27 -> x23, waiting for transfers between devices: 110 us -> 88.5 us  [send(): return lax.ppermute(value, ('seg', 'item'), flat)]
    concatenate x1 -> x3, local copies, waits for them, and re-layouts: 10.3 us -> 0.3 us  [order(): jnp.concatenate([block[:, mem:mem + texts], block[:, :mem], zero, block[:...]
    ppermute x27 -> x23, starting transfers between devices: 34.7 us -> 29.8 us  [send(): return lax.ppermute(value, ('seg', 'item'), flat)]
    unnamed x94 -> x92, local copies, waits for them, and re-layouts: 15.7 us -> 14.9 us
  transfers between devices with their start and end apart: 33 -> 30, of which waited for: 8 -> 7; matrix products, arithmetic and copies ran while one was open for 16% -> 14% of each run, Pallas kernels for 0% -> 19%
where the time goes in v5:
time: 659 us; the launch traced here: 650 us
  Pallas kernels  242 us (37%)
  waiting for transfers between devices  223 us (34%)
  local copies, waits for them, and re-layouts  43.9 us (7%)
  other arithmetic  36.7 us (6%)
  starting transfers between devices  36.1 us (5%)
  between operations  36 us (5%)
  matrix products  32.6 us (5%)
    pallas_call x1, Pallas kernels, forward_chain(): pl.pallas_call(forward_kernel, grid=(segments,), in_specs=[SMEM, block((t...  123 us
    all_gather x1, waiting for transfers between devices, body(): gathered = lax.all_gather(shard, 'seg')  122 us
    pallas_call x1, Pallas kernels, backward_chain(): pl.pallas_call(backward_kernel, grid=(segments,), in_specs=[SMEM, block(r...  116 us
    ppermute x23, waiting for transfers between devices, send(): return lax.ppermute(value, ('seg', 'item'), flat)  88.5 us
    dot_general x4, matrix products, dot(): return lax.dot_general(left, right, dims, preferred_element_type=F32)  32.6 us
    ppermute x23, starting transfers between devices, send(): return lax.ppermute(value, ('seg', 'item'), flat)  29.8 us
    convert_element_type x9, other arithmetic, add(): return total.astype(LOW)  15.4 us
    unnamed x92, local copies, waits for them, and re-layouts  14.9 us
  transfers between devices with their start and end apart: 30, of which 7 were waited for; matrix products, arithmetic and copies ran while one was open for 14% of the time, Pallas kernels for 19%

profile of v5, /device:TPU:0, one launch (start us, length us, event | category | flops | bytes accessed | tf_op | source)
XLA Modules:
  0.0 650.2 jit_solution(5467988792469223965)
XLA Ops:
  7.3 2.8 pack.1
  11.1 4.9 collective-permute-start.4
  18.1 12.3 %collective-permute-done = bf16[8,144]{1,0:T(8,128)(2,1)S(1)} collective-permute-done((bf16[8,144]{1,0:T(8,128)(2,1)S(1)}, bf16[8,144]{1,0:T(8,128)(2,1)S(1)}, u32[]{:S(2)}, u32[]{:S(2)}) %collective-permute-start) | collective-permute-done | bytes 2336 | tf_op jit(solution)/shard_map/ppermute | solution.py:507
  35.0 122.2 %all-gather.6.cloned.1.call-done = bf16[18432,768]{1,0:T(8,128)(2,1)} async-done(((bf16[1152,768]{1,0:T(8,128)(2,1)}), bf16[18432,768]{1,0:T(8,128)(2,1)}) %all-gather.6.cloned.1.call-update) | async-done | bytes 28311568 | tf_op jit(solution)/shard_map/all_gather | solution.py:763
  168.7 123.4 %forward_chain.1 = (bf16[16,96,768]{2,1,0:T(8,128)(2,1)}, bf16[16,96,768]{2,1,0:T(8,128)(2,1)}, bf16[16,96,2304]{2,1,0:T(8,128)(2,1)}, bf16[16,96,2304]{2,1,0:T(...) custom-call(s32[16]{0:T(128)} %or_convert_fusion.refs_0_, ...), custom_call_target="tpu_custom_call" | custom-call | flops 173946175488 | bytes 28311552 | tf_op jit(solution)/shard_map/forward_chain/pallas_call | solution.py:402
  292.1 2.3 dynamic-slice_bitcast_fusion.3
  294.4 3.2 dynamic-slice_bitcast_fusion.1.refs_1_
  297.6 115.7 %backward_chain.1 = (bf16[16,96,2304]{2,1,0:T(8,128)(2,1)}, bf16[16,96,2304]{2,1,0:T(8,128)(2,1)}, bf16[16,96,768]{2,1,0:T(8,128)(2,1)}, bf16[16,96,768]{2,1,0:T...) custom-call(s32[16]{0:T(128)} %or_convert_fusion.refs_0_, ...), custom_call_target="tpu_custom_call", output_to_operand_aliasing={{0}: (5, {}), {1}: (6, {}), {2}: (9, {}), {3}: (10, {}), {4... | custom-call | flops 173946175488 | bytes 28311552 | tf_op jit(solution)/shard_map/backward_chain/pallas_call | solution.py:434
  417.4 9.3 %bitcast_convert_fusion.2 = bf16[768,2304]{1,0:T(8,128)(2,1)S(1)} fusion(bf16[16,96,2304]{2,1,0:T(8,128)(2,1)} %get-tuple-element.74, bf16[16,96,2304]{2,1,0:T(8,128)(2,1)} %get-tuple-element.75, pred[]{:T(512)S(6)} %eq.85, bf16[16,96,768]{2,1,0:T(8,128)(2,1)S(1)} %copy-done.37, bf16[16,96,768]{2,1,0:T(8,128)(2,1)} %get-tuple-element.73), kind=kOutput, calls=%fused_computation.8 | convolution fusion | flops 5442306048 | bytes 22413312 | tf_op jit(solution)/shard_map/dot_general | solution.py:24
  431.1 2.2 bitcast_convert_fusion.3
  435.2 2.3 collective-permute-start.10
  437.5 10.6 %bitcast_convert_fusion.1 = bf16[3072,768]{1,0:T(8,128)(2,1)S(1)} fusion(bf16[16,96,3072]{2,1,0:T(8,128)(2,1)} %get-tuple-element.81, bf16[16,96,3072]{2,1,0:T(8,128)(2,1)} %get-tuple-element.82, pred[]{:T(512)S(6)} %eq.85, bf16[16,96,768]{2,1,0:T(8,128)(2,1)S(1)} %copy-done.40, bf16[16,96,768]{2,1,0:T(8,128)(2,1)S(1)} %copy-done.41), kind=kOutput, calls=%fused_computation.1 | convolution fusion | flops 7256014848 | bytes 28311552 | tf_op jit(solution)/shard_map/dot_general | solution.py:24
  451.6 2.2 collective-permute-start.17
  453.8 10.5 %bitcast_convert_fusion = bf16[768,3072]{1,0:T(8,128)(2,1)S(1)} fusion(bf16[16,96,3072]{2,1,0:T(8,128)(2,1)} %get-tuple-element.87, bf16[16,96,3072]{2,1,0:T(8,128)(2,1)} %get-tuple-element.88, pred[]{:T(512)S(6)} %eq.85, bf16[16,96,768]{2,1,0:T(8,128)(2,1)S(1)} %copy-done.38, bf16[16,96,768]{2,1,0:T(8,128)(2,1)S(1)} %copy-done.39), kind=kOutput, calls=%fused_computation | convolution fusion | flops 7256014848 | bytes 28311552 | tf_op jit(solution)/shard_map/dot_general | solution.py:24
  479.9 2.8 add_convert_fusion.2
  484.3 32.2 %collective-permute-done.9 = bf16[2,2,160,768]{3,2,0,1:T(8,128)(2,1)S(1)} collective-permute-done((bf16[2,2,160,768]{3,2,0,1:T(8,128)(2,1)}, bf16[2,2,160,768]{3,2,0,1:T(8,128)(2,1)S(1)}, u32[]{:S(2)}, u32[]{:S(2)}) %collective-permute-start.9) | collective-permute-done | bytes 983072 | tf_op jit(solution)/shard_map/ppermute | solution.py:507
  522.8 2.9 add_convert_fusion.1
  529.4 3.3 add_convert_fusion
  550.2 2.3 add_convert_fusion.8
  565.0 2.3 fusion.38
  575.6 30.2 %collective-permute-done.24 = bf16[48,4608]{1,0:T(8,128)(2,1)S(1)} collective-permute-done((bf16[48,4608]{1,0:T(8,128)(2,1)S(1)}, bf16[48,4608]{1,0:T(8,128)(2,1)S(1)}, u32[]{:S(2)}, u32[]{:S(2)}) %collective-permute-start.24) | collective-permute-done | bytes 442400 | tf_op jit(solution)/shard_map/ppermute | solution.py:507
  605.8 10.9 %collective-permute-done.26 = bf16[48,4608]{1,0:T(8,128)(2,1)S(1)} collective-permute-done((bf16[48,4608]{1,0:T(8,128)(2,1)S(1)}, bf16[48,4608]{1,0:T(8,128)(2,1)S(1)}, u32[]{:S(2)}, u32[]{:S(2)}) %collective-permute-start.26) | collective-permute-done | bytes 442400 | tf_op jit(solution)/shard_map/ppermute | solution.py:507
  621.0 2.9 collective-permute-done.16
  626.4 12.2 %collective-permute-done.27 = bf16[2,48,4608]{2,1,0:T(8,128)(2,1)S(1)} collective-permute-done((bf16[2,48,4608]{2,1,0:T(8,128)(2,1)S(1)}, bf16[2,48,4608]{2,1,0:T(8,128)(2,1)S(1)}, u32[]{:S(2)}, u32[]{:S(2)}) %collective-permute-start.27) | collective-permute-done | bytes 884768 | tf_op jit(solution)/shard_map/ppermute | solution.py:660
  (244 shorter events, 88.2 us)
Async XLA Ops:
  7.2 150.1 %all-gather.6.cloned.1.call-start = ((), (), s32[]{:S(2)}) async-start(), calls=%async_computation.1 | async-start | bytes 30081024 | tf_op jit(solution)/shard_map/all_gather | solution.py:763
  10.3 284.1 %all-gather.4.cloned.1.call-start = ((), (), s32[]{:S(2)}) async-start(), calls=%async_computation | async-start | bytes 10027008 | tf_op jit(solution)/shard_map/all_gather | solution.py:772
  11.1 20.0 %collective-permute-start.4 = (bf16[4,64,768]{2,1,0:T(8,128)(2,1)S(1)}, bf16[4,64,768]{2,1,0:T(8,128)(2,1)S(1)}, u32[]{:S(2)}, u32[]{:S(2)}) collective-permute-start(bf16[4,64,768]{2,1,0:T(8,128)(2,1)S(1)} %bitcast.220), channel_id=1, source_target_pairs={{0,8},{1,9},{2,10},{3,11},{4,12},{5,13},{6,14},{7,15},{24,16},{25,... | collective-permute-start | bytes 1179656 | tf_op jit(solution)/shard_map/ppermute | solution.py:507
  16.4 14.0 %collective-permute-start = (bf16[8,144]{1,0:T(8,128)(2,1)S(1)}, bf16[8,144]{1,0:T(8,128)(2,1)S(1)}, u32[]{:S(2)}, u32[]{:S(2)}) collective-permute-start(bf16[8,144]{1,0:T(8,128)(2,1)S(1)} %reshape.682), channel_id=1, source_target_pairs={{0,8},{1,9},{2,10},{3,11},{4,12},{5,13},{6,14},{7,15},{24,16},{25,... | collective-permute-start | bytes 6920 | tf_op jit(solution)/shard_map/ppermute | solution.py:507
  33.5 130.3 %collective-permute-start.3 = (bf16[2,2,2,8,144]{4,3,2,1,0:T(8,128)(2,1)S(1)}, bf16[2,2,2,8,144]{4,3,2,1,0:T(8,128)(2,1)S(1)}, u32[]{:S(2)}, u32[]{:S(2)}) collective-permute-start(bf16[2,2,2,8,144]{4,3,2,1,0:T(8,128)(2,1)S(1)} %get-tuple-element.206), channel_id=1, source_target_pairs={{8,10},{9,11},{10,8},{11,9},{12,14},{13,15},{14,12},{15,13},{16,18... | collective-permute-start | bytes 55304 | tf_op jit(solution)/shard_map/ppermute | solution.py:507
  34.3 129.6 %collective-permute-start.6 = (bf16[1,2,2,1,1,64,768]{6,5,1,2,4,3,0:T(8,128)(2,1)S(1)}, bf16[1,2,2,1,1,64,768]{6,5,1,2,4,3,0:T(8,128)(2,1)S(1)}, u32[]{:S(2)}, u32[]{:S(2)}) collective-permute-start(bf16[1,2,2,1,1,64,768]{6,5,1,2,4,3,0:T(8,128)(2,1)S(1)} %get-tuple-element.161), channel_id=1, source_target_pairs={{8,16},{9,17},{10,18},{11,19},{12,20},{13,21},{14,22},{15,23},{16,... | collective-permute-start | bytes 1179656 | tf_op jit(solution)/shard_map/ppermute | solution.py:507
  415.8 59.6 %collective-permute-start.8 = (bf16[2,2,160,768]{3,2,0,1:T(8,128)(2,1)}, bf16[2,2,160,768]{3,2,0,1:T(8,128)(2,1)}, u32[]{:S(2)}, u32[]{:S(2)}) collective-permute-start(bf16[2,2,160,768]{3,2,0,1:T(8,128)(2,1)} %pad_maximum_fusion.1), channel_id=1, source_target_pairs={{8,16},{9,17},{10,18},{11,19},{12,20},{13,21},{14,22},{15,23},{16,... | collective-permute-start | bytes 2949128 | tf_op jit(solution)/shard_map/ppermute | solution.py:507
  435.2 44.7 %collective-permute-start.10 = (bf16[2,2,2,2,48,1536]{5,4,3,2,1,0:T(8,128)(2,1)}, bf16[2,2,2,2,48,1536]{5,4,3,2,1,0:T(8,128)(2,1)}, u32[]{:S(2)}, u32[]{:S(2)}) collective-permute-start(bf16[2,2,2,2,48,1536]{5,4,3,2,1,0:T(8,128)(2,1)} %pad_maximum_fusion), channel_id=1, source_target_pairs={{8,9},{9,8},{10,11},{11,10},{12,13},{13,12},{14,15},{15,14},{16,17... | collective-permute-start | bytes 7077896 | tf_op jit(solution)/shard_map/ppermute | solution.py:515
  451.6 71.2 %collective-permute-start.17 = (bf16[2,2,1,2,192,768]{5,4,3,1,2,0:T(8,128)(2,1)}, bf16[2,2,1,2,192,768]{5,4,3,1,2,0:T(8,128)(2,1)}, u32[]{:S(2)}, u32[]{:S(2)}) collective-permute-start(bf16[2,2,1,2,192,768]{5,4,3,1,2,0:T(8,128)(2,1)} %dynamic-slice_bitcast_fusion), channel_id=1, source_target_pairs={{8,12},{9,13},{10,14},{11,15},{12,8},{13,9},{14,10},{15,11},{16,20... | collective-permute-start | bytes 7077896 | tf_op jit(solution)/shard_map/ppermute | solution.py:507
  468.1 61.2 %collective-permute-start.20 = (bf16[1,2,2,2,48,3072]{5,4,3,1,2,0:T(8,128)(2,1)}, bf16[1,2,2,2,48,3072]{5,4,3,1,2,0:T(8,128)(2,1)}, u32[]{:S(2)}, u32[]{:S(2)}) collective-permute-start(bf16[1,2,2,2,48,3072]{5,4,3,1,2,0:T(8,128)(2,1)} %copy.98), channel_id=1, source_target_pairs={{8,16},{9,17},{10,18},{11,19},{12,20},{13,21},{14,22},{15,23},{16,... | collective-permute-start | bytes 7077896 | tf_op jit(solution)/shard_map/ppermute | solution.py:507
  478.5 38.1 %collective-permute-start.9 = (bf16[2,2,160,768]{3,2,0,1:T(8,128)(2,1)}, bf16[2,2,160,768]{3,2,0,1:T(8,128)(2,1)S(1)}, u32[]{:S(2)}, u32[]{:S(2)}) collective-permute-start(bf16[2,2,160,768]{3,2,0,1:T(8,128)(2,1)} %pad_maximum_fusion.2), channel_id=1, source_target_pairs={{8,0},{9,1},{10,2},{11,3},{12,4},{13,5},{14,6},{15,7},{16,24},{17,... | collective-permute-start | bytes 2949128 | tf_op jit(solution)/shard_map/ppermute | solution.py:507
  482.7 67.5 %collective-permute-start.12 = (bf16[2,2,1,2,48,1536]{5,4,3,2,1,0:T(8,128)(2,1)}, bf16[2,2,1,2,48,1536]{5,4,3,2,1,0:T(8,128)(2,1)}, u32[]{:S(2)}, u32[]{:S(2)}) collective-permute-start(bf16[2,2,1,2,48,1536]{5,4,3,2,1,0:T(8,128)(2,1)} %add_convert_fusion.2), channel_id=1, source_target_pairs={{8,12},{9,13},{10,14},{11,15},{12,8},{13,9},{14,10},{15,11},{16,20... | collective-permute-start | bytes 3538952 | tf_op jit(solution)/shard_map/ppermute | solution.py:507
  525.8 32.2 %collective-permute-start.18 = (bf16[1,2,1,2,192,768]{5,4,3,1,2,0:T(8,128)(2,1)}, bf16[1,2,1,2,192,768]{5,4,3,1,2,0:T(8,128)(2,1)}, u32[]{:S(2)}, u32[]{:S(2)}) collective-permute-start(bf16[1,2,1,2,192,768]{5,4,3,1,2,0:T(8,128)(2,1)} %add_convert_fusion.1), channel_id=1, source_target_pairs={{8,16},{9,17},{10,18},{11,19},{12,20},{13,21},{14,22},{15,23},{16,... | collective-permute-start | bytes 3538952 | tf_op jit(solution)/shard_map/ppermute | solution.py:507
  528.4 18.4 %collective-permute-start.11 = (bf16[2,160,768]{2,1,0:T(8,128)(2,1)}, bf16[2,160,768]{2,1,0:T(8,128)(2,1)S(1)}, u32[]{:S(2)}, u32[]{:S(2)}) collective-permute-start(bf16[2,160,768]{2,1,0:T(8,128)(2,1)} %get-tuple-element.141), channel_id=1, source_target_pairs={{8,12},{9,13},{0,4},{1,5},{10,14},{11,15},{2,6},{3,7},{12,8},{13,9... | collective-permute-start | bytes 1474568 | tf_op jit(solution)/shard_map/ppermute | solution.py:507
  532.6 28.9 %collective-permute-start.21 = (bf16[1,2,2,2,48,1536]{5,4,3,1,2,0:T(8,128)(2,1)}, bf16[1,2,2,2,48,1536]{5,4,3,1,2,0:T(8,128)(2,1)}, u32[]{:S(2)}, u32[]{:S(2)}) collective-permute-start(bf16[1,2,2,2,48,1536]{5,4,3,1,2,0:T(8,128)(2,1)} %add_convert_fusion), channel_id=1, source_target_pairs={{8,9},{9,8},{10,11},{11,10},{12,13},{13,12},{14,15},{15,14},{16,17... | collective-permute-start | bytes 3538952 | tf_op jit(solution)/shard_map/ppermute | solution.py:515
  552.5 17.1 %collective-permute-start.23 = (bf16[1,2,1,2,48,1536]{5,4,3,2,1,0:T(8,128)(2,1)}, bf16[1,2,1,2,48,1536]{5,4,3,2,1,0:T(8,128)(2,1)}, u32[]{:S(2)}, u32[]{:S(2)}) collective-permute-start(bf16[1,2,1,2,48,1536]{5,4,3,2,1,0:T(8,128)(2,1)} %add_convert_fusion.8), channel_id=1, source_target_pairs={{8,16},{9,17},{10,18},{11,19},{12,20},{13,21},{14,22},{15,23},{16,... | collective-permute-start | bytes 1769480 | tf_op jit(solution)/shard_map/ppermute | solution.py:507
  560.1 4.9 collective-permute-start.19
  564.3 8.6 %collective-permute-start.14 = (bf16[40,768]{1,0:T(8,128)(2,1)S(1)}, bf16[40,768]{1,0:T(8,128)(2,1)S(1)}, u32[]{:S(2)}, u32[]{:S(2)}) collective-permute-start(bf16[40,768]{1,0:T(8,128)(2,1)S(1)} %add_convert_fusion.11), channel_id=1, source_target_pairs={{8,16},{9,17},{10,18},{11,19},{12,20},{13,21},{14,22},{15,23},{16,... | collective-permute-start | bytes 184328 | tf_op jit(solution)/shard_map/ppermute | solution.py:507
  571.4 34.3 %collective-permute-start.24 = (bf16[48,4608]{1,0:T(8,128)(2,1)S(1)}, bf16[48,4608]{1,0:T(8,128)(2,1)S(1)}, u32[]{:S(2)}, u32[]{:S(2)}) collective-permute-start(bf16[48,4608]{1,0:T(8,128)(2,1)S(1)} %get-tuple-element.124), channel_id=1, source_target_pairs={{8,0},{9,1},{10,2},{11,3},{12,4},{13,5},{14,6},{15,7},{16,24},{17,... | collective-permute-start | bytes 1327112 | tf_op jit(solution)/shard_map/ppermute | solution.py:507
  572.9 44.8 %collective-permute-start.15 = (bf16[40,768]{1,0:T(8,128)(2,1)S(1)}, bf16[40,768]{1,0:T(8,128)(2,1)S(1)}, u32[]{:S(2)}, u32[]{:S(2)}) collective-permute-start(bf16[40,768]{1,0:T(8,128)(2,1)S(1)} %add_convert_fusion.10), channel_id=1, source_target_pairs={{8,9},{9,8},{10,11},{11,10},{12,13},{13,12},{14,15},{15,14},{16,17... | collective-permute-start | bytes 184328 | tf_op jit(solution)/shard_map/ppermute | solution.py:515
  573.6 32.2 %collective-permute-start.25 = (bf16[48,4608]{1,0:T(8,128)(2,1)S(1)}, bf16[48,4608]{1,0:T(8,128)(2,1)S(1)}, u32[]{:S(2)}, u32[]{:S(2)}) collective-permute-start(bf16[48,4608]{1,0:T(8,128)(2,1)S(1)} %get-tuple-element.126), channel_id=1, source_target_pairs={{8,10},{9,11},{10,8},{11,9},{12,14},{13,15},{14,12},{15,13},{16,18... | collective-permute-start | bytes 1327112 | tf_op jit(solution)/shard_map/ppermute | solution.py:507
  574.3 42.4 %collective-permute-start.26 = (bf16[48,4608]{1,0:T(8,128)(2,1)S(1)}, bf16[48,4608]{1,0:T(8,128)(2,1)S(1)}, u32[]{:S(2)}, u32[]{:S(2)}) collective-permute-start(bf16[48,4608]{1,0:T(8,128)(2,1)S(1)} %get-tuple-element.125), channel_id=1, source_target_pairs={{8,2},{9,3},{10,0},{11,1},{12,6},{13,7},{14,4},{15,5},{16,26},{17,... | collective-permute-start | bytes 1327112 | tf_op jit(solution)/shard_map/ppermute | solution.py:507
  616.9 21.7 %collective-permute-start.27 = (bf16[2,48,4608]{2,1,0:T(8,128)(2,1)S(1)}, bf16[2,48,4608]{2,1,0:T(8,128)(2,1)S(1)}, u32[]{:S(2)}, u32[]{:S(2)}) collective-permute-start(bf16[2,48,4608]{2,1,0:T(8,128)(2,1)S(1)} %maximum_select_fusion.2), channel_id=1, source_target_pairs={{0,1},{1,0},{2,3},{3,2},{4,5},{5,4},{6,7},{7,6},{8,9},{9,8},{10,11... | collective-permute-start | bytes 2654216 | tf_op jit(solution)/shard_map/ppermute | solution.py:660
  617.8 6.1 collective-permute-start.16
  (48 other events, 406.8 us)
Sparse Core Ops, SparseCore 0:
  10.4 146.8 all-gather.5
  162.1 88.5 all-gather.3
